TPU v7x, 32 devices: a whole 2x2x4 slice. The times are simulated.
32 devices in a mesh: pts: 8 (over z, x), lmk: 4 (over y, core).
Axes of the slice: x: 2, y: 2, z: 4, core: 2. Of those that a mesh axis runs over, the one named last changes fastest.
Arguments:
- points: bfloat16 [12288, 768], P('pts'), may hold values from -8 to 8
- landmarks: bfloat16 [4096, 768], P(('pts', 'lmk')), may hold values from -8 to 8
- eigvecs: bfloat16 [4096, 128], P(('pts', 'lmk')), may hold values from -0.09375 to 0.09375
Outputs:
- spectral: float32 [12288, 128], P('pts')
All inputs are finite; a program needn't handle non-finite values.
Results may differ from a plain program's by a relative error of at most 0.0076.
Values may be sent and summed in bfloat16 or wider, within the bound.
No kernel may reach another device: no remote copies, remote signals or barrier semaphores. Data moves between devices by JAX's collectives and lax.ppermute only.
A program may use at most 128 MiB of HBM per device.

v0:
```python
import math

import jax
import jax.numpy as jnp
from jax import lax
from jax.sharding import PartitionSpec as P

kernel_gain = 16.0


def unit_rows(values):
    floats = values.astype(jnp.float32)
    factor = lax.rsqrt(jnp.mean(floats * floats, axis=-1, keepdims=True) + 1e-06) / math.sqrt(
        values.shape[-1]
    )
    return (floats * factor).astype(jnp.bfloat16)


def finish(embed, gram):
    lower = jnp.linalg.cholesky(gram)
    return lax.linalg.triangular_solve(lower, embed, left_side=False, lower=True, transpose_a=True)


def per_device(points, landmarks, eigvecs):
    unit_pts = unit_rows(points)
    num_rows = points.shape[0]
    total_points = num_rows * lax.axis_size("pts")
    land_piece = lax.all_gather(landmarks, "pts", axis=0, tiled=True)
    vec_piece = lax.all_gather(eigvecs, "pts", axis=0, tiled=True)
    unit_land = unit_rows(land_piece)
    cosine = lax.dot_general(
        unit_pts, unit_land, (((1,), (1,)), ((), ())), preferred_element_type=jnp.float32
    )
    kernel = jnp.exp(2.0 * kernel_gain * (cosine - 1.0))
    degree = jnp.sum(kernel, axis=1)
    projected = jnp.dot(kernel.astype(jnp.bfloat16), vec_piece, preferred_element_type=jnp.float32)
    degree, projected = (degree, projected)
    degree, projected = lax.psum((degree, projected), "lmk")
    embed = projected / jnp.sqrt(degree)[:, None]
    local_gram = jnp.dot(embed.T, embed, precision=lax.Precision.HIGHEST)
    gram = lax.psum(local_gram, "pts") / total_points
    spectral = finish(embed, gram)
    return spectral


def solution(mesh):
    placed = (P("pts", None), P(("pts", "lmk"), None), P(("pts", "lmk"), None))
    return jax.shard_map(
        per_device, mesh=mesh, in_specs=placed, out_specs=P("pts", None), check_vma=False
    )
```

profile of v0, /device:TPU:0, one launch (start us, length us, event | category | flops | bytes accessed | tf_op | source)
XLA Modules:
  0.0 205.9 jit_solution(4317958814257063332)
XLA Ops:
  6.5 0.0 all-gather.2.cloned.1.call-start
  6.5 0.7 all-gather.2.cloned.1.call-update
  7.3 0.0 all-reduce.3.cloned.1.call-start
  7.3 33.2 %all_gather.7 = bf16[1024,128]{1,0:T(8,128)(2,1)S(1)} all-gather(bf16[128,128]{1,0:T(8,128)(2,1)} %param.5), channel_id=1, replica_groups=mesh['pts'=8,'lmk'=4] {'pts'}, dimensions={0}, use_global_device_ids=true | all-gather | bytes 294912 | tf_op jit(solution)/shard_map/all_gather | solution.py:29
  40.5 2.2 %fusion.2 = f32[1536]{0:T(1024)S(1)} fusion(bf16[1536,768]{1,0:T(8,128)(2,1)} %param.3), kind=kLoop, calls=%fused_computation.5 | loop fusion | flops 3537408 | bytes 2365440 | tf_op jit(solution)/shard_map/reduce_sum | solution.py:13
  42.7 14.0 %all-gather.2.cloned.1.call-done = bf16[1024,768]{1,0:T(8,128)(2,1)} async-done(((bf16[128,768]{1,0:T(8,128)(2,1)}), bf16[1024,768]{1,0:T(8,128)(2,1)}) %all-gather.2.cloned.1.call-update) | async-done | bytes 1572880 | tf_op jit(solution)/shard_map/all_gather | solution.py:28
  56.7 1.8 fusion.4
  58.5 5.0 %fusion = (f32[1536]{0:T(1024)S(1)}, f32[1536,1024]{0,1:T(8,128)S(1)}) fusion(bf16[1024,768]{1,0:T(8,128)(2,1)} %all-gather.2.cloned.1.call-done, f32[1024]{0:T(1024)S(1)} %rsqrt_multiply_fusion.1, bf16[1536,768]{1,0:T(8,128)(2,1)} %param.3, f32[1536]{0:T(1024)S(1)} %rsqrt_multiply_fusion), kind=kOutput, calls=%fused_computation.3 | convolution fusion | flops 2426534400 | bytes 10240000 | tf_op jit(solution)/shard_map/dot_general | solution.py:31
  63.4 2.1 fusion.6
  65.5 0.0 all-reduce.3.cloned.1.call-update
  65.5 0.0 all-reduce.5.cloned.1.call-start
  65.6 6.2 %psum.22 = f32[1536]{0:T(1024)S(1)} all-reduce(f32[1536]{0:T(1024)S(1)} %get-tuple-element.5), channel_id=1, replica_groups=mesh['pts'=8,'lmk'=4] {'lmk'}, use_global_device_ids=true, to_apply=%region_4.0 | all-reduce | flops 1536 | bytes 12288 | tf_op jit(solution)/shard_map/psum | solution.py:38
  71.8 27.5 %all-reduce.3.cloned.1.call-done = f32[1536,128]{1,0:T(8,128)} async-done(((f32[1536,128]{1,0:T(8,128)}), f32[1536,128]{1,0:T(8,128)}) %all-reduce.3.cloned.1.call-update) | async-done | bytes 786448 | tf_op jit(solution)/shard_map/psum | solution.py:38
  99.3 3.8 %fusion.16 = f32[128,128]{0,1:T(8,128)} fusion(f32[1536,128]{1,0:T(8,128)} %all-reduce.3.cloned.1.call-done, f32[1536]{0:T(1024)S(1)} %sqrt.3), kind=kOutput, calls=%fused_computation.19 | convolution fusion | flops 302186496 | bytes 858112 | tf_op jit(solution)/shard_map/dot_general | solution.py:40
  103.2 0.0 all-reduce.5.cloned.1.call-update
  103.2 68.7 %all-reduce.5.cloned.1.call-done = f32[128,128]{0,1:T(8,128)} async-done(((f32[128,128]{0,1:T(8,128)}), f32[128,128]{0,1:T(8,128)}) %all-reduce.5.cloned.1.call-update) | async-done | bytes 65552 | tf_op jit(solution)/shard_map/psum | solution.py:41
  171.9 0.8 broadcast_multiply_fusion
  172.7 0.1 copy.5
  172.8 0.9 fusion.19
  173.7 11.7 %cholesky.16 = f32[128,128]{1,0:T(8,128)S(1)} custom-call(f32[128,128]{1,0:T(8,128)S(1)} %fusion.19), custom_call_target="Cholesky" | custom-call | tf_op jit(solution)/shard_map/jit(cholesky)/cholesky | solution.py:20
  185.4 0.6 compare_reduce_fusion
  186.1 0.7 fusion.17
  186.7 9.8 %custom-call.6 = f32[1,128,128]{1,2,0:T(8,128)S(1)} custom-call(f32[1,128,128]{2,1,0:T(8,128)S(1)} %fusion.17), custom_call_target="InvertDiagBlocksLowerTriangular" | custom-call | tf_op jit(solution)/shard_map/triangular_solve | solution.py:21
  196.5 2.8 %fusion.15 = f32[1536,128]{1,0:T(8,128)} fusion(f32[1536,128]{1,0:T(8,128)} %all-reduce.3.cloned.1.call-done, f32[1536]{0:T(1024)S(1)} %sqrt.3, f32[1,128,128]{1,2,0:T(8,128)S(1)} %custom-call.6), kind=kOutput, calls=%fused_computation.18 | convolution fusion | flops 302186496 | bytes 1644544 | tf_op jit(solution)/shard_map/triangular_solve | solution.py:21
  (4 shorter events, 0.1 us)
Async XLA Ops:
  6.5 50.1 %all-gather.2.cloned.1.call-start = ((), (), s32[]{:S(2)}) async-start(), calls=%async_computation | async-start | bytes 1769472 | tf_op jit(solution)/shard_map/all_gather | solution.py:28
  7.3 92.1 %all-reduce.3.cloned.1.call-start = ((), (), s32[]{:S(2)}) async-start(), calls=%async_computation.1 | async-start | bytes 1572864 | tf_op jit(solution)/shard_map/psum | solution.py:38
  65.5 106.3 %all-reduce.5.cloned.1.call-start = ((), (), s32[]{:S(2)}) async-start(), calls=%async_computation.2 | async-start | bytes 131072 | tf_op jit(solution)/shard_map/psum | solution.py:41
Sparse Core Ops, SparseCore 0:
  9.5 47.0 all-gather.1
  65.6 33.6 all-reduce.2
  103.3 68.5 all-reduce.4
where the time goes:
time: 206 us
  waiting for transfers between devices  111 us (54%)
  blocking collectives  39.4 us (19%)
  other arithmetic  28.5 us (14%)
  matrix products  13.7 us (7%)
  between operations  13.2 us (6%)
    psum x1, waiting for transfers between devices, per_device(): gram = lax.psum(local_gram, 'pts') / total_points  68.7 us
    all_gather x1, blocking collectives, per_device(): vec_piece = lax.all_gather(eigvecs, 'pts', axis=0, tiled=True)  33.2 us
    psum x1, waiting for transfers between devices, per_device(): degree, projected = lax.psum((degree, projected), 'lmk')  27.5 us
    all_gather x1, waiting for transfers between devices, per_device(): land_piece = lax.all_gather(landmarks, 'pts', axis=0, tiled=True)  14 us
    another operation x3, other arithmetic, finish(): lower = jnp.linalg.cholesky(gram)  12.4 us
    another operation x2, other arithmetic, finish(): lax.linalg.triangular_solve(lower, embed, left_side=False, lower=True, tr...  10.5 us
    psum x1, blocking collectives, per_device(): degree, projected = lax.psum((degree, projected), 'lmk')  6.24 us
    dot_general x1, matrix products, per_device(): lax.dot_general(unit_pts, unit_land, (((1,), (1,)), ((), ())), preferred_...  4.96 us
  transfers between devices with their start and end apart: 3, of which 3 were waited for; matrix products, arithmetic and copies ran while one was open for 1% of the time, Pallas kernels for 0%

commit v1 on v0

v1 whole, which is shorter than its diff:
```python
import math

import jax
import jax.numpy as jnp
from jax import lax
from jax.sharding import PartitionSpec as P

kernel_gain = 16.0


def unit_rows(values):
    floats = values.astype(jnp.float32)
    factor = lax.rsqrt(jnp.mean(floats * floats, axis=-1, keepdims=True) + 1e-06) / math.sqrt(
        values.shape[-1]
    )
    return (floats * factor).astype(jnp.bfloat16)


def swap(value, axis, size, bit):
    return lax.ppermute(value, axis, [(i, i ^ bit) for i in range(size)])


def finish(embed, gram):
    lower = jnp.linalg.cholesky(gram)
    return lax.linalg.triangular_solve(lower, embed, left_side=False, lower=True, transpose_a=True)


def per_device(points, landmarks, eigvecs):
    num_pts = lax.axis_size("pts")
    num_lmk = lax.axis_size("lmk")
    num_rows = points.shape[0]
    features = points.shape[1]
    total_points = num_rows * num_pts
    half = num_rows // 2
    pts_bits = [1 << b for b in reversed(range(num_pts.bit_length() - 1))]
    lmk_bits = [1 << b for b in range(num_lmk.bit_length() - 1)]

    blocks = [jnp.concatenate([unit_rows(landmarks), eigvecs], axis=1)]
    unit_pts = unit_rows(points)
    degree, projected = 0.0, 0.0

    def meet(some):
        piece = jnp.concatenate(some, axis=0)
        cosine = lax.dot_general(
            unit_pts,
            piece[:, :features],
            (((1,), (1,)), ((), ())),
            preferred_element_type=jnp.float32,
        )
        kernel = jnp.exp(2.0 * kernel_gain * (cosine - 1.0))
        return jnp.sum(kernel, axis=1), jnp.dot(
            kernel.astype(jnp.bfloat16), piece[:, features:], preferred_element_type=jnp.float32
        )

    for bit in pts_bits:
        blocks = blocks + [swap(block, "pts", num_pts, bit) for block in blocks]
    for first in range(0, num_pts, 4):
        more = meet(blocks[first : first + 4])
        degree, projected = degree + more[0], projected + more[1]

    core = lax.axis_index("lmk") % 2
    own_rows = core * half
    other_rows = half - own_rows

    def rows_of(value, start):
        return lax.dynamic_slice_in_dim(value, start, half, 0)

    deg = rows_of(degree, own_rows) + swap(rows_of(degree, other_rows), "lmk", num_lmk, 1)
    proj = rows_of(projected, own_rows) + swap(rows_of(projected, other_rows), "lmk", num_lmk, 1)
    for bit in lmk_bits[1:]:
        deg = deg + swap(deg, "lmk", num_lmk, bit)
        proj = proj + swap(proj, "lmk", num_lmk, bit)
    embed = proj / jnp.sqrt(deg)[:, None]
    gram = jnp.dot(embed.T, embed, precision=lax.Precision.HIGHEST)
    other = swap(embed, "lmk", num_lmk, 1)
    gram = gram + swap(gram, "lmk", num_lmk, 1)
    for bit in pts_bits:
        gram = gram + swap(gram, "pts", num_pts, bit)
    gram = gram / total_points
    first = jnp.where(core == 0, embed, other)
    second = jnp.where(core == 0, other, embed)
    return finish(jnp.concatenate([first, second], axis=0), gram)


def solution(mesh):
    placed = (P("pts", None), P(("pts", "lmk"), None), P(("pts", "lmk"), None))
    return jax.shard_map(
        per_device, mesh=mesh, in_specs=placed, out_specs=P("pts", None), check_vma=False
    )
```

time: 206 us -> 93.9 us (0.46)
  waiting for transfers between devices: 111 us -> 37.9 us
  blocking collectives: 39.4 us -> 0 us
  starting transfers between devices: 0.08 us -> 18.9 us
  between operations: 13.2 us -> 0.21 us
  matrix products: 13.7 us -> 6.92 us
    psum x2 -> x0, waiting for transfers between devices: 96.2 us -> none  [the longest x1 68.7 us: per_device(): gram = lax.psum(local_gram, 'pts') / total_points]
    ppermute x0 -> x16, waiting for transfers between devices: none -> 37.9 us  [swap(): return lax.ppermute(value, axis, [(i, i ^ bit) for i in range(size)])]
    all_gather x1 -> x0, blocking collectives: 33.2 us -> none  [per_device(): vec_piece = lax.all_gather(eigvecs, 'pts', axis=0, tiled=True)]
    ppermute x0 -> x16, starting transfers between devices: none -> 18.9 us  [swap(): return lax.ppermute(value, axis, [(i, i ^ bit) for i in range(size)])]
    all_gather x1 -> x0, waiting for transfers between devices: 14 us -> none  [per_device(): land_piece = lax.all_gather(landmarks, 'pts', axis=0, tiled=True)]
    psum x1 -> x0, blocking collectives: 6.24 us -> none  [per_device(): degree, projected = lax.psum((degree, projected), 'lmk')]
    dot_general x3 -> x5, matrix products: 10.9 us -> 5.27 us  [the longest x2 3.25 us: meet(): lax.dot_general(unit_pts, piece[:, :features], (((1,), (1,)), ((), ())),...]
  transfers between devices with their start and end apart: 3 -> 16, of which waited for: 3 -> 10; matrix products, arithmetic and copies ran while one was open for 1% -> 31% of each run, Pallas kernels for 0% -> 0%
where the time goes in v1:
time: 93.9 us; the launch traced here: 93.6 us
  waiting for transfers between devices  37.9 us (40%)
  other arithmetic  28.4 us (30%)
  starting transfers between devices  18.9 us (20%)
  matrix products  6.92 us (7%)
  local copies, waits for them, and re-layouts  1.25 us (1%)
    ppermute x16, waiting for transfers between devices, swap(): return lax.ppermute(value, axis, [(i, i ^ bit) for i in range(size)])  37.9 us
    ppermute x16, starting transfers between devices, swap(): return lax.ppermute(value, axis, [(i, i ^ bit) for i in range(size)])  18.9 us
    another operation x3, other arithmetic, finish(): lower = jnp.linalg.cholesky(gram)  12.4 us
    another operation x2, other arithmetic, finish(): lax.linalg.triangular_solve(lower, embed, left_side=False, lower=True, tr...  10.5 us
    dot_general x2, matrix products, meet(): lax.dot_general(unit_pts, piece[:, :features], (((1,), (1,)), ((), ())),...  3.25 us
    reduce_sum x2, other arithmetic, unit_rows(): jnp.mean(floats * floats, axis=-1, keepdims=True) + 1e-06  3.25 us
  transfers between devices with their start and end apart: 16, of which 10 were waited for; matrix products, arithmetic and copies ran while one was open for 31% of the time, Pallas kernels for 0%

profile of v1, /device:TPU:0, one launch (start us, length us, event | category | flops | bytes accessed | tf_op | source)
XLA Modules:
  0.0 93.6 jit_solution(1054440496728985524)
XLA Ops:
  0.0 0.0 copy-start.1
  0.0 1.1 %fusion.17 = f32[128]{0:T(128)S(1)} fusion(bf16[128,768]{1,0:T(8,128)(2,1)} %param.4), kind=kLoop, calls=%fused_computation.23 | loop fusion | flops 294784 | bytes 197120 | tf_op jit(solution)/shard_map/reduce_sum | solution.py:13
  1.1 1.0 %fusion.18 = bf16[128,768]{1,0:T(8,128)(2,1)S(1)} fusion(bf16[128,768]{1,0:T(8,128)(2,1)} %param.4, f32[128]{0:T(128)S(1)} %rsqrt_multiply_fusion.1), kind=kLoop, calls=%fused_computation.24 | loop fusion | flops 294912 | bytes 393728 | tf_op jit(solution)/shard_map/convert_element_type | solution.py:16
  2.1 0.8 pad_maximum_fusion.1
  2.9 0.0 copy-start
  2.9 4.1 %collective-permute-start = (bf16[128,896]{1,0:T(8,128)(2,1)S(1)}, bf16[128,896]{1,0:T(8,128)(2,1)S(1)}, u32[]{:S(2)}, u32[]{:S(2)}) collective-permute-start(bf16[128,896]{1,0:T(8,128)(2,1)S(1)} %pad_maximum_fusion.1), channel_id=1, source_target_pairs={{0,16},{4,20},{8,24},{12,28},{16,0},{20,4},{24,8},{28,12},{1,17},{... | collective-permute-start | bytes 688136 | tf_op jit(solution)/shard_map/ppermute | solution.py:20
  7.0 1.6 %collective-permute-start.1 = (bf16[128,896]{1,0:T(8,128)(2,1)S(1)}, bf16[128,896]{1,0:T(8,128)(2,1)S(1)}, u32[]{:S(2)}, u32[]{:S(2)}) collective-permute-start(bf16[128,896]{1,0:T(8,128)(2,1)S(1)} %pad_maximum_fusion.1), channel_id=1, source_target_pairs={{0,8},{4,12},{8,0},{12,4},{16,24},{20,28},{24,16},{28,20},{1,9},{5... | collective-permute-start | bytes 688136 | tf_op jit(solution)/shard_map/ppermute | solution.py:20
  8.6 1.5 %collective-permute-start.3 = (bf16[128,896]{1,0:T(8,128)(2,1)S(1)}, bf16[128,896]{1,0:T(8,128)(2,1)}, u32[]{:S(2)}, u32[]{:S(2)}) collective-permute-start(bf16[128,896]{1,0:T(8,128)(2,1)S(1)} %pad_maximum_fusion.1), channel_id=1, source_target_pairs={{0,4},{4,0},{8,12},{12,8},{16,20},{20,16},{24,28},{28,24},{1,5},{5... | collective-permute-start | bytes 688136 | tf_op jit(solution)/shard_map/ppermute | solution.py:20
  10.1 2.2 %fusion = f32[1536]{0:T(1024)S(1)} fusion(bf16[1536,768]{1,0:T(8,128)(2,1)} %param.3), kind=kLoop, calls=%fused_computation.2 | loop fusion | flops 3537408 | bytes 2365440 | tf_op jit(solution)/shard_map/reduce_sum | solution.py:13
  12.3 5.4 %collective-permute-done = bf16[128,896]{1,0:T(8,128)(2,1)S(1)} collective-permute-done((bf16[128,896]{1,0:T(8,128)(2,1)S(1)}, bf16[128,896]{1,0:T(8,128)(2,1)S(1)}, u32[]{:S(2)}, u32[]{:S(2)}) %collective-permute-start) | collective-permute-done | bytes 229408 | tf_op jit(solution)/shard_map/ppermute | solution.py:20
  17.6 0.6 collective-permute-start.2
  18.2 1.5 %collective-permute-start.4 = (bf16[128,896]{1,0:T(8,128)(2,1)S(1)}, bf16[128,896]{1,0:T(8,128)(2,1)S(1)}, u32[]{:S(2)}, u32[]{:S(2)}) collective-permute-start(bf16[128,896]{1,0:T(8,128)(2,1)S(1)} %collective-permute-done), channel_id=1, source_target_pairs={{0,4},{4,0},{8,12},{12,8},{16,20},{20,16},{24,28},{28,24},{1,5},{5... | collective-permute-start | bytes 688136 | tf_op jit(solution)/shard_map/ppermute | solution.py:20
  19.7 0.0 collective-permute-done.1
  19.7 0.5 collective-permute-start.5
  20.3 0.0 collective-permute-done.3
  20.3 1.0 %constant_dynamic-update-slice_fusion.3 = bf16[512,896]{1,0:T(8,128)(2,1)S(1)} fusion(bf16[128,896]{1,0:T(8,128)(2,1)} %collective-permute-done.3), kind=kLoop, calls=%fused_computation.52 | loop fusion | bytes 458752
  21.2 3.1 %collective-permute-done.2 = bf16[128,896]{1,0:T(8,128)(2,1)S(1)} collective-permute-done((bf16[128,896]{1,0:T(8,128)(2,1)S(1)}, bf16[128,896]{1,0:T(8,128)(2,1)S(1)}, u32[]{:S(2)}, u32[]{:S(2)}) %collective-permute-start.2) | collective-permute-done | bytes 229408 | tf_op jit(solution)/shard_map/ppermute | solution.py:20
  24.4 0.0 copy-done.1
  24.4 0.1 pad_maximum_fusion
  24.4 0.0 copy-done
  24.4 1.6 %fusion.34 = (f32[1536]{0:T(1024)S(1)}, bf16[1536,512]{0,1:T(8,128)(2,1)S(1)}) fusion(bf16[512,896]{1,0:T(8,128)(2,1)S(1)} %pad_maximum_fusion, bf16[1536,768]{1,0:T(8,128)(2,1)S(1)} %copy-done, f32[1536]{0:T(1024)S(1)} %rsqrt_multiply_fusion), kind=kOutput, calls=%fused_computation.61 | convolution fusion | flops 1214642688 | bytes 4732928 | tf_op jit(solution)/shard_map/dot_general | solution.py:44
  26.1 1.3 %collective-permute-start.6 = (bf16[128,896]{1,0:T(8,128)(2,1)S(1)}, bf16[128,896]{1,0:T(8,128)(2,1)S(1)}, u32[]{:S(2)}, u32[]{:S(2)}) collective-permute-start(bf16[128,896]{1,0:T(8,128)(2,1)S(1)} %collective-permute-done.2), channel_id=1, source_target_pairs={{0,4},{4,0},{8,12},{12,8},{16,20},{20,16},{24,28},{28,24},{1,5},{5... | collective-permute-start | bytes 688136 | tf_op jit(solution)/shard_map/ppermute | solution.py:20
  27.4 0.0 collective-permute-done.4
  27.4 4.3 %collective-permute-done.5 = bf16[128,896]{1,0:T(8,128)(2,1)S(1)} collective-permute-done((bf16[128,896]{1,0:T(8,128)(2,1)S(1)}, bf16[128,896]{1,0:T(8,128)(2,1)S(1)}, u32[]{:S(2)}, u32[]{:S(2)}) %collective-permute-start.5) | collective-permute-done | bytes 229408 | tf_op jit(solution)/shard_map/ppermute | solution.py:20
  31.7 0.6 fusion.7
  32.3 3.0 %collective-permute-done.6 = bf16[128,896]{1,0:T(8,128)(2,1)S(1)} collective-permute-done((bf16[128,896]{1,0:T(8,128)(2,1)S(1)}, bf16[128,896]{1,0:T(8,128)(2,1)S(1)}, u32[]{:S(2)}, u32[]{:S(2)}) %collective-permute-start.6) | collective-permute-done | bytes 229408 | tf_op jit(solution)/shard_map/ppermute | solution.py:20
  35.4 1.6 %fusion.35 = (f32[1536]{0:T(1024)S(1)}, bf16[1536,512]{0,1:T(8,128)(2,1)S(1)}) fusion(bf16[512,896]{1,0:T(8,128)(2,1)S(1)} %constant_dynamic-update-slice_fusion, bf16[1536,768]{1,0:T(8,128)(2,1)S(1)} %copy-done, f32[1536]{0:T(1024)S(1)} %rsqrt_multiply_fusion), kind=kOutput, calls=%fused_computation.62 | convolution fusion | flops 1214642688 | bytes 4732928 | tf_op jit(solution)/shard_map/dot_general | solution.py:44
  37.0 0.6 convolution_add_fusion.2
  37.6 0.1 collective-permute-start.7
  37.7 0.1 dynamic_slice.15
  37.8 0.5 collective-permute-start.9
  38.3 1.1 %collective-permute-done.7 = f32[768,128]{1,0:T(8,128)S(1)} collective-permute-done((f32[768,128]{1,0:T(8,128)S(1)}, f32[768,128]{1,0:T(8,128)S(1)}, u32[]{:S(2)}, u32[]{:S(2)}) %collective-permute-start.7) | collective-permute-done | bytes 393248 | tf_op jit(solution)/shard_map/ppermute | solution.py:20
  39.5 1.6 %collective-permute-start.8 = (f32[768,128]{1,0:T(8,128)S(1)}, f32[768,128]{1,0:T(8,128)S(1)}, u32[]{:S(2)}, u32[]{:S(2)}) collective-permute-start(f32[768,128]{1,0:T(8,128)S(1)} %dynamic-slice_add_fusion), channel_id=1, source_target_pairs={{0,2},{1,3},{2,0},{3,1},{4,6},{5,7},{6,4},{7,5},{8,10},{9,11},{10,... | collective-permute-start | bytes 1179656 | tf_op jit(solution)/shard_map/ppermute | solution.py:20
  41.1 0.0 collective-permute-done.9
  41.1 0.1 dynamic-slice_add_fusion.1
  41.1 0.5 collective-permute-start.10
  41.7 9.1 %collective-permute-done.10 = f32[768]{0:T(1024)S(1)} collective-permute-done((f32[768]{0:T(1024)S(1)}, f32[768]{0:T(1024)S(1)}, u32[]{:S(2)}, u32[]{:S(2)}) %collective-permute-start.10) | collective-permute-done | bytes 3104 | tf_op jit(solution)/shard_map/ppermute | solution.py:20
  50.8 0.0 collective-permute-done.8
  50.8 0.2 add_divide_fusion
  51.0 0.8 fusion.36
  51.8 0.1 collective-permute-start.12
  51.9 1.2 %collective-permute-done.12 = f32[128,128]{0,1:T(8,128)S(1)} collective-permute-done((f32[128,128]{0,1:T(8,128)S(1)}, f32[128,128]{0,1:T(8,128)S(1)}, u32[]{:S(2)}, u32[]{:S(2)}) %collective-permute-start.12) | collective-permute-done | bytes 65568 | tf_op jit(solution)/shard_map/ppermute | solution.py:20
  53.1 3.4 %collective-permute-start.13 = (f32[128,128]{0,1:T(8,128)S(1)}, f32[128,128]{0,1:T(8,128)S(1)}, u32[]{:S(2)}, u32[]{:S(2)}) collective-permute-start(f32[128,128]{0,1:T(8,128)S(1)} %add.91), channel_id=1, source_target_pairs={{0,16},{4,20},{8,24},{12,28},{16,0},{20,4},{24,8},{28,12},{1,17},{... | collective-permute-start | bytes 196616 | tf_op jit(solution)/shard_map/ppermute | solution.py:20
  56.6 3.6 %collective-permute-done.13 = f32[128,128]{0,1:T(8,128)S(1)} collective-permute-done((f32[128,128]{0,1:T(8,128)S(1)}, f32[128,128]{0,1:T(8,128)S(1)}, u32[]{:S(2)}, u32[]{:S(2)}) %collective-permute-start.13) | collective-permute-done | bytes 65568 | tf_op jit(solution)/shard_map/ppermute | solution.py:20
  60.2 0.1 collective-permute-start.14
  60.3 4.3 %collective-permute-done.14 = f32[128,128]{0,1:T(8,128)S(1)} collective-permute-done((f32[128,128]{0,1:T(8,128)S(1)}, f32[128,128]{0,1:T(8,128)S(1)}, u32[]{:S(2)}, u32[]{:S(2)}) %collective-permute-start.14) | collective-permute-done | bytes 65568 | tf_op jit(solution)/shard_map/ppermute | solution.py:20
  64.5 1.6 %collective-permute-start.15 = (f32[128,128]{0,1:T(8,128)S(1)}, f32[128,128]{0,1:T(8,128)S(1)}, u32[]{:S(2)}, u32[]{:S(2)}) collective-permute-start(f32[128,128]{0,1:T(8,128)S(1)} %add.93), channel_id=1, source_target_pairs={{0,4},{4,0},{8,12},{12,8},{16,20},{20,16},{24,28},{28,24},{1,5},{5... | collective-permute-start | bytes 196616 | tf_op jit(solution)/shard_map/ppermute | solution.py:20
  66.1 0.0 collective-permute-start.11
  66.1 2.8 %collective-permute-done.15 = f32[128,128]{0,1:T(8,128)S(1)} collective-permute-done((f32[128,128]{0,1:T(8,128)S(1)}, f32[128,128]{0,1:T(8,128)S(1)}, u32[]{:S(2)}, u32[]{:S(2)}) %collective-permute-start.15) | collective-permute-done | bytes 65568 | tf_op jit(solution)/shard_map/ppermute | solution.py:20
  68.9 0.1 copy.6
  69.0 11.7 %cholesky.16 = f32[128,128]{1,0:T(8,128)S(1)} custom-call(f32[128,128]{1,0:T(8,128)S(1)} %fusion.31), custom_call_target="Cholesky" | custom-call | tf_op jit(solution)/shard_map/jit(cholesky)/cholesky | solution.py:24
  80.8 0.6 compare_reduce_fusion
  81.4 0.7 fusion.29
  82.1 9.8 %custom-call.6 = f32[1,128,128]{1,2,0:T(8,128)S(1)} custom-call(f32[1,128,128]{2,1,0:T(8,128)S(1)} %fusion.29), custom_call_target="InvertDiagBlocksLowerTriangular" | custom-call | tf_op jit(solution)/shard_map/triangular_solve | solution.py:25
  91.9 0.0 collective-permute-done.11
  91.9 0.1 broadcast_select_fusion.1
  92.0 1.7 %fusion.13 = f32[1536,128]{1,0:T(8,128)} fusion(f32[768,128]{1,0:T(8,128)S(1)} %get-tuple-element.6, f32[768,128]{1,0:T(8,128)S(1)} %get-tuple-element.5, f32[1,128,128]{1,2,0:T(8,128)S(1)} %custom-call.6), kind=kOutput, calls=%fused_computation.17 | convolution fusion | flops 302186496 | bytes 1638400 | tf_op jit(solution)/shard_map/triangular_solve | solution.py:25
  (15 shorter events, 0.3 us)
Async XLA Ops:
  0.0 24.4 %copy-start.1 = (bf16[128,128]{1,0:T(8,128)(2,1)S(1)}, bf16[128,128]{1,0:T(8,128)(2,1)}, u32[]{:S(2)}) copy-start(bf16[128,128]{1,0:T(8,128)(2,1)} %param.5) | copy-start | bytes 98308
  2.9 21.6 %copy-start = (bf16[1536,768]{1,0:T(8,128)(2,1)S(1)}, bf16[1536,768]{1,0:T(8,128)(2,1)}, u32[]{:S(2)}) copy-start(bf16[1536,768]{1,0:T(8,128)(2,1)} %param.3) | copy-start | bytes 7077892
  2.9 14.7 %collective-permute-start = (bf16[128,896]{1,0:T(8,128)(2,1)S(1)}, bf16[128,896]{1,0:T(8,128)(2,1)S(1)}, u32[]{:S(2)}, u32[]{:S(2)}) collective-permute-start(bf16[128,896]{1,0:T(8,128)(2,1)S(1)} %pad_maximum_fusion.1), channel_id=1, source_target_pairs={{0,16},{4,20},{8,24},{12,28},{16,0},{20,4},{24,8},{28,12},{1,17},{... | collective-permute-start | bytes 688136 | tf_op jit(solution)/shard_map/ppermute | solution.py:20
  7.0 12.7 %collective-permute-start.1 = (bf16[128,896]{1,0:T(8,128)(2,1)S(1)}, bf16[128,896]{1,0:T(8,128)(2,1)S(1)}, u32[]{:S(2)}, u32[]{:S(2)}) collective-permute-start(bf16[128,896]{1,0:T(8,128)(2,1)S(1)} %pad_maximum_fusion.1), channel_id=1, source_target_pairs={{0,8},{4,12},{8,0},{12,4},{16,24},{20,28},{24,16},{28,20},{1,9},{5... | collective-permute-start | bytes 688136 | tf_op jit(solution)/shard_map/ppermute | solution.py:20
  8.6 11.7 %collective-permute-start.3 = (bf16[128,896]{1,0:T(8,128)(2,1)S(1)}, bf16[128,896]{1,0:T(8,128)(2,1)}, u32[]{:S(2)}, u32[]{:S(2)}) collective-permute-start(bf16[128,896]{1,0:T(8,128)(2,1)S(1)} %pad_maximum_fusion.1), channel_id=1, source_target_pairs={{0,4},{4,0},{8,12},{12,8},{16,20},{20,16},{24,28},{28,24},{1,5},{5... | collective-permute-start | bytes 688136 | tf_op jit(solution)/shard_map/ppermute | solution.py:20
  17.6 6.7 %collective-permute-start.2 = (bf16[128,896]{1,0:T(8,128)(2,1)S(1)}, bf16[128,896]{1,0:T(8,128)(2,1)S(1)}, u32[]{:S(2)}, u32[]{:S(2)}) collective-permute-start(bf16[128,896]{1,0:T(8,128)(2,1)S(1)} %collective-permute-done), channel_id=1, source_target_pairs={{0,8},{4,12},{8,0},{12,4},{16,24},{20,28},{24,16},{28,20},{1,9},{5... | collective-permute-start | bytes 688136 | tf_op jit(solution)/shard_map/ppermute | solution.py:20
  18.2 9.1 %collective-permute-start.4 = (bf16[128,896]{1,0:T(8,128)(2,1)S(1)}, bf16[128,896]{1,0:T(8,128)(2,1)S(1)}, u32[]{:S(2)}, u32[]{:S(2)}) collective-permute-start(bf16[128,896]{1,0:T(8,128)(2,1)S(1)} %collective-permute-done), channel_id=1, source_target_pairs={{0,4},{4,0},{8,12},{12,8},{16,20},{20,16},{24,28},{28,24},{1,5},{5... | collective-permute-start | bytes 688136 | tf_op jit(solution)/shard_map/ppermute | solution.py:20
  19.7 11.9 %collective-permute-start.5 = (bf16[128,896]{1,0:T(8,128)(2,1)S(1)}, bf16[128,896]{1,0:T(8,128)(2,1)S(1)}, u32[]{:S(2)}, u32[]{:S(2)}) collective-permute-start(bf16[128,896]{1,0:T(8,128)(2,1)S(1)} %collective-permute-done.1), channel_id=1, source_target_pairs={{0,4},{4,0},{8,12},{12,8},{16,20},{20,16},{24,28},{28,24},{1,5},{5... | collective-permute-start | bytes 688136 | tf_op jit(solution)/shard_map/ppermute | solution.py:20
  26.1 9.3 %collective-permute-start.6 = (bf16[128,896]{1,0:T(8,128)(2,1)S(1)}, bf16[128,896]{1,0:T(8,128)(2,1)S(1)}, u32[]{:S(2)}, u32[]{:S(2)}) collective-permute-start(bf16[128,896]{1,0:T(8,128)(2,1)S(1)} %collective-permute-done.2), channel_id=1, source_target_pairs={{0,4},{4,0},{8,12},{12,8},{16,20},{20,16},{24,28},{28,24},{1,5},{5... | collective-permute-start | bytes 688136 | tf_op jit(solution)/shard_map/ppermute | solution.py:20
  37.6 1.8 %collective-permute-start.7 = (f32[768,128]{1,0:T(8,128)S(1)}, f32[768,128]{1,0:T(8,128)S(1)}, u32[]{:S(2)}, u32[]{:S(2)}) collective-permute-start(f32[768,128]{1,0:T(8,128)S(1)} %constant_dynamic-slice_fusion), channel_id=1, source_target_pairs={{0,1},{1,0},{2,3},{3,2},{4,5},{5,4},{6,7},{7,6},{8,9},{9,8},{10,11... | collective-permute-start | bytes 1179656 | tf_op jit(solution)/shard_map/ppermute | solution.py:20
  37.8 3.2 %collective-permute-start.9 = (f32[768]{0:T(1024)S(1)}, f32[768]{0:T(1024)S(1)}, u32[]{:S(2)}, u32[]{:S(2)}) collective-permute-start(f32[768]{0:T(1024)S(1)} %dynamic_slice.15), channel_id=1, source_target_pairs={{0,1},{1,0},{2,3},{3,2},{4,5},{5,4},{6,7},{7,6},{8,9},{9,8},{10,11... | collective-permute-start | bytes 9224 | tf_op jit(solution)/shard_map/ppermute | solution.py:20
  39.5 11.3 %collective-permute-start.8 = (f32[768,128]{1,0:T(8,128)S(1)}, f32[768,128]{1,0:T(8,128)S(1)}, u32[]{:S(2)}, u32[]{:S(2)}) collective-permute-start(f32[768,128]{1,0:T(8,128)S(1)} %dynamic-slice_add_fusion), channel_id=1, source_target_pairs={{0,2},{1,3},{2,0},{3,1},{4,6},{5,7},{6,4},{7,5},{8,10},{9,11},{10,... | collective-permute-start | bytes 1179656 | tf_op jit(solution)/shard_map/ppermute | solution.py:20
  41.1 9.6 %collective-permute-start.10 = (f32[768]{0:T(1024)S(1)}, f32[768]{0:T(1024)S(1)}, u32[]{:S(2)}, u32[]{:S(2)}) collective-permute-start(f32[768]{0:T(1024)S(1)} %dynamic-slice_add_fusion.1), channel_id=1, source_target_pairs={{0,2},{1,3},{2,0},{3,1},{4,6},{5,7},{6,4},{7,5},{8,10},{9,11},{10,... | collective-permute-start | bytes 9224 | tf_op jit(solution)/shard_map/ppermute | solution.py:20
  51.8 1.3 %collective-permute-start.12 = (f32[128,128]{0,1:T(8,128)S(1)}, f32[128,128]{0,1:T(8,128)S(1)}, u32[]{:S(2)}, u32[]{:S(2)}) collective-permute-start(f32[128,128]{0,1:T(8,128)S(1)} %fusion.36), channel_id=1, source_target_pairs={{0,1},{1,0},{2,3},{3,2},{4,5},{5,4},{6,7},{7,6},{8,9},{9,8},{10,11... | collective-permute-start | bytes 196616 | tf_op jit(solution)/shard_map/ppermute | solution.py:20
  53.1 7.1 %collective-permute-start.13 = (f32[128,128]{0,1:T(8,128)S(1)}, f32[128,128]{0,1:T(8,128)S(1)}, u32[]{:S(2)}, u32[]{:S(2)}) collective-permute-start(f32[128,128]{0,1:T(8,128)S(1)} %add.91), channel_id=1, source_target_pairs={{0,16},{4,20},{8,24},{12,28},{16,0},{20,4},{24,8},{28,12},{1,17},{... | collective-permute-start | bytes 196616 | tf_op jit(solution)/shard_map/ppermute | solution.py:20
  60.2 4.3 %collective-permute-start.14 = (f32[128,128]{0,1:T(8,128)S(1)}, f32[128,128]{0,1:T(8,128)S(1)}, u32[]{:S(2)}, u32[]{:S(2)}) collective-permute-start(f32[128,128]{0,1:T(8,128)S(1)} %add.92), channel_id=1, source_target_pairs={{0,8},{4,12},{8,0},{12,4},{16,24},{20,28},{24,16},{28,20},{1,9},{5... | collective-permute-start | bytes 196616 | tf_op jit(solution)/shard_map/ppermute | solution.py:20
  64.5 4.3 %collective-permute-start.15 = (f32[128,128]{0,1:T(8,128)S(1)}, f32[128,128]{0,1:T(8,128)S(1)}, u32[]{:S(2)}, u32[]{:S(2)}) collective-permute-start(f32[128,128]{0,1:T(8,128)S(1)} %add.93), channel_id=1, source_target_pairs={{0,4},{4,0},{8,12},{12,8},{16,20},{20,16},{24,28},{28,24},{1,5},{5... | collective-permute-start | bytes 196616 | tf_op jit(solution)/shard_map/ppermute | solution.py:20
  66.1 25.8 %collective-permute-start.11 = (f32[768,128]{1,0:T(8,128)S(1)}, f32[768,128]{1,0:T(8,128)S(1)}, u32[]{:S(2)}, u32[]{:S(2)}) collective-permute-start(f32[768,128]{1,0:T(8,128)S(1)} %add_divide_fusion), channel_id=1, source_target_pairs={{0,1},{1,0},{2,3},{3,2},{4,5},{5,4},{6,7},{7,6},{8,9},{9,8},{10,11... | collective-permute-start | bytes 1179656 | tf_op jit(solution)/shard_map/ppermute | solution.py:20

commit v2 on v0

v2 whole, which is shorter than its diff:
```python
import functools
import math

import jax
import jax.numpy as jnp
from jax import lax
from jax.experimental import pallas as pl
from jax.experimental.pallas import tpu as pltpu
from jax.sharding import PartitionSpec as P

kernel_gain = 16.0
LANES = 128
TILE = 256
PANEL = 16
VMEM = pl.BlockSpec(memory_space=pltpu.VMEM)
BF16 = jnp.bfloat16
F32 = jnp.float32


def unit_rows(values):
    floats = values.astype(F32)
    factor = lax.rsqrt(jnp.mean(floats * floats, axis=-1, keepdims=True) + 1e-06) / math.sqrt(
        values.shape[-1]
    )
    return (floats * factor).astype(BF16)


def split3(value):
    high = value.astype(BF16)
    rest = value - high.astype(F32)
    mid = rest.astype(BF16)
    low = (rest - mid.astype(F32)).astype(BF16)
    return high, mid, low


def swap(value, axis, size, bit):
    return lax.ppermute(value, axis, [(i, i ^ bit) for i in range(size)])


def eye(size):
    row = lax.broadcasted_iota(jnp.int32, (size, size), 0)
    column = lax.broadcasted_iota(jnp.int32, (size, size), 1)
    return row == column


def call_on(kernel, out, operands, **rest):
    return pl.pallas_call(
        kernel,
        out_shape=out,
        in_specs=[VMEM] * len(operands),
        out_specs=jax.tree.map(lambda _: VMEM, out),
        scratch_shapes=rest.get("scratch", ()),
        input_output_aliases=rest.get("aliases", {}),
        cost_estimate=pl.CostEstimate(
            flops=rest.get("flops", 0), bytes_accessed=1 << 20, transcendentals=0
        ),
        compiler_params=pltpu.CompilerParams(vmem_limit_bytes=48 << 20),
    )(*operands)


def meet(unit, blocks, total, fresh):
    features = unit.shape[1]
    lands = jnp.concatenate([unit_rows(block[:, :features]) for block in blocks], axis=0)
    vectors = jnp.concatenate([block[:, features:] for block in blocks], axis=0)
    vectors = jnp.concatenate([vectors, jnp.ones_like(vectors)], axis=1)
    for start in range(0, unit.shape[0], TILE):
        rows = slice(start, start + TILE)
        cosine = lax.dot_general(
            unit[rows, :], lands, (((1,), (1,)), ((), ())), preferred_element_type=F32
        )
        kernel = jnp.exp(2.0 * kernel_gain * (cosine - 1.0)).astype(BF16)
        more = jnp.dot(kernel, vectors, preferred_element_type=F32)
        total[rows, :] = more if fresh else total[rows, :] + more


def first_kernel(points, block, unit, total):
    for start in range(0, points.shape[0], TILE):
        rows = slice(start, start + TILE)
        unit[rows, :] = unit_rows(points[rows, :])
    meet(unit, [block], total, True)


def next_kernel(count, unit, *refs):
    blocks, before, total = refs[:count], refs[count], refs[count + 1]
    total[...] = before[...]
    meet(unit, blocks, total, False)


def compact(total, begin, half, out):
    out[:half, :] = total[pl.ds(begin, half), :LANES]
    diagonal = eye(LANES)
    lines = []
    for block in range(half // LANES):
        wide = total[pl.ds(begin + block * LANES, LANES), LANES:]
        lines.append(jnp.sum(jnp.where(diagonal, wide, 0.0), axis=0, keepdims=True))
    lines += [jnp.ones_like(lines[0])] * (-len(lines) % 8)
    out[half:, :] = jnp.concatenate(lines, axis=0)


def last_kernel(count, unit, *refs):
    blocks, before, keep, send, total = refs[:count], *refs[count:]
    total[...] = before[...]
    meet(unit, blocks, total, False)
    half = unit.shape[0] // 2
    core = lax.rem(lax.axis_index("lmk"), 2)
    compact(total, pl.multiple_of(core * half, half), half, keep)
    compact(total, pl.multiple_of(half - core * half, half), half, send)


def pack(value, half, out):
    out[:half, :] = value[:half, :].astype(BF16)
    tail = value[half:, :]
    parts = [part for part in split3(tail)]
    parts.append(jnp.zeros_like(parts[0]))
    out[half:, :] = jnp.concatenate([part.astype(F32) for part in parts], axis=0).astype(BF16)


def unpack(packed, half):
    value = packed[...].astype(F32)
    some = (value.shape[0] - half) // 4
    tail = value[half:, :]
    degree = (tail[2 * some : 3 * some] + tail[some : 2 * some]) + tail[:some]
    return value[:half], degree


def pack_kernel(half, mine, other, out):
    pack(mine[...] + other[...], half, out)


def repack_kernel(half, mine, other, out):
    value, degree = unpack(mine, half)
    more, plus = unpack(other, half)
    pack(jnp.concatenate([value + more, degree + plus], axis=0), half, out)


def gram_kernel(half, mine, other, embed, gram):
    value, degree = unpack(mine, half)
    more, plus = unpack(other, half)
    projected = value + more
    scale = lax.rsqrt(degree + plus)
    diagonal = eye(LANES)
    for block in range(half // LANES):
        rows = slice(block * LANES, (block + 1) * LANES)
        line = jnp.broadcast_to(scale[block : block + 1, :], (LANES, LANES))
        column = jnp.sum(jnp.where(diagonal, line, 0.0), axis=1, keepdims=True)
        embed[rows, :] = projected[rows, :] * column
    gram[...] = lax.dot_general(
        embed[...],
        embed[...],
        (((0,), (0,)), ((), ())),
        precision=lax.Precision.HIGHEST,
        preferred_element_type=F32,
    )


def eliminate(work, rows):
    size = work.shape[0]
    for start in range(0, size, PANEL):
        lines = [
            jnp.broadcast_to(work[start + i : start + i + 1, :], (8, 2 * size))
            for i in range(PANEL)
        ]
        block = {
            (i, k): jnp.broadcast_to(lines[i][:, start + k : start + k + 1], (8, size))
            for i in range(PANEL)
            for k in range(i, PANEL)
        }
        for j in range(PANEL):
            scale = lax.rsqrt(block[j, j])
            line = lines[j] * jnp.concatenate([scale, scale], axis=1)
            rows[start + j : start + j + 1, :] = line[:1]
            times = {i: block[j, i] * scale for i in range(j + 1, PANEL)}
            for i in range(j + 1, PANEL):
                lines[i] = lines[i] - jnp.concatenate([times[i], times[i]], axis=1) * line
                for k in range(i, PANEL):
                    block[i, k] = block[i, k] - times[i] * times[k]
        after = start + PANEL
        if after < size:
            high, mid, low = split3(rows[start:after, :])
            left = jnp.concatenate([high, high, mid, high, low, mid], axis=0)[:, :size]
            right = jnp.concatenate([high, mid, high, low, high, mid], axis=0)
            update = lax.dot_general(
                left, right, (((0,), (0,)), ((), ())), preferred_element_type=F32
            )
            work[after:, :] = work[after:, :] - update[after:, :]


def finish_kernel(points, mine, other, own, theirs, out, work, rows):
    size = mine.shape[0]
    half = own.shape[0]
    work[:, :size] = (mine[...] + other[...]) / points
    work[:, size:] = jnp.where(eye(size), 1.0, 0.0)
    eliminate(work, rows)
    core = lax.rem(lax.axis_index("lmk"), 2)
    for embed, begin in ((own, core * half), (theirs, half - core * half)):
        out[pl.ds(pl.multiple_of(begin, half), half), :] = lax.dot_general(
            embed[...],
            rows[:, size:],
            (((1,), (1,)), ((), ())),
            precision=lax.Precision.HIGHEST,
            preferred_element_type=F32,
        )


def per_device(points, landmarks, eigvecs):
    num_pts = lax.axis_size("pts")
    num_lmk = lax.axis_size("lmk")
    num_rows, features = points.shape
    size = eigvecs.shape[1]
    half = num_rows // 2
    pts_bits = [1 << b for b in reversed(range(num_pts.bit_length() - 1))]
    lmk_bits = [1 << b for b in range(1, num_lmk.bit_length() - 1)]
    shape = jax.ShapeDtypeStruct

    held = {0: jnp.concatenate([landmarks, eigvecs], axis=1)}
    if num_pts == 8:
        hops = [(0, 4), (0, 1), (0, 2), (4, 2), (4, 1), (1, 2), (6, 1)]
        groups = [(1, 2), (4, 6), (5, 3, 7)]
    else:
        hops = []
        for bit in pts_bits:
            hops += [(mask, bit) for mask in [0] + [m ^ b for m, b in hops]]
        order = [mask ^ bit for mask, bit in hops]
        groups = [order[i : i + 4] for i in range(0, len(order), 4)]
    for mask, bit in hops:
        held[mask ^ bit] = swap(held[mask], "pts", num_pts, bit)

    flops = 2 * num_rows * landmarks.shape[0] * (features + 2 * size)
    unit, total = call_on(
        first_kernel,
        (shape((num_rows, features), BF16), shape((num_rows, 2 * size), F32)),
        (points, held[0]),
        flops=flops,
    )
    for group in groups[:-1]:
        total = call_on(
            functools.partial(next_kernel, len(group)),
            shape((num_rows, 2 * size), F32),
            (unit, *[held[mask] for mask in group], total),
            aliases={len(group) + 1: 0},
            flops=flops * len(group),
        )
    group = groups[-1]
    extra = -(-(half // LANES) // 8) * 8
    keep, send = call_on(
        functools.partial(last_kernel, len(group)),
        (shape((half + extra, size), F32),) * 2,
        (unit, *[held[mask] for mask in group], total),
        scratch=[pltpu.VMEM((num_rows, 2 * size), F32)],
        flops=flops * len(group),
    )
    packed = shape((half + 4 * extra, size), BF16)
    mine = call_on(
        functools.partial(pack_kernel, half), packed, (keep, swap(send, "lmk", num_lmk, 1))
    )
    for bit in lmk_bits[:-1]:
        mine = call_on(
            functools.partial(repack_kernel, half), packed, (mine, swap(mine, "lmk", num_lmk, bit))
        )
    embed, gram = call_on(
        functools.partial(gram_kernel, half),
        (shape((half, size), F32), shape((size, size), F32)),
        (mine, swap(mine, "lmk", num_lmk, lmk_bits[-1])),
    )
    gram = gram + swap(gram, "lmk", num_lmk, 1)
    other = swap(embed, "lmk", num_lmk, 1)
    for bit in pts_bits[:-1]:
        gram = gram + swap(gram, "pts", num_pts, bit)
    return call_on(
        functools.partial(finish_kernel, float(num_rows * num_pts)),
        shape((num_rows, size), F32),
        (gram, swap(gram, "pts", num_pts, pts_bits[-1]), embed, other),
        scratch=[pltpu.VMEM((size, 2 * size), F32)] * 2,
    )


def solution(mesh):
    placed = (P("pts", None), P(("pts", "lmk"), None), P(("pts", "lmk"), None))
    return jax.shard_map(
        per_device, mesh=mesh, in_specs=placed, out_specs=P("pts", None), check_vma=False
    )
```

time: 206 us -> 69.8 us (0.34)
  waiting for transfers between devices: 111 us -> 33.5 us
  blocking collectives: 39.4 us -> 0 us
  other arithmetic: 28.5 us -> 0.03 us
  starting transfers between devices: 0.08 us -> 17.3 us
  Pallas kernels: 0 us -> 16.9 us
  matrix products: 13.7 us -> 0 us
  between operations: 13.2 us -> 0.11 us
    psum x2 -> x0, waiting for transfers between devices: 96.2 us -> none  [the longest x1 68.7 us: per_device(): gram = lax.psum(local_gram, 'pts') / total_points]
    ppermute x0 -> x14, waiting for transfers between devices: none -> 33.5 us  [swap(): return lax.ppermute(value, axis, [(i, i ^ bit) for i in range(size)])]
    all_gather x1 -> x0, blocking collectives: 33.2 us -> none  [per_device(): vec_piece = lax.all_gather(eigvecs, 'pts', axis=0, tiled=True)]
    another operation x5 -> x0, other arithmetic: 22.9 us -> none  [the longest x3 12.4 us: finish(): lower = jnp.linalg.cholesky(gram)]
    ppermute x0 -> x14, starting transfers between devices: none -> 17.3 us  [swap(): return lax.ppermute(value, axis, [(i, i ^ bit) for i in range(size)])]
    pallas_call x0 -> x7, Pallas kernels: none -> 16.9 us  [call_on(): pl.pallas_call(kernel, out_shape=out, in_specs=[VMEM] * len(operands), ou...]
    all_gather x1 -> x0, waiting for transfers between devices: 14 us -> none  [per_device(): land_piece = lax.all_gather(landmarks, 'pts', axis=0, tiled=True)]
    dot_general x3 -> x0, matrix products: 10.9 us -> none  [the longest x1 4.96 us: per_device(): lax.dot_general(unit_pts, unit_land, (((1,), (1,)), ((), ())), preferred_...]
  transfers between devices with their start and end apart: 3 -> 14, of which waited for: 3 -> 8; matrix products, arithmetic and copies ran while one was open for 1% -> 0% of each run, Pallas kernels for 0% -> 11%
where the time goes in v2:
time: 69.8 us; the launch traced here: 69.6 us
  waiting for transfers between devices  33.5 us (48%)
  starting transfers between devices  17.3 us (25%)
  Pallas kernels  16.9 us (24%)
  local copies, waits for them, and re-layouts  1.71 us (2%)
    ppermute x14, waiting for transfers between devices, swap(): return lax.ppermute(value, axis, [(i, i ^ bit) for i in range(size)])  33.5 us
    ppermute x14, starting transfers between devices, swap(): return lax.ppermute(value, axis, [(i, i ^ bit) for i in range(size)])  17.3 us
    pallas_call x7, Pallas kernels, call_on(): pl.pallas_call(kernel, out_shape=out, in_specs=[VMEM] * len(operands), ou...  16.9 us
  transfers between devices with their start and end apart: 14, of which 8 were waited for; matrix products, arithmetic and copies ran while one was open for 0% of the time, Pallas kernels for 11%

profile of v2, /device:TPU:0, one launch (start us, length us, event | category | flops | bytes accessed | tf_op | source)
XLA Modules:
  0.0 69.6 jit_solution(13338496930529993011)
XLA Ops:
  0.0 0.9 %constant_dynamic-update-slice_fusion.1 = bf16[128,896]{1,0:T(8,128)(2,1)S(1)} fusion(bf16[128,768]{1,0:T(8,128)(2,1)} %param.4), kind=kLoop, calls=%fused_computation.1 | loop fusion | bytes 393216
  0.9 0.8 %constant_dynamic-update-slice_fusion.block = bf16[128,896]{1,0:T(8,128)(2,1)S(1)} fusion(bf16[128,896]{1,0:T(8,128)(2,1)S(1)} %constant_dynamic-update-slice_fusion.1, bf16[128,128]{1,0:T(8,128)(2,1)} %param.5), kind=kLoop, calls=%fused_computation | loop fusion | bytes 65536 | tf_op jit(solution)/shard_map/concatenate | solution.py:215
  1.7 4.1 %collective-permute-start = (bf16[128,896]{1,0:T(8,128)(2,1)S(1)}, bf16[128,896]{1,0:T(8,128)(2,1)S(1)}, u32[]{:S(2)}, u32[]{:S(2)}) collective-permute-start(bf16[128,896]{1,0:T(8,128)(2,1)S(1)} %constant_dynamic-update-slice_fusion.block), channel_id=1, source_target_pairs={{0,16},{4,20},{8,24},{12,28},{16,0},{20,4},{24,8},{28,12},{1,17},{... | collective-permute-start | bytes 688136 | tf_op jit(solution)/shard_map/ppermute | solution.py:37
  5.8 1.5 %collective-permute-start.2 = (bf16[128,896]{1,0:T(8,128)(2,1)S(1)}, bf16[128,896]{1,0:T(8,128)(2,1)S(1)}, u32[]{:S(2)}, u32[]{:S(2)}) collective-permute-start(bf16[128,896]{1,0:T(8,128)(2,1)S(1)} %constant_dynamic-update-slice_fusion.block), channel_id=1, source_target_pairs={{0,4},{4,0},{8,12},{12,8},{16,20},{20,16},{24,28},{28,24},{1,5},{5... | collective-permute-start | bytes 688136 | tf_op jit(solution)/shard_map/ppermute | solution.py:37
  7.3 9.0 %collective-permute-done.refs_0_ = bf16[128,896]{1,0:T(8,128)(2,1)S(1)} collective-permute-done((bf16[128,896]{1,0:T(8,128)(2,1)S(1)}, bf16[128,896]{1,0:T(8,128)(2,1)S(1)}, u32[]{:S(2)}, u32[]{:S(2)}) %collective-permute-start) | collective-permute-done | bytes 229408 | tf_op jit(solution)/shard_map/ppermute | solution.py:37
  16.3 0.7 %collective-permute-start.4 = (bf16[128,896]{1,0:T(8,128)(2,1)S(1)}, bf16[128,896]{1,0:T(8,128)(2,1)S(1)}, u32[]{:S(2)}, u32[]{:S(2)}) collective-permute-start(bf16[128,896]{1,0:T(8,128)(2,1)S(1)} %collective-permute-done.refs_0_), channel_id=1, source_target_pairs={{0,8},{4,12},{8,0},{12,4},{16,24},{20,28},{24,16},{28,20},{1,9},{5... | collective-permute-start | bytes 688136 | tf_op jit(solution)/shard_map/ppermute | solution.py:37
  17.1 1.3 %collective-permute-start.6 = (bf16[128,896]{1,0:T(8,128)(2,1)S(1)}, bf16[128,896]{1,0:T(8,128)(2,1)S(1)}, u32[]{:S(2)}, u32[]{:S(2)}) collective-permute-start(bf16[128,896]{1,0:T(8,128)(2,1)S(1)} %constant_dynamic-update-slice_fusion.block), channel_id=1, source_target_pairs={{0,8},{4,12},{8,0},{12,4},{16,24},{20,28},{24,16},{28,20},{1,9},{5... | collective-permute-start | bytes 688136 | tf_op jit(solution)/shard_map/ppermute | solution.py:37
  18.4 1.6 %collective-permute-start.1 = (bf16[128,896]{1,0:T(8,128)(2,1)S(1)}, bf16[128,896]{1,0:T(8,128)(2,1)S(1)}, u32[]{:S(2)}, u32[]{:S(2)}) collective-permute-start(bf16[128,896]{1,0:T(8,128)(2,1)S(1)} %collective-permute-done.refs_0_), channel_id=1, source_target_pairs={{0,4},{4,0},{8,12},{12,8},{16,20},{20,16},{24,28},{28,24},{1,5},{5... | collective-permute-start | bytes 688136 | tf_op jit(solution)/shard_map/ppermute | solution.py:37
  19.9 0.0 collective-permute-done.2.refs_0_
  19.9 0.6 collective-permute-start.3
  20.6 4.3 %collective-permute-done.4.refs_1_ = bf16[128,896]{1,0:T(8,128)(2,1)S(1)} collective-permute-done((bf16[128,896]{1,0:T(8,128)(2,1)S(1)}, bf16[128,896]{1,0:T(8,128)(2,1)S(1)}, u32[]{:S(2)}, u32[]{:S(2)}) %collective-permute-start.4) | collective-permute-done | bytes 229408 | tf_op jit(solution)/shard_map/ppermute | solution.py:37
  24.9 1.5 %collective-permute-start.5 = (bf16[128,896]{1,0:T(8,128)(2,1)S(1)}, bf16[128,896]{1,0:T(8,128)(2,1)S(1)}, u32[]{:S(2)}, u32[]{:S(2)}) collective-permute-start(bf16[128,896]{1,0:T(8,128)(2,1)S(1)} %collective-permute-done.4.refs_1_), channel_id=1, source_target_pairs={{0,4},{4,0},{8,12},{12,8},{16,20},{20,16},{24,28},{28,24},{1,5},{5... | collective-permute-start | bytes 688136 | tf_op jit(solution)/shard_map/ppermute | solution.py:37
  26.4 3.4 %shard_map.37 = (bf16[1536,768]{1,0:T(8,128)(2,1)S(1)}, f32[1536,256]{1,0:T(8,128)S(1)}) custom-call(bf16[1536,768]{1,0:T(8,128)(2,1)} %points.1, bf16[128,896]{1,0:T(8,128)(2,1)S(1)} %constant_dynamic-update-slice_fusion.block), custom_call_target="tpu_custom_call" | custom-call | flops 402653184 | bytes 1048576 | tf_op jit(solution)/shard_map/pallas_call | solution.py:47
  29.8 0.0 collective-permute-done.6.refs_1_
  29.8 2.2 %shard_map.38.refs_2_ = f32[1536,256]{1,0:T(8,128)S(1)} custom-call(bf16[1536,768]{1,0:T(8,128)(2,1)S(1)} %get-tuple-element.11.unit, bf16[128,896]{1,0:T(8,128)(2,1)S(1)} %collective-permute-done.2.refs_0_, bf16[128,896]{1,0:T(8,128)(2,1)S(1)} %collective-permute-done.6.refs_1_, ...), custom_call_target="tpu_custom_call", output_to_operand_aliasing={{}: (3, {})} | custom-call | flops 805306368 | bytes 1048576 | tf_op jit(solution)/shard_map/pallas_call | solution.py:47
  32.0 2.2 %shard_map.39.refs_3_ = f32[1536,256]{1,0:T(8,128)S(1)} custom-call(bf16[1536,768]{1,0:T(8,128)(2,1)S(1)} %get-tuple-element.11.unit, bf16[128,896]{1,0:T(8,128)(2,1)S(1)} %collective-permute-done.refs_0_, bf16[128,896]{1,0:T(8,128)(2,1)S(1)} %collective-permute-done.4.refs_1_, f32[1536,256]{1,0:T(8,128)S(1)} %shard_map.38.refs_2_), custom_call_target="tpu_custom_call", output_to_operand_aliasing={{}: (3, {})} | custom-call | flops 805306368 | bytes 1048576 | tf_op jit(solution)/shard_map/pallas_call | solution.py:47
  34.2 0.0 collective-permute-done.1.refs_0_
  34.2 0.0 collective-permute-done.3.refs_1_
  34.2 0.0 collective-permute-done.5.refs_2_
  34.2 2.4 %shard_map.40 = (f32[776,128]{1,0:T(8,128)S(1)}, f32[776,128]{1,0:T(8,128)S(1)}) custom-call(bf16[1536,768]{1,0:T(8,128)(2,1)S(1)} %get-tuple-element.11.unit, bf16[128,896]{1,0:T(8,128)(2,1)S(1)} %collective-permute-done.1.refs_0_, bf16[128,896]{1,0:T(8,128)(2,1)S(1)} %collective-permute-done.3.refs_1_, ...), custom_call_target="tpu_custom_call" | custom-call | flops 1207959552 | bytes 1048576 | tf_op jit(solution)/shard_map/pallas_call | solution.py:47
  36.6 0.1 collective-permute-start.7
  36.7 1.7 %collective-permute-done.7.other = f32[776,128]{1,0:T(8,128)S(1)} collective-permute-done((f32[776,128]{1,0:T(8,128)S(1)}, f32[776,128]{1,0:T(8,128)S(1)}, u32[]{:S(2)}, u32[]{:S(2)}) %collective-permute-start.7) | collective-permute-done | bytes 397344 | tf_op jit(solution)/shard_map/ppermute | solution.py:37
  38.4 1.6 %collective-permute-start.8 = (bf16[800,128]{1,0:T(8,128)(2,1)S(1)}, bf16[800,128]{1,0:T(8,128)(2,1)S(1)}, u32[]{:S(2)}, u32[]{:S(2)}) collective-permute-start(bf16[800,128]{1,0:T(8,128)(2,1)S(1)} %shard_map.41.mine), channel_id=1, source_target_pairs={{0,2},{1,3},{2,0},{3,1},{4,6},{5,7},{6,4},{7,5},{8,10},{9,11},{10,... | collective-permute-start | bytes 614408 | tf_op jit(solution)/shard_map/ppermute | solution.py:37
  40.1 5.5 %collective-permute-done.8.other = bf16[800,128]{1,0:T(8,128)(2,1)S(1)} collective-permute-done((bf16[800,128]{1,0:T(8,128)(2,1)S(1)}, bf16[800,128]{1,0:T(8,128)(2,1)S(1)}, u32[]{:S(2)}, u32[]{:S(2)}) %collective-permute-start.8) | collective-permute-done | bytes 204832 | tf_op jit(solution)/shard_map/ppermute | solution.py:37
  45.6 0.7 %shard_map.42 = (f32[768,128]{1,0:T(8,128)S(1)}, f32[128,128]{1,0:T(8,128)S(1)}) custom-call(bf16[800,128]{1,0:T(8,128)(2,1)S(1)} %shard_map.41.mine, bf16[800,128]{1,0:T(8,128)(2,1)S(1)} %collective-permute-done.8.other), custom_call_target="tpu_custom_call" | custom-call | bytes 1048576 | tf_op jit(solution)/shard_map/pallas_call | solution.py:47
  46.3 0.1 collective-permute-start.13
  46.4 0.5 collective-permute-start.9
  46.9 1.3 %collective-permute-done.9 = f32[128,128]{1,0:T(8,128)S(1)} collective-permute-done((f32[128,128]{1,0:T(8,128)S(1)}, f32[128,128]{1,0:T(8,128)S(1)}, u32[]{:S(2)}, u32[]{:S(2)}) %collective-permute-start.9) | collective-permute-done | bytes 65568 | tf_op jit(solution)/shard_map/ppermute | solution.py:37
  48.2 2.0 %collective-permute-start.10 = (f32[128,128]{1,0:T(8,128)S(1)}, f32[128,128]{1,0:T(8,128)S(1)}, u32[]{:S(2)}, u32[]{:S(2)}) collective-permute-start(f32[128,128]{1,0:T(8,128)S(1)} %add.9), channel_id=1, source_target_pairs={{0,16},{4,20},{8,24},{12,28},{16,0},{20,4},{24,8},{28,12},{1,17},{... | collective-permute-start | bytes 196616 | tf_op jit(solution)/shard_map/ppermute | solution.py:37
  50.2 4.6 %collective-permute-done.10 = f32[128,128]{1,0:T(8,128)S(1)} collective-permute-done((f32[128,128]{1,0:T(8,128)S(1)}, f32[128,128]{1,0:T(8,128)S(1)}, u32[]{:S(2)}, u32[]{:S(2)}) %collective-permute-start.10) | collective-permute-done | bytes 65568 | tf_op jit(solution)/shard_map/ppermute | solution.py:37
  54.9 0.1 collective-permute-start.11
  54.9 4.3 %collective-permute-done.11 = f32[128,128]{1,0:T(8,128)S(1)} collective-permute-done((f32[128,128]{1,0:T(8,128)S(1)}, f32[128,128]{1,0:T(8,128)S(1)}, u32[]{:S(2)}, u32[]{:S(2)}) %collective-permute-start.11) | collective-permute-done | bytes 65568 | tf_op jit(solution)/shard_map/ppermute | solution.py:37
  59.2 1.6 %collective-permute-start.12 = (f32[128,128]{1,0:T(8,128)S(1)}, f32[128,128]{1,0:T(8,128)S(1)}, u32[]{:S(2)}, u32[]{:S(2)}) collective-permute-start(f32[128,128]{1,0:T(8,128)S(1)} %add.11.mine), channel_id=1, source_target_pairs={{0,4},{4,0},{8,12},{12,8},{16,20},{20,16},{24,28},{28,24},{1,5},{5... | collective-permute-start | bytes 196616 | tf_op jit(solution)/shard_map/ppermute | solution.py:37
  60.8 2.8 %collective-permute-done.12.other = f32[128,128]{1,0:T(8,128)S(1)} collective-permute-done((f32[128,128]{1,0:T(8,128)S(1)}, f32[128,128]{1,0:T(8,128)S(1)}, u32[]{:S(2)}, u32[]{:S(2)}) %collective-permute-start.12) | collective-permute-done | bytes 65568 | tf_op jit(solution)/shard_map/ppermute | solution.py:37
  63.5 0.0 collective-permute-done.13.theirs
  63.5 6.1 %shard_map.43 = f32[1536,128]{1,0:T(8,128)} custom-call(f32[128,128]{1,0:T(8,128)S(1)} %add.11.mine, f32[128,128]{1,0:T(8,128)S(1)} %collective-permute-done.12.other, f32[768,128]{1,0:T(8,128)S(1)} %get-tuple-element.16.own, f32[768,128]{1,0:T(8,128)S(1)} %collective-permute-done.13.theirs), custom_call_target="tpu_custom_call" | custom-call | bytes 1048576 | tf_op jit(solution)/shard_map/pallas_call | solution.py:47
  (4 shorter events, 0.1 us)
Async XLA Ops:
  1.7 14.6 %collective-permute-start = (bf16[128,896]{1,0:T(8,128)(2,1)S(1)}, bf16[128,896]{1,0:T(8,128)(2,1)S(1)}, u32[]{:S(2)}, u32[]{:S(2)}) collective-permute-start(bf16[128,896]{1,0:T(8,128)(2,1)S(1)} %constant_dynamic-update-slice_fusion.block), channel_id=1, source_target_pairs={{0,16},{4,20},{8,24},{12,28},{16,0},{20,4},{24,8},{28,12},{1,17},{... | collective-permute-start | bytes 688136 | tf_op jit(solution)/shard_map/ppermute | solution.py:37
  5.8 14.1 %collective-permute-start.2 = (bf16[128,896]{1,0:T(8,128)(2,1)S(1)}, bf16[128,896]{1,0:T(8,128)(2,1)S(1)}, u32[]{:S(2)}, u32[]{:S(2)}) collective-permute-start(bf16[128,896]{1,0:T(8,128)(2,1)S(1)} %constant_dynamic-update-slice_fusion.block), channel_id=1, source_target_pairs={{0,4},{4,0},{8,12},{12,8},{16,20},{20,16},{24,28},{28,24},{1,5},{5... | collective-permute-start | bytes 688136 | tf_op jit(solution)/shard_map/ppermute | solution.py:37
  16.3 8.5 %collective-permute-start.4 = (bf16[128,896]{1,0:T(8,128)(2,1)S(1)}, bf16[128,896]{1,0:T(8,128)(2,1)S(1)}, u32[]{:S(2)}, u32[]{:S(2)}) collective-permute-start(bf16[128,896]{1,0:T(8,128)(2,1)S(1)} %collective-permute-done.refs_0_), channel_id=1, source_target_pairs={{0,8},{4,12},{8,0},{12,4},{16,24},{20,28},{24,16},{28,20},{1,9},{5... | collective-permute-start | bytes 688136 | tf_op jit(solution)/shard_map/ppermute | solution.py:37
  17.1 12.7 %collective-permute-start.6 = (bf16[128,896]{1,0:T(8,128)(2,1)S(1)}, bf16[128,896]{1,0:T(8,128)(2,1)S(1)}, u32[]{:S(2)}, u32[]{:S(2)}) collective-permute-start(bf16[128,896]{1,0:T(8,128)(2,1)S(1)} %constant_dynamic-update-slice_fusion.block), channel_id=1, source_target_pairs={{0,8},{4,12},{8,0},{12,4},{16,24},{20,28},{24,16},{28,20},{1,9},{5... | collective-permute-start | bytes 688136 | tf_op jit(solution)/shard_map/ppermute | solution.py:37
  18.4 15.8 %collective-permute-start.1 = (bf16[128,896]{1,0:T(8,128)(2,1)S(1)}, bf16[128,896]{1,0:T(8,128)(2,1)S(1)}, u32[]{:S(2)}, u32[]{:S(2)}) collective-permute-start(bf16[128,896]{1,0:T(8,128)(2,1)S(1)} %collective-permute-done.refs_0_), channel_id=1, source_target_pairs={{0,4},{4,0},{8,12},{12,8},{16,20},{20,16},{24,28},{28,24},{1,5},{5... | collective-permute-start | bytes 688136 | tf_op jit(solution)/shard_map/ppermute | solution.py:37
  19.9 14.3 %collective-permute-start.3 = (bf16[128,896]{1,0:T(8,128)(2,1)S(1)}, bf16[128,896]{1,0:T(8,128)(2,1)S(1)}, u32[]{:S(2)}, u32[]{:S(2)}) collective-permute-start(bf16[128,896]{1,0:T(8,128)(2,1)S(1)} %collective-permute-done.2.refs_0_), channel_id=1, source_target_pairs={{0,8},{4,12},{8,0},{12,4},{16,24},{20,28},{24,16},{28,20},{1,9},{5... | collective-permute-start | bytes 688136 | tf_op jit(solution)/shard_map/ppermute | solution.py:37
  24.9 9.3 %collective-permute-start.5 = (bf16[128,896]{1,0:T(8,128)(2,1)S(1)}, bf16[128,896]{1,0:T(8,128)(2,1)S(1)}, u32[]{:S(2)}, u32[]{:S(2)}) collective-permute-start(bf16[128,896]{1,0:T(8,128)(2,1)S(1)} %collective-permute-done.4.refs_1_), channel_id=1, source_target_pairs={{0,4},{4,0},{8,12},{12,8},{16,20},{20,16},{24,28},{28,24},{1,5},{5... | collective-permute-start | bytes 688136 | tf_op jit(solution)/shard_map/ppermute | solution.py:37
  36.6 1.8 %collective-permute-start.7 = (f32[776,128]{1,0:T(8,128)S(1)}, f32[776,128]{1,0:T(8,128)S(1)}, u32[]{:S(2)}, u32[]{:S(2)}) collective-permute-start(f32[776,128]{1,0:T(8,128)S(1)} %get-tuple-element.14), channel_id=1, source_target_pairs={{0,1},{1,0},{2,3},{3,2},{4,5},{5,4},{6,7},{7,6},{8,9},{9,8},{10,11... | collective-permute-start | bytes 1191944 | tf_op jit(solution)/shard_map/ppermute | solution.py:37
  38.4 7.2 %collective-permute-start.8 = (bf16[800,128]{1,0:T(8,128)(2,1)S(1)}, bf16[800,128]{1,0:T(8,128)(2,1)S(1)}, u32[]{:S(2)}, u32[]{:S(2)}) collective-permute-start(bf16[800,128]{1,0:T(8,128)(2,1)S(1)} %shard_map.41.mine), channel_id=1, source_target_pairs={{0,2},{1,3},{2,0},{3,1},{4,6},{5,7},{6,4},{7,5},{8,10},{9,11},{10,... | collective-permute-start | bytes 614408 | tf_op jit(solution)/shard_map/ppermute | solution.py:37
  46.3 17.2 %collective-permute-start.13 = (f32[768,128]{1,0:T(8,128)S(1)}, f32[768,128]{1,0:T(8,128)S(1)}, u32[]{:S(2)}, u32[]{:S(2)}) collective-permute-start(f32[768,128]{1,0:T(8,128)S(1)} %get-tuple-element.16.own), channel_id=1, source_target_pairs={{0,1},{1,0},{2,3},{3,2},{4,5},{5,4},{6,7},{7,6},{8,9},{9,8},{10,11... | collective-permute-start | bytes 1179656 | tf_op jit(solution)/shard_map/ppermute | solution.py:37
  46.4 1.8 %collective-permute-start.9 = (f32[128,128]{1,0:T(8,128)S(1)}, f32[128,128]{1,0:T(8,128)S(1)}, u32[]{:S(2)}, u32[]{:S(2)}) collective-permute-start(f32[128,128]{1,0:T(8,128)S(1)} %get-tuple-element.15), channel_id=1, source_target_pairs={{0,1},{1,0},{2,3},{3,2},{4,5},{5,4},{6,7},{7,6},{8,9},{9,8},{10,11... | collective-permute-start | bytes 196616 | tf_op jit(solution)/shard_map/ppermute | solution.py:37
  48.2 6.6 %collective-permute-start.10 = (f32[128,128]{1,0:T(8,128)S(1)}, f32[128,128]{1,0:T(8,128)S(1)}, u32[]{:S(2)}, u32[]{:S(2)}) collective-permute-start(f32[128,128]{1,0:T(8,128)S(1)} %add.9), channel_id=1, source_target_pairs={{0,16},{4,20},{8,24},{12,28},{16,0},{20,4},{24,8},{28,12},{1,17},{... | collective-permute-start | bytes 196616 | tf_op jit(solution)/shard_map/ppermute | solution.py:37
  54.9 4.3 %collective-permute-start.11 = (f32[128,128]{1,0:T(8,128)S(1)}, f32[128,128]{1,0:T(8,128)S(1)}, u32[]{:S(2)}, u32[]{:S(2)}) collective-permute-start(f32[128,128]{1,0:T(8,128)S(1)} %add.10), channel_id=1, source_target_pairs={{0,8},{4,12},{8,0},{12,4},{16,24},{20,28},{24,16},{28,20},{1,9},{5... | collective-permute-start | bytes 196616 | tf_op jit(solution)/shard_map/ppermute | solution.py:37
  59.2 4.3 %collective-permute-start.12 = (f32[128,128]{1,0:T(8,128)S(1)}, f32[128,128]{1,0:T(8,128)S(1)}, u32[]{:S(2)}, u32[]{:S(2)}) collective-permute-start(f32[128,128]{1,0:T(8,128)S(1)} %add.11.mine), channel_id=1, source_target_pairs={{0,4},{4,0},{8,12},{12,8},{16,20},{20,16},{24,28},{28,24},{1,5},{5... | collective-permute-start | bytes 196616 | tf_op jit(solution)/shard_map/ppermute | solution.py:37

commit v3 on v2

--- a/solution.py
+++ b/solution.py
@@ -58,7 +58,19 @@
     )(*operands)
 
 
-def meet(unit, blocks, total, fresh):
+def beside_kernel(left, right, out, sems):
+    width = left.shape[1]
+    copies = [
+        pltpu.make_async_copy(left, out.at[:, :width], sems.at[0]),
+        pltpu.make_async_copy(right, out.at[:, width:], sems.at[1]),
+    ]
+    for copy in copies:
+        copy.start()
+    for copy in copies:
+        copy.wait()
+
+
+def meet(unit, blocks, before, total):
     features = unit.shape[1]
     lands = jnp.concatenate([unit_rows(block[:, :features]) for block in blocks], axis=0)
     vectors = jnp.concatenate([block[:, features:] for block in blocks], axis=0)
@@ -70,20 +82,19 @@
         )
         kernel = jnp.exp(2.0 * kernel_gain * (cosine - 1.0)).astype(BF16)
         more = jnp.dot(kernel, vectors, preferred_element_type=F32)
-        total[rows, :] = more if fresh else total[rows, :] + more
+        total[rows, :] = more if before is None else before[rows, :] + more
 
 
 def first_kernel(points, block, unit, total):
     for start in range(0, points.shape[0], TILE):
         rows = slice(start, start + TILE)
         unit[rows, :] = unit_rows(points[rows, :])
-    meet(unit, [block], total, True)
+    meet(unit, [block], None, total)
 
 
 def next_kernel(count, unit, *refs):
     blocks, before, total = refs[:count], refs[count], refs[count + 1]
-    total[...] = before[...]
-    meet(unit, blocks, total, False)
+    meet(unit, blocks, before, total)
 
 
 def compact(total, begin, half, out):
@@ -99,8 +110,7 @@
 
 def last_kernel(count, unit, *refs):
     blocks, before, keep, send, total = refs[:count], *refs[count:]
-    total[...] = before[...]
-    meet(unit, blocks, total, False)
+    meet(unit, blocks, before, total)
     half = unit.shape[0] // 2
     core = lax.rem(lax.axis_index("lmk"), 2)
     compact(total, pl.multiple_of(core * half, half), half, keep)
@@ -192,12 +202,14 @@
     work[:, size:] = jnp.where(eye(size), 1.0, 0.0)
     eliminate(work, rows)
     core = lax.rem(lax.axis_index("lmk"), 2)
+    high, low, _ = split3(rows[:, size:])
+    right = jnp.concatenate([high, low, high], axis=1)
     for embed, begin in ((own, core * half), (theirs, half - core * half)):
+        high, low, _ = split3(embed[...])
         out[pl.ds(pl.multiple_of(begin, half), half), :] = lax.dot_general(
-            embed[...],
-            rows[:, size:],
+            jnp.concatenate([high, high, low], axis=1),
+            right,
             (((1,), (1,)), ((), ())),
-            precision=lax.Precision.HIGHEST,
             preferred_element_type=F32,
         )
 
@@ -212,35 +224,47 @@
     lmk_bits = [1 << b for b in range(1, num_lmk.bit_length() - 1)]
     shape = jax.ShapeDtypeStruct
 
-    held = {0: jnp.concatenate([landmarks, eigvecs], axis=1)}
+    held = {
+        0: pl.pallas_call(
+            beside_kernel,
+            out_shape=shape((landmarks.shape[0], features + size), BF16),
+            in_specs=[pl.BlockSpec(memory_space=pltpu.HBM)] * 2,
+            out_specs=VMEM,
+            scratch_shapes=[pltpu.SemaphoreType.DMA((2,))],
+        )(landmarks, eigvecs)
+    }
     if num_pts == 8:
-        hops = [(0, 4), (0, 1), (0, 2), (4, 2), (4, 1), (1, 2), (6, 1)]
-        groups = [(1, 2), (4, 6), (5, 3, 7)]
+        rounds = [[(0, 4), (0, 1), (0, 2)], [(4, 2), (4, 1)], [(6, 1), (1, 2)]]
     else:
-        hops = []
+        rounds, order = [], [0]
         for bit in pts_bits:
-            hops += [(mask, bit) for mask in [0] + [m ^ b for m, b in hops]]
-        order = [mask ^ bit for mask, bit in hops]
-        groups = [order[i : i + 4] for i in range(0, len(order), 4)]
-    for mask, bit in hops:
-        held[mask ^ bit] = swap(held[mask], "pts", num_pts, bit)
-
-    flops = 2 * num_rows * landmarks.shape[0] * (features + 2 * size)
-    unit, total = call_on(
-        first_kernel,
-        (shape((num_rows, features), BF16), shape((num_rows, 2 * size), F32)),
-        (points, held[0]),
-        flops=flops,
-    )
-    for group in groups[:-1]:
-        total = call_on(
-            functools.partial(next_kernel, len(group)),
-            shape((num_rows, 2 * size), F32),
-            (unit, *[held[mask] for mask in group], total),
-            aliases={len(group) + 1: 0},
-            flops=flops * len(group),
-        )
-    group = groups[-1]
+            rounds.append([(mask, bit) for mask in order])
+            order = order + [mask ^ bit for mask in order]
+
+    flops = 8 * num_rows * landmarks.shape[0] * (features + 2 * size)
+    ready, unit, total = [0], None, None
+    for hops in rounds:
+        for mask, bit in hops:
+            held[mask ^ bit] = swap(held[mask], "pts", num_pts, bit)
+        if unit is None:
+            unit, total = call_on(
+                first_kernel,
+                (shape((num_rows, features), BF16), shape((num_rows, 2 * size), F32)),
+                (points, held[0]),
+                flops=flops,
+            )
+        else:
+            total = call_on(
+                functools.partial(next_kernel, len(ready)),
+                shape((num_rows, 2 * size), F32),
+                (unit, *[held[mask] for mask in ready], total),
+                aliases={len(ready) + 1: 0},
+                flops=flops * len(ready),
+            )
+        ready = [mask ^ bit for mask, bit in hops]
+        if hops is not rounds[-1]:
+            held, total = lax.optimization_barrier((held, total))
+    group = ready
     extra = -(-(half // LANES) // 8) * 8
     keep, send = call_on(
         functools.partial(last_kernel, len(group)),

time: 69.8 us -> 69.2 us (level)
  starting transfers between devices: 17.3 us -> 14.2 us
  waiting for transfers between devices: 33.5 us -> 35.6 us
  Pallas kernels: 16.9 us -> 18.2 us
  local copies, waits for them, and re-layouts: 1.71 us -> 0.97 us
    ppermute x14, starting transfers between devices: 17.3 us -> 14.2 us  [swap(): return lax.ppermute(value, axis, [(i, i ^ bit) for i in range(size)])]
    ppermute x14, waiting for transfers between devices: 33.5 us -> 35.6 us  [swap(): return lax.ppermute(value, axis, [(i, i ^ bit) for i in range(size)])]
    pallas_call x0 -> x1, Pallas kernels: none -> 1.63 us  [per_device(): pl.pallas_call(beside_kernel, out_shape=shape((landmarks.shape[0], featur...]
    concatenate x1 -> x0, local copies, waits for them, and re-layouts: 0.77 us -> none  [per_device(): held = {0: jnp.concatenate([landmarks, eigvecs], axis=1)}]
  transfers between devices with their start and end apart: 14 -> 14, of which waited for: 8 -> 11; matrix products, arithmetic and copies ran while one was open for 0% -> 0% of each run, Pallas kernels for 11% -> 11%
where the time goes in v3:
time: 69.2 us; the launch traced here: 69 us
  waiting for transfers between devices  35.6 us (51%)
  Pallas kernels  18.2 us (26%)
  starting transfers between devices  14.2 us (21%)
  local copies, waits for them, and re-layouts  0.97 us (1%)
    ppermute x14, waiting for transfers between devices, swap(): return lax.ppermute(value, axis, [(i, i ^ bit) for i in range(size)])  35.6 us
    pallas_call x7, Pallas kernels, call_on(): pl.pallas_call(kernel, out_shape=out, in_specs=[VMEM] * len(operands), ou...  16.5 us
    ppermute x14, starting transfers between devices, swap(): return lax.ppermute(value, axis, [(i, i ^ bit) for i in range(size)])  14.2 us
    pallas_call x1, Pallas kernels, per_device(): pl.pallas_call(beside_kernel, out_shape=shape((landmarks.shape[0], featur...  1.63 us
  transfers between devices with their start and end apart: 14, of which 11 were waited for; matrix products, arithmetic and copies ran while one was open for 0% of the time, Pallas kernels for 11%

profile of v3, /device:TPU:0, one launch (start us, length us, event | category | flops | bytes accessed | tf_op | source)
XLA Modules:
  0.0 69.0 jit_solution(9115598277428365072)
XLA Ops:
  0.0 1.6 %shard_map.37.block = bf16[128,896]{1,0:T(8,128)(2,1)} custom-call(bf16[128,768]{1,0:T(8,128)(2,1)} %left.1, bf16[128,128]{1,0:T(8,128)(2,1)} %right.1), custom_call_target="tpu_custom_call" | custom-call | tf_op jit(solution)/shard_map/pallas_call | solution.py:228
  1.6 3.0 %collective-permute-start = (bf16[128,896]{1,0:T(8,128)(2,1)}, bf16[128,896]{1,0:T(8,128)(2,1)S(1)}, u32[]{:S(2)}, u32[]{:S(2)}) collective-permute-start(bf16[128,896]{1,0:T(8,128)(2,1)} %shard_map.37.block), channel_id=1, source_target_pairs={{0,4},{4,0},{8,12},{12,8},{16,20},{20,16},{24,28},{28,24},{1,5},{5... | collective-permute-start | bytes 688136 | tf_op jit(solution)/shard_map/ppermute | solution.py:37
  4.6 1.6 %collective-permute-start.1 = (bf16[128,896]{1,0:T(8,128)(2,1)}, bf16[128,896]{1,0:T(8,128)(2,1)S(1)}, u32[]{:S(2)}, u32[]{:S(2)}) collective-permute-start(bf16[128,896]{1,0:T(8,128)(2,1)} %shard_map.37.block), channel_id=1, source_target_pairs={{0,8},{4,12},{8,0},{12,4},{16,24},{20,28},{24,16},{28,20},{1,9},{5... | collective-permute-start | bytes 688136 | tf_op jit(solution)/shard_map/ppermute | solution.py:37
  6.2 2.6 %collective-permute-start.2 = (bf16[128,896]{1,0:T(8,128)(2,1)}, bf16[128,896]{1,0:T(8,128)(2,1)S(1)}, u32[]{:S(2)}, u32[]{:S(2)}) collective-permute-start(bf16[128,896]{1,0:T(8,128)(2,1)} %shard_map.37.block), channel_id=1, source_target_pairs={{0,16},{4,20},{8,24},{12,28},{16,0},{20,4},{24,8},{28,12},{1,17},{... | collective-permute-start | bytes 688136 | tf_op jit(solution)/shard_map/ppermute | solution.py:37
  8.8 0.0 copy-start
  8.8 1.0 %copy-done = bf16[128,896]{1,0:T(8,128)(2,1)S(1)} copy-done((bf16[128,896]{1,0:T(8,128)(2,1)S(1)}, bf16[128,896]{1,0:T(8,128)(2,1)}, u32[]{:S(2)}) %copy-start) | copy-done | bytes 229400
  9.8 3.3 %shard_map.38 = (bf16[1536,768]{1,0:T(8,128)(2,1)S(1)}, f32[1536,256]{1,0:T(8,128)S(1)}) custom-call(bf16[1536,768]{1,0:T(8,128)(2,1)} %points.1, bf16[128,896]{1,0:T(8,128)(2,1)S(1)} %copy-done), custom_call_target="tpu_custom_call" | custom-call | flops 1610612736 | bytes 1048576 | tf_op jit(solution)/shard_map/pallas_call | solution.py:47
  13.1 0.0 collective-permute-done.refs_1_
  13.1 3.6 %collective-permute-done.1.refs_2_ = bf16[128,896]{1,0:T(8,128)(2,1)S(1)} collective-permute-done((bf16[128,896]{1,0:T(8,128)(2,1)}, bf16[128,896]{1,0:T(8,128)(2,1)S(1)}, u32[]{:S(2)}, u32[]{:S(2)}) %collective-permute-start.1) | collective-permute-done | bytes 229408 | tf_op jit(solution)/shard_map/ppermute | solution.py:37
  16.7 2.4 %collective-permute-done.2.refs_0_ = bf16[128,896]{1,0:T(8,128)(2,1)S(1)} collective-permute-done((bf16[128,896]{1,0:T(8,128)(2,1)}, bf16[128,896]{1,0:T(8,128)(2,1)S(1)}, u32[]{:S(2)}, u32[]{:S(2)}) %collective-permute-start.2) | collective-permute-done | bytes 229408 | tf_op jit(solution)/shard_map/ppermute | solution.py:37
  19.1 0.5 collective-permute-start.3
  19.6 0.4 collective-permute-start.4
  20.1 2.2 %shard_map.39.refs_2_ = f32[1536,256]{1,0:T(8,128)S(1)} custom-call(bf16[1536,768]{1,0:T(8,128)(2,1)S(1)} %get-tuple-element.19.unit, bf16[128,896]{1,0:T(8,128)(2,1)S(1)} %collective-permute-done.2.refs_0_, bf16[128,896]{1,0:T(8,128)(2,1)S(1)} %collective-permute-done.refs_1_, ...), custom_call_target="tpu_custom_call", output_to_operand_aliasing={{}: (4, {})} | custom-call | flops 4831838208 | bytes 1048576 | tf_op jit(solution)/shard_map/pallas_call | solution.py:47
  22.3 3.8 %collective-permute-done.3.refs_1_ = bf16[128,896]{1,0:T(8,128)(2,1)S(1)} collective-permute-done((bf16[128,896]{1,0:T(8,128)(2,1)S(1)}, bf16[128,896]{1,0:T(8,128)(2,1)S(1)}, u32[]{:S(2)}, u32[]{:S(2)}) %collective-permute-start.3) | collective-permute-done | bytes 229408 | tf_op jit(solution)/shard_map/ppermute | solution.py:37
  26.1 0.0 collective-permute-done.4.refs_0_
  26.1 2.0 %collective-permute-start.5 = (bf16[128,896]{1,0:T(8,128)(2,1)S(1)}, bf16[128,896]{1,0:T(8,128)(2,1)S(1)}, u32[]{:S(2)}, u32[]{:S(2)}) collective-permute-start(bf16[128,896]{1,0:T(8,128)(2,1)S(1)} %collective-permute-done.4.refs_0_), channel_id=1, source_target_pairs={{0,4},{4,0},{8,12},{12,8},{16,20},{20,16},{24,28},{28,24},{1,5},{5... | collective-permute-start | bytes 688136 | tf_op jit(solution)/shard_map/ppermute | solution.py:37
  28.1 0.0 collective-permute-start.6
  28.1 2.2 %shard_map.40.refs_2_ = f32[1536,256]{1,0:T(8,128)S(1)} custom-call(bf16[1536,768]{1,0:T(8,128)(2,1)S(1)} %get-tuple-element.19.unit, bf16[128,896]{1,0:T(8,128)(2,1)S(1)} %collective-permute-done.4.refs_0_, bf16[128,896]{1,0:T(8,128)(2,1)S(1)} %collective-permute-done.3.refs_1_, f32[1536,256]{1,0:T(8,128)S(1)} %shard_map.39.refs_2_), custom_call_target="tpu_custom_call", output_to_operand_aliasing={{}: (3, {})} | custom-call | flops 3221225472 | bytes 1048576 | tf_op jit(solution)/shard_map/pallas_call | solution.py:47
  30.3 1.8 %collective-permute-done.5.refs_0_ = bf16[128,896]{1,0:T(8,128)(2,1)S(1)} collective-permute-done((bf16[128,896]{1,0:T(8,128)(2,1)S(1)}, bf16[128,896]{1,0:T(8,128)(2,1)S(1)}, u32[]{:S(2)}, u32[]{:S(2)}) %collective-permute-start.5) | collective-permute-done | bytes 229408 | tf_op jit(solution)/shard_map/ppermute | solution.py:37
  32.1 2.0 %collective-permute-done.6.refs_1_ = bf16[128,896]{1,0:T(8,128)(2,1)S(1)} collective-permute-done((bf16[128,896]{1,0:T(8,128)(2,1)S(1)}, bf16[128,896]{1,0:T(8,128)(2,1)S(1)}, u32[]{:S(2)}, u32[]{:S(2)}) %collective-permute-start.6) | collective-permute-done | bytes 229408 | tf_op jit(solution)/shard_map/ppermute | solution.py:37
  34.1 2.3 %shard_map.41 = (f32[776,128]{1,0:T(8,128)S(1)}, f32[776,128]{1,0:T(8,128)S(1)}) custom-call(bf16[1536,768]{1,0:T(8,128)(2,1)S(1)} %get-tuple-element.19.unit, bf16[128,896]{1,0:T(8,128)(2,1)S(1)} %collective-permute-done.5.refs_0_, bf16[128,896]{1,0:T(8,128)(2,1)S(1)} %collective-permute-done.6.refs_1_, f32[1536,256]{1,0:T(8,128)S(1)} %shard_map.40.refs_2_), custom_call_target="tpu_custom_call" | custom-call | flops 3221225472 | bytes 1048576 | tf_op jit(solution)/shard_map/pallas_call | solution.py:47
  36.4 0.1 collective-permute-start.7
  36.5 1.7 %collective-permute-done.7.other = f32[776,128]{1,0:T(8,128)S(1)} collective-permute-done((f32[776,128]{1,0:T(8,128)S(1)}, f32[776,128]{1,0:T(8,128)S(1)}, u32[]{:S(2)}, u32[]{:S(2)}) %collective-permute-start.7) | collective-permute-done | bytes 397344 | tf_op jit(solution)/shard_map/ppermute | solution.py:37
  38.2 0.1 shard_map.42.mine
  38.3 1.6 %collective-permute-start.8 = (bf16[800,128]{1,0:T(8,128)(2,1)S(1)}, bf16[800,128]{1,0:T(8,128)(2,1)S(1)}, u32[]{:S(2)}, u32[]{:S(2)}) collective-permute-start(bf16[800,128]{1,0:T(8,128)(2,1)S(1)} %shard_map.42.mine), channel_id=1, source_target_pairs={{0,2},{1,3},{2,0},{3,1},{4,6},{5,7},{6,4},{7,5},{8,10},{9,11},{10,... | collective-permute-start | bytes 614408 | tf_op jit(solution)/shard_map/ppermute | solution.py:37
  39.9 5.6 %collective-permute-done.8.other = bf16[800,128]{1,0:T(8,128)(2,1)S(1)} collective-permute-done((bf16[800,128]{1,0:T(8,128)(2,1)S(1)}, bf16[800,128]{1,0:T(8,128)(2,1)S(1)}, u32[]{:S(2)}, u32[]{:S(2)}) %collective-permute-start.8) | collective-permute-done | bytes 204832 | tf_op jit(solution)/shard_map/ppermute | solution.py:37
  45.5 0.7 %shard_map.43 = (f32[768,128]{1,0:T(8,128)S(1)}, f32[128,128]{1,0:T(8,128)S(1)}) custom-call(bf16[800,128]{1,0:T(8,128)(2,1)S(1)} %shard_map.42.mine, bf16[800,128]{1,0:T(8,128)(2,1)S(1)} %collective-permute-done.8.other), custom_call_target="tpu_custom_call" | custom-call | bytes 1048576 | tf_op jit(solution)/shard_map/pallas_call | solution.py:47
  46.2 0.1 collective-permute-start.13
  46.3 0.5 collective-permute-start.9
  46.8 1.3 %collective-permute-done.9 = f32[128,128]{1,0:T(8,128)S(1)} collective-permute-done((f32[128,128]{1,0:T(8,128)S(1)}, f32[128,128]{1,0:T(8,128)S(1)}, u32[]{:S(2)}, u32[]{:S(2)}) %collective-permute-start.9) | collective-permute-done | bytes 65568 | tf_op jit(solution)/shard_map/ppermute | solution.py:37
  48.1 1.7 %collective-permute-start.10 = (f32[128,128]{1,0:T(8,128)S(1)}, f32[128,128]{1,0:T(8,128)S(1)}, u32[]{:S(2)}, u32[]{:S(2)}) collective-permute-start(f32[128,128]{1,0:T(8,128)S(1)} %add.9), channel_id=1, source_target_pairs={{0,16},{4,20},{8,24},{12,28},{16,0},{20,4},{24,8},{28,12},{1,17},{... | collective-permute-start | bytes 196616 | tf_op jit(solution)/shard_map/ppermute | solution.py:37
  49.8 4.8 %collective-permute-done.10 = f32[128,128]{1,0:T(8,128)S(1)} collective-permute-done((f32[128,128]{1,0:T(8,128)S(1)}, f32[128,128]{1,0:T(8,128)S(1)}, u32[]{:S(2)}, u32[]{:S(2)}) %collective-permute-start.10) | collective-permute-done | bytes 65568 | tf_op jit(solution)/shard_map/ppermute | solution.py:37
  54.6 0.1 collective-permute-start.11
  54.7 4.3 %collective-permute-done.11 = f32[128,128]{1,0:T(8,128)S(1)} collective-permute-done((f32[128,128]{1,0:T(8,128)S(1)}, f32[128,128]{1,0:T(8,128)S(1)}, u32[]{:S(2)}, u32[]{:S(2)}) %collective-permute-start.11) | collective-permute-done | bytes 65568 | tf_op jit(solution)/shard_map/ppermute | solution.py:37
  59.0 0.1 collective-permute-start.12
  59.0 4.2 %collective-permute-done.12.other = f32[128,128]{1,0:T(8,128)S(1)} collective-permute-done((f32[128,128]{1,0:T(8,128)S(1)}, f32[128,128]{1,0:T(8,128)S(1)}, u32[]{:S(2)}, u32[]{:S(2)}) %collective-permute-start.12) | collective-permute-done | bytes 65568 | tf_op jit(solution)/shard_map/ppermute | solution.py:37
  63.3 0.0 collective-permute-done.13.theirs
  63.3 5.8 %shard_map.44 = f32[1536,128]{1,0:T(8,128)} custom-call(f32[128,128]{1,0:T(8,128)S(1)} %add.11.mine, f32[128,128]{1,0:T(8,128)S(1)} %collective-permute-done.12.other, f32[768,128]{1,0:T(8,128)S(1)} %get-tuple-element.32.own, f32[768,128]{1,0:T(8,128)S(1)} %collective-permute-done.13.theirs), custom_call_target="tpu_custom_call" | custom-call | bytes 1048576 | tf_op jit(solution)/shard_map/pallas_call | solution.py:47
  (3 shorter events, 0.0 us)
Async XLA Ops:
  1.6 11.5 %collective-permute-start = (bf16[128,896]{1,0:T(8,128)(2,1)}, bf16[128,896]{1,0:T(8,128)(2,1)S(1)}, u32[]{:S(2)}, u32[]{:S(2)}) collective-permute-start(bf16[128,896]{1,0:T(8,128)(2,1)} %shard_map.37.block), channel_id=1, source_target_pairs={{0,4},{4,0},{8,12},{12,8},{16,20},{20,16},{24,28},{28,24},{1,5},{5... | collective-permute-start | bytes 688136 | tf_op jit(solution)/shard_map/ppermute | solution.py:37
  4.6 12.1 %collective-permute-start.1 = (bf16[128,896]{1,0:T(8,128)(2,1)}, bf16[128,896]{1,0:T(8,128)(2,1)S(1)}, u32[]{:S(2)}, u32[]{:S(2)}) collective-permute-start(bf16[128,896]{1,0:T(8,128)(2,1)} %shard_map.37.block), channel_id=1, source_target_pairs={{0,8},{4,12},{8,0},{12,4},{16,24},{20,28},{24,16},{28,20},{1,9},{5... | collective-permute-start | bytes 688136 | tf_op jit(solution)/shard_map/ppermute | solution.py:37
  6.2 12.9 %collective-permute-start.2 = (bf16[128,896]{1,0:T(8,128)(2,1)}, bf16[128,896]{1,0:T(8,128)(2,1)S(1)}, u32[]{:S(2)}, u32[]{:S(2)}) collective-permute-start(bf16[128,896]{1,0:T(8,128)(2,1)} %shard_map.37.block), channel_id=1, source_target_pairs={{0,16},{4,20},{8,24},{12,28},{16,0},{20,4},{24,8},{28,12},{1,17},{... | collective-permute-start | bytes 688136 | tf_op jit(solution)/shard_map/ppermute | solution.py:37
  8.8 1.0 %copy-start = (bf16[128,896]{1,0:T(8,128)(2,1)S(1)}, bf16[128,896]{1,0:T(8,128)(2,1)}, u32[]{:S(2)}) copy-start(bf16[128,896]{1,0:T(8,128)(2,1)} %shard_map.37.block) | copy-start | bytes 688132
  19.1 7.0 %collective-permute-start.3 = (bf16[128,896]{1,0:T(8,128)(2,1)S(1)}, bf16[128,896]{1,0:T(8,128)(2,1)S(1)}, u32[]{:S(2)}, u32[]{:S(2)}) collective-permute-start(bf16[128,896]{1,0:T(8,128)(2,1)S(1)} %collective-permute-done.2.refs_0_), channel_id=1, source_target_pairs={{0,4},{4,0},{8,12},{12,8},{16,20},{20,16},{24,28},{28,24},{1,5},{5... | collective-permute-start | bytes 688136 | tf_op jit(solution)/shard_map/ppermute | solution.py:37
  19.6 6.5 %collective-permute-start.4 = (bf16[128,896]{1,0:T(8,128)(2,1)S(1)}, bf16[128,896]{1,0:T(8,128)(2,1)S(1)}, u32[]{:S(2)}, u32[]{:S(2)}) collective-permute-start(bf16[128,896]{1,0:T(8,128)(2,1)S(1)} %collective-permute-done.2.refs_0_), channel_id=1, source_target_pairs={{0,8},{4,12},{8,0},{12,4},{16,24},{20,28},{24,16},{28,20},{1,9},{5... | collective-permute-start | bytes 688136 | tf_op jit(solution)/shard_map/ppermute | solution.py:37
  26.1 6.0 %collective-permute-start.5 = (bf16[128,896]{1,0:T(8,128)(2,1)S(1)}, bf16[128,896]{1,0:T(8,128)(2,1)S(1)}, u32[]{:S(2)}, u32[]{:S(2)}) collective-permute-start(bf16[128,896]{1,0:T(8,128)(2,1)S(1)} %collective-permute-done.4.refs_0_), channel_id=1, source_target_pairs={{0,4},{4,0},{8,12},{12,8},{16,20},{20,16},{24,28},{28,24},{1,5},{5... | collective-permute-start | bytes 688136 | tf_op jit(solution)/shard_map/ppermute | solution.py:37
  28.1 6.0 %collective-permute-start.6 = (bf16[128,896]{1,0:T(8,128)(2,1)S(1)}, bf16[128,896]{1,0:T(8,128)(2,1)S(1)}, u32[]{:S(2)}, u32[]{:S(2)}) collective-permute-start(bf16[128,896]{1,0:T(8,128)(2,1)S(1)} %collective-permute-done.refs_1_), channel_id=1, source_target_pairs={{0,8},{4,12},{8,0},{12,4},{16,24},{20,28},{24,16},{28,20},{1,9},{5... | collective-permute-start | bytes 688136 | tf_op jit(solution)/shard_map/ppermute | solution.py:37
  36.4 1.8 %collective-permute-start.7 = (f32[776,128]{1,0:T(8,128)S(1)}, f32[776,128]{1,0:T(8,128)S(1)}, u32[]{:S(2)}, u32[]{:S(2)}) collective-permute-start(f32[776,128]{1,0:T(8,128)S(1)} %get-tuple-element.30), channel_id=1, source_target_pairs={{0,1},{1,0},{2,3},{3,2},{4,5},{5,4},{6,7},{7,6},{8,9},{9,8},{10,11... | collective-permute-start | bytes 1191944 | tf_op jit(solution)/shard_map/ppermute | solution.py:37
  38.3 7.2 %collective-permute-start.8 = (bf16[800,128]{1,0:T(8,128)(2,1)S(1)}, bf16[800,128]{1,0:T(8,128)(2,1)S(1)}, u32[]{:S(2)}, u32[]{:S(2)}) collective-permute-start(bf16[800,128]{1,0:T(8,128)(2,1)S(1)} %shard_map.42.mine), channel_id=1, source_target_pairs={{0,2},{1,3},{2,0},{3,1},{4,6},{5,7},{6,4},{7,5},{8,10},{9,11},{10,... | collective-permute-start | bytes 614408 | tf_op jit(solution)/shard_map/ppermute | solution.py:37
  46.2 17.1 %collective-permute-start.13 = (f32[768,128]{1,0:T(8,128)S(1)}, f32[768,128]{1,0:T(8,128)S(1)}, u32[]{:S(2)}, u32[]{:S(2)}) collective-permute-start(f32[768,128]{1,0:T(8,128)S(1)} %get-tuple-element.32.own), channel_id=1, source_target_pairs={{0,1},{1,0},{2,3},{3,2},{4,5},{5,4},{6,7},{7,6},{8,9},{9,8},{10,11... | collective-permute-start | bytes 1179656 | tf_op jit(solution)/shard_map/ppermute | solution.py:37
  46.3 1.8 %collective-permute-start.9 = (f32[128,128]{1,0:T(8,128)S(1)}, f32[128,128]{1,0:T(8,128)S(1)}, u32[]{:S(2)}, u32[]{:S(2)}) collective-permute-start(f32[128,128]{1,0:T(8,128)S(1)} %get-tuple-element.31), channel_id=1, source_target_pairs={{0,1},{1,0},{2,3},{3,2},{4,5},{5,4},{6,7},{7,6},{8,9},{9,8},{10,11... | collective-permute-start | bytes 196616 | tf_op jit(solution)/shard_map/ppermute | solution.py:37
  48.1 6.5 %collective-permute-start.10 = (f32[128,128]{1,0:T(8,128)S(1)}, f32[128,128]{1,0:T(8,128)S(1)}, u32[]{:S(2)}, u32[]{:S(2)}) collective-permute-start(f32[128,128]{1,0:T(8,128)S(1)} %add.9), channel_id=1, source_target_pairs={{0,16},{4,20},{8,24},{12,28},{16,0},{20,4},{24,8},{28,12},{1,17},{... | collective-permute-start | bytes 196616 | tf_op jit(solution)/shard_map/ppermute | solution.py:37
  54.6 4.3 %collective-permute-start.11 = (f32[128,128]{1,0:T(8,128)S(1)}, f32[128,128]{1,0:T(8,128)S(1)}, u32[]{:S(2)}, u32[]{:S(2)}) collective-permute-start(f32[128,128]{1,0:T(8,128)S(1)} %add.10), channel_id=1, source_target_pairs={{0,8},{4,12},{8,0},{12,4},{16,24},{20,28},{24,16},{28,20},{1,9},{5... | collective-permute-start | bytes 196616 | tf_op jit(solution)/shard_map/ppermute | solution.py:37
  59.0 4.3 %collective-permute-start.12 = (f32[128,128]{1,0:T(8,128)S(1)}, f32[128,128]{1,0:T(8,128)S(1)}, u32[]{:S(2)}, u32[]{:S(2)}) collective-permute-start(f32[128,128]{1,0:T(8,128)S(1)} %add.11.mine), channel_id=1, source_target_pairs={{0,4},{4,0},{8,12},{12,8},{16,20},{20,16},{24,28},{28,24},{1,5},{5... | collective-permute-start | bytes 196616 | tf_op jit(solution)/shard_map/ppermute | solution.py:37

commit v4 on v3

--- a/solution.py
+++ b/solution.py
@@ -10,7 +10,7 @@
 
 kernel_gain = 16.0
 LANES = 128
-TILE = 256
+TILE = 512
 PANEL = 16
 VMEM = pl.BlockSpec(memory_space=pltpu.VMEM)
 BF16 = jnp.bfloat16
@@ -70,19 +70,23 @@
         copy.wait()
 
 
-def meet(unit, blocks, before, total):
+def meet(unit, blocks, before, total, begin=0):
     features = unit.shape[1]
     lands = jnp.concatenate([unit_rows(block[:, :features]) for block in blocks], axis=0)
     vectors = jnp.concatenate([block[:, features:] for block in blocks], axis=0)
     vectors = jnp.concatenate([vectors, jnp.ones_like(vectors)], axis=1)
-    for start in range(0, unit.shape[0], TILE):
-        rows = slice(start, start + TILE)
-        cosine = lax.dot_general(
-            unit[rows, :], lands, (((1,), (1,)), ((), ())), preferred_element_type=F32
+    lands = lands.T
+    for start in range(0, total.shape[0], TILE):
+        size = min(TILE, total.shape[0] - start)
+        rows = pl.ds(start, size)
+        cosine = jnp.dot(
+            unit[pl.ds(begin + start, size), :], lands, preferred_element_type=F32
         )
         kernel = jnp.exp(2.0 * kernel_gain * (cosine - 1.0)).astype(BF16)
         more = jnp.dot(kernel, vectors, preferred_element_type=F32)
-        total[rows, :] = more if before is None else before[rows, :] + more
+        if before is not None:
+            more = more + before[pl.ds(begin + start, size), :]
+        total[rows, :] = more
 
 
 def first_kernel(points, block, unit, total):
@@ -97,24 +101,20 @@
     meet(unit, blocks, before, total)
 
 
-def compact(total, begin, half, out):
-    out[:half, :] = total[pl.ds(begin, half), :LANES]
+def last_kernel(count, mine, unit, *refs):
+    blocks, before, out, total = refs[:count], *refs[count:]
+    half = total.shape[0]
+    core = lax.rem(lax.axis_index("lmk"), 2)
+    begin = core * half if mine else half - core * half
+    meet(unit, blocks, before, total, pl.multiple_of(begin, half))
+    out[:half, :] = total[:, :LANES]
     diagonal = eye(LANES)
     lines = []
-    for block in range(half // LANES):
-        wide = total[pl.ds(begin + block * LANES, LANES), LANES:]
+    for start in range(0, half, LANES):
+        wide = total[start : start + LANES, LANES:]
         lines.append(jnp.sum(jnp.where(diagonal, wide, 0.0), axis=0, keepdims=True))
     lines += [jnp.ones_like(lines[0])] * (-len(lines) % 8)
     out[half:, :] = jnp.concatenate(lines, axis=0)
-
-
-def last_kernel(count, unit, *refs):
-    blocks, before, keep, send, total = refs[:count], *refs[count:]
-    meet(unit, blocks, before, total)
-    half = unit.shape[0] // 2
-    core = lax.rem(lax.axis_index("lmk"), 2)
-    compact(total, pl.multiple_of(core * half, half), half, keep)
-    compact(total, pl.multiple_of(half - core * half, half), half, send)
 
 
 def pack(value, half, out):
@@ -195,10 +195,10 @@
             work[after:, :] = work[after:, :] - update[after:, :]
 
 
-def finish_kernel(points, mine, other, own, theirs, out, work, rows):
-    size = mine.shape[0]
+def finish_kernel(points, gram, own, theirs, out, work, rows):
+    size = gram.shape[0]
     half = own.shape[0]
-    work[:, :size] = (mine[...] + other[...]) / points
+    work[:, :size] = gram[...] / points
     work[:, size:] = jnp.where(eye(size), 1.0, 0.0)
     eliminate(work, rows)
     core = lax.rem(lax.axis_index("lmk"), 2)
@@ -243,7 +243,7 @@
 
     flops = 8 * num_rows * landmarks.shape[0] * (features + 2 * size)
     ready, unit, total = [0], None, None
-    for hops in rounds:
+    for turn, hops in enumerate(rounds):
         for mask, bit in hops:
             held[mask ^ bit] = swap(held[mask], "pts", num_pts, bit)
         if unit is None:
@@ -262,17 +262,22 @@
                 flops=flops * len(ready),
             )
         ready = [mask ^ bit for mask, bit in hops]
-        if hops is not rounds[-1]:
-            held, total = lax.optimization_barrier((held, total))
+        if turn + 1 < len(rounds):
+            tied = list(dict.fromkeys([mask for mask, _ in rounds[turn + 1]] + ready))
+            *fresh, total = lax.optimization_barrier((*[held[mask] for mask in tied], total))
+            held.update(zip(tied, fresh))
     group = ready
     extra = -(-(half // LANES) // 8) * 8
-    keep, send = call_on(
-        functools.partial(last_kernel, len(group)),
-        (shape((half + extra, size), F32),) * 2,
-        (unit, *[held[mask] for mask in group], total),
-        scratch=[pltpu.VMEM((num_rows, 2 * size), F32)],
-        flops=flops * len(group),
-    )
+    send, keep = [
+        call_on(
+            functools.partial(last_kernel, len(group), mine),
+            shape((half + extra, size), F32),
+            (unit, *[held[mask] for mask in group], total),
+            scratch=[pltpu.VMEM((half, 2 * size), F32)],
+            flops=flops * len(group) // 2,
+        )
+        for mine in (False, True)
+    ]
     packed = shape((half + 4 * extra, size), BF16)
     mine = call_on(
         functools.partial(pack_kernel, half), packed, (keep, swap(send, "lmk", num_lmk, 1))
@@ -288,12 +293,14 @@
     )
     gram = gram + swap(gram, "lmk", num_lmk, 1)
     other = swap(embed, "lmk", num_lmk, 1)
-    for bit in pts_bits[:-1]:
-        gram = gram + swap(gram, "pts", num_pts, bit)
+    pieces = gram.reshape(num_pts, size // num_pts, size)
+    pieces = jnp.sum(lax.all_to_all(pieces, "pts", 0, 0, tiled=False), axis=0)
+    pieces = jnp.broadcast_to(pieces, (num_pts, *pieces.shape))
+    gram = lax.all_to_all(pieces, "pts", 0, 0, tiled=False).reshape(size, size)
     return call_on(
         functools.partial(finish_kernel, float(num_rows * num_pts)),
         shape((num_rows, size), F32),
-        (gram, swap(gram, "pts", num_pts, pts_bits[-1]), embed, other),
+        (gram, embed, other),
         scratch=[pltpu.VMEM((size, 2 * size), F32)] * 2,
     )
 

time: 69.2 us -> 71.6 us (1.035)
  blocking collectives: 0 us -> 20.7 us
  waiting for transfers between devices: 35.6 us -> 18.9 us
  starting transfers between devices: 14.2 us -> 13.2 us
    all_to_all x0 -> x2, blocking collectives: none -> 20.7 us  [the longest x1 11.4 us: per_device(): pieces = jnp.sum(lax.all_to_all(pieces, 'pts', 0, 0, tiled=False), axis=0)]
    ppermute x14 -> x11, waiting for transfers between devices: 35.6 us -> 18.9 us  [swap(): return lax.ppermute(value, axis, [(i, i ^ bit) for i in range(size)])]
    ppermute x14 -> x11, starting transfers between devices: 14.2 us -> 13.2 us  [swap(): return lax.ppermute(value, axis, [(i, i ^ bit) for i in range(size)])]
    pallas_call x7 -> x8, Pallas kernels: 16.5 us -> 15.9 us  [call_on(): pl.pallas_call(kernel, out_shape=out, in_specs=[VMEM] * len(operands), ou...]
  transfers between devices with their start and end apart: 14 -> 11, of which waited for: 11 -> 9; matrix products, arithmetic and copies ran while one was open for 0% -> 0% of each run, Pallas kernels for 11% -> 12%
where the time goes in v4:
time: 71.6 us; the launch traced here: 71.4 us
  blocking collectives  20.7 us (29%)
  waiting for transfers between devices  18.9 us (26%)
  Pallas kernels  17.6 us (25%)
  starting transfers between devices  13.2 us (18%)
  local copies, waits for them, and re-layouts  0.98 us (1%)
    ppermute x11, waiting for transfers between devices, swap(): return lax.ppermute(value, axis, [(i, i ^ bit) for i in range(size)])  18.9 us
    pallas_call x8, Pallas kernels, call_on(): pl.pallas_call(kernel, out_shape=out, in_specs=[VMEM] * len(operands), ou...  15.9 us
    ppermute x11, starting transfers between devices, swap(): return lax.ppermute(value, axis, [(i, i ^ bit) for i in range(size)])  13.2 us
    all_to_all x1, blocking collectives, per_device(): pieces = jnp.sum(lax.all_to_all(pieces, 'pts', 0, 0, tiled=False), axis=0)  11.4 us
    all_to_all x1, blocking collectives, per_device(): gram = lax.all_to_all(pieces, 'pts', 0, 0, tiled=False).reshape(size, size)  9.29 us
    pallas_call x1, Pallas kernels, per_device(): pl.pallas_call(beside_kernel, out_shape=shape((landmarks.shape[0], featur...  1.63 us
  transfers between devices with their start and end apart: 11, of which 9 were waited for; matrix products, arithmetic and copies ran while one was open for 0% of the time, Pallas kernels for 12%

profile of v4, /device:TPU:0, one launch (start us, length us, event | category | flops | bytes accessed | tf_op | source)
XLA Modules:
  0.0 71.4 jit_solution(8189333360452300877)
XLA Ops:
  0.0 1.6 %shard_map.37.block = bf16[128,896]{1,0:T(8,128)(2,1)} custom-call(bf16[128,768]{1,0:T(8,128)(2,1)} %left.1, bf16[128,128]{1,0:T(8,128)(2,1)} %right.1), custom_call_target="tpu_custom_call" | custom-call | tf_op jit(solution)/shard_map/pallas_call | solution.py:228
  1.6 4.1 %collective-permute-start = (bf16[128,896]{1,0:T(8,128)(2,1)}, bf16[128,896]{1,0:T(8,128)(2,1)S(1)}, u32[]{:S(2)}, u32[]{:S(2)}) collective-permute-start(bf16[128,896]{1,0:T(8,128)(2,1)} %shard_map.37.block), channel_id=1, source_target_pairs={{0,16},{4,20},{8,24},{12,28},{16,0},{20,4},{24,8},{28,12},{1,17},{... | collective-permute-start | bytes 688136 | tf_op jit(solution)/shard_map/ppermute | solution.py:37
  5.7 1.5 %collective-permute-start.1 = (bf16[128,896]{1,0:T(8,128)(2,1)}, bf16[128,896]{1,0:T(8,128)(2,1)S(1)}, u32[]{:S(2)}, u32[]{:S(2)}) collective-permute-start(bf16[128,896]{1,0:T(8,128)(2,1)} %shard_map.37.block), channel_id=1, source_target_pairs={{0,4},{4,0},{8,12},{12,8},{16,20},{20,16},{24,28},{28,24},{1,5},{5... | collective-permute-start | bytes 688136 | tf_op jit(solution)/shard_map/ppermute | solution.py:37
  7.2 1.6 %collective-permute-start.2 = (bf16[128,896]{1,0:T(8,128)(2,1)}, bf16[128,896]{1,0:T(8,128)(2,1)S(1)}, u32[]{:S(2)}, u32[]{:S(2)}) collective-permute-start(bf16[128,896]{1,0:T(8,128)(2,1)} %shard_map.37.block), channel_id=1, source_target_pairs={{0,8},{4,12},{8,0},{12,4},{16,24},{20,28},{24,16},{28,20},{1,9},{5... | collective-permute-start | bytes 688136 | tf_op jit(solution)/shard_map/ppermute | solution.py:37
  8.8 0.0 copy-start
  8.8 1.0 %copy-done = bf16[128,896]{1,0:T(8,128)(2,1)S(1)} copy-done((bf16[128,896]{1,0:T(8,128)(2,1)S(1)}, bf16[128,896]{1,0:T(8,128)(2,1)}, u32[]{:S(2)}) %copy-start) | copy-done | bytes 229400
  9.8 3.1 %shard_map.38 = (bf16[1536,768]{1,0:T(8,128)(2,1)S(1)}, f32[1536,256]{1,0:T(8,128)S(1)}) custom-call(bf16[1536,768]{1,0:T(8,128)(2,1)} %points.1, bf16[128,896]{1,0:T(8,128)(2,1)S(1)} %copy-done), custom_call_target="tpu_custom_call" | custom-call | flops 1610612736 | bytes 1048576 | tf_op jit(solution)/shard_map/pallas_call | solution.py:47
  12.9 3.7 %collective-permute-done.refs_0_ = bf16[128,896]{1,0:T(8,128)(2,1)S(1)} collective-permute-done((bf16[128,896]{1,0:T(8,128)(2,1)}, bf16[128,896]{1,0:T(8,128)(2,1)S(1)}, u32[]{:S(2)}, u32[]{:S(2)}) %collective-permute-start) | collective-permute-done | bytes 229408 | tf_op jit(solution)/shard_map/ppermute | solution.py:37
  16.6 0.0 collective-permute-done.1.refs_1_
  16.6 1.4 %collective-permute-done.2.refs_2_ = bf16[128,896]{1,0:T(8,128)(2,1)S(1)} collective-permute-done((bf16[128,896]{1,0:T(8,128)(2,1)}, bf16[128,896]{1,0:T(8,128)(2,1)S(1)}, u32[]{:S(2)}, u32[]{:S(2)}) %collective-permute-start.2) | collective-permute-done | bytes 229408 | tf_op jit(solution)/shard_map/ppermute | solution.py:37
  18.0 0.3 collective-permute-start.3
  18.3 1.5 %collective-permute-start.4 = (bf16[128,896]{1,0:T(8,128)(2,1)S(1)}, bf16[128,896]{1,0:T(8,128)(2,1)S(1)}, u32[]{:S(2)}, u32[]{:S(2)}) collective-permute-start(bf16[128,896]{1,0:T(8,128)(2,1)S(1)} %collective-permute-done.refs_0_), channel_id=1, source_target_pairs={{0,4},{4,0},{8,12},{12,8},{16,20},{20,16},{24,28},{28,24},{1,5},{5... | collective-permute-start | bytes 688136 | tf_op jit(solution)/shard_map/ppermute | solution.py:37
  19.7 2.3 %shard_map.39.refs_2_ = f32[1536,256]{1,0:T(8,128)S(1)} custom-call(bf16[1536,768]{1,0:T(8,128)(2,1)S(1)} %get-tuple-element.17.unit, bf16[128,896]{1,0:T(8,128)(2,1)S(1)} %collective-permute-done.refs_0_, bf16[128,896]{1,0:T(8,128)(2,1)S(1)} %collective-permute-done.1.refs_1_, ...), custom_call_target="tpu_custom_call", output_to_operand_aliasing={{}: (4, {})} | custom-call | flops 4831838208 | bytes 1048576 | tf_op jit(solution)/shard_map/pallas_call | solution.py:47
  22.1 2.0 %collective-permute-done.3.refs_0_ = bf16[128,896]{1,0:T(8,128)(2,1)S(1)} collective-permute-done((bf16[128,896]{1,0:T(8,128)(2,1)S(1)}, bf16[128,896]{1,0:T(8,128)(2,1)S(1)}, u32[]{:S(2)}, u32[]{:S(2)}) %collective-permute-start.3) | collective-permute-done | bytes 229408 | tf_op jit(solution)/shard_map/ppermute | solution.py:37
  24.0 0.6 collective-permute-done.4.refs_1_
  24.6 1.4 %collective-permute-start.5 = (bf16[128,896]{1,0:T(8,128)(2,1)S(1)}, bf16[128,896]{1,0:T(8,128)(2,1)S(1)}, u32[]{:S(2)}, u32[]{:S(2)}) collective-permute-start(bf16[128,896]{1,0:T(8,128)(2,1)S(1)} %collective-permute-done.3.refs_0_), channel_id=1, source_target_pairs={{0,4},{4,0},{8,12},{12,8},{16,20},{20,16},{24,28},{28,24},{1,5},{5... | collective-permute-start | bytes 688136 | tf_op jit(solution)/shard_map/ppermute | solution.py:37
  26.0 0.6 collective-permute-start.6
  26.6 1.7 %shard_map.40.refs_2_ = f32[1536,256]{1,0:T(8,128)S(1)} custom-call(bf16[1536,768]{1,0:T(8,128)(2,1)S(1)} %get-tuple-element.17.unit, bf16[128,896]{1,0:T(8,128)(2,1)S(1)} %collective-permute-done.3.refs_0_, bf16[128,896]{1,0:T(8,128)(2,1)S(1)} %collective-permute-done.4.refs_1_, f32[1536,256]{1,0:T(8,128)S(1)} %shard_map.39.refs_2_), custom_call_target="tpu_custom_call", output_to_operand_aliasing={{}: (3, {})} | custom-call | flops 3221225472 | bytes 1048576 | tf_op jit(solution)/shard_map/pallas_call | solution.py:47
  28.3 2.3 %collective-permute-done.5.refs_0_ = bf16[128,896]{1,0:T(8,128)(2,1)S(1)} collective-permute-done((bf16[128,896]{1,0:T(8,128)(2,1)S(1)}, bf16[128,896]{1,0:T(8,128)(2,1)S(1)}, u32[]{:S(2)}, u32[]{:S(2)}) %collective-permute-start.5) | collective-permute-done | bytes 229408 | tf_op jit(solution)/shard_map/ppermute | solution.py:37
  30.6 1.4 %collective-permute-done.6.refs_1_ = bf16[128,896]{1,0:T(8,128)(2,1)S(1)} collective-permute-done((bf16[128,896]{1,0:T(8,128)(2,1)S(1)}, bf16[128,896]{1,0:T(8,128)(2,1)S(1)}, u32[]{:S(2)}, u32[]{:S(2)}) %collective-permute-start.6) | collective-permute-done | bytes 229408 | tf_op jit(solution)/shard_map/ppermute | solution.py:37
  32.1 1.2 %shard_map.42 = f32[776,128]{1,0:T(8,128)S(1)} custom-call(bf16[1536,768]{1,0:T(8,128)(2,1)S(1)} %get-tuple-element.17.unit, bf16[128,896]{1,0:T(8,128)(2,1)S(1)} %collective-permute-done.5.refs_0_, bf16[128,896]{1,0:T(8,128)(2,1)S(1)} %collective-permute-done.6.refs_1_, f32[1536,256]{1,0:T(8,128)S(1)} %shard_map.40.refs_2_), custom_call_target="tpu_custom_call" | custom-call | flops 1610612736 | bytes 1048576 | tf_op jit(solution)/shard_map/pallas_call | solution.py:47
  33.2 0.1 collective-permute-start.7
  33.3 1.2 %shard_map.41.mine = f32[776,128]{1,0:T(8,128)S(1)} custom-call(bf16[1536,768]{1,0:T(8,128)(2,1)S(1)} %get-tuple-element.17.unit, bf16[128,896]{1,0:T(8,128)(2,1)S(1)} %collective-permute-done.5.refs_0_, bf16[128,896]{1,0:T(8,128)(2,1)S(1)} %collective-permute-done.6.refs_1_, f32[1536,256]{1,0:T(8,128)S(1)} %shard_map.40.refs_2_), custom_call_target="tpu_custom_call" | custom-call | flops 1610612736 | bytes 1048576 | tf_op jit(solution)/shard_map/pallas_call | solution.py:47
  34.5 0.6 collective-permute-done.7.other
  35.0 0.1 shard_map.43.mine
  35.1 1.6 %collective-permute-start.8 = (bf16[800,128]{1,0:T(8,128)(2,1)S(1)}, bf16[800,128]{1,0:T(8,128)(2,1)S(1)}, u32[]{:S(2)}, u32[]{:S(2)}) collective-permute-start(bf16[800,128]{1,0:T(8,128)(2,1)S(1)} %shard_map.43.mine), channel_id=1, source_target_pairs={{0,2},{1,3},{2,0},{3,1},{4,6},{5,7},{6,4},{7,5},{8,10},{9,11},{10,... | collective-permute-start | bytes 614408 | tf_op jit(solution)/shard_map/ppermute | solution.py:37
  36.7 5.6 %collective-permute-done.8.other = bf16[800,128]{1,0:T(8,128)(2,1)S(1)} collective-permute-done((bf16[800,128]{1,0:T(8,128)(2,1)S(1)}, bf16[800,128]{1,0:T(8,128)(2,1)S(1)}, u32[]{:S(2)}, u32[]{:S(2)}) %collective-permute-start.8) | collective-permute-done | bytes 204832 | tf_op jit(solution)/shard_map/ppermute | solution.py:37
  42.3 0.7 shard_map.44
  43.0 0.1 collective-permute-start.10
  43.1 0.5 collective-permute-start.9
  43.6 1.3 %collective-permute-done.9 = f32[128,128]{1,0:T(8,128)S(1)} collective-permute-done((f32[128,128]{1,0:T(8,128)S(1)}, f32[128,128]{1,0:T(8,128)S(1)}, u32[]{:S(2)}, u32[]{:S(2)}) %collective-permute-start.9) | collective-permute-done | bytes 65568 | tf_op jit(solution)/shard_map/ppermute | solution.py:37
  44.9 11.4 %all_to_all.10 = f32[8,16,128]{2,1,0:T(8,128)S(1)} all-to-all(f32[8,16,128]{2,1,0:T(8,128)S(1)} %bitcast.3), channel_id=1, replica_groups=mesh['pts'=8,'lmk'=4] {'pts'}, dimensions={0} | all-to-all | bytes 131072 | tf_op jit(solution)/shard_map/all_to_all | solution.py:297
  56.3 9.3 %all_to_all.11 = f32[8,16,128]{2,1,0:T(8,128)S(1)} all-to-all(f32[8,16,128]{2,1,0:T(8,128)S(1)} %broadcast_in_dim.3), channel_id=1, replica_groups=mesh['pts'=8,'lmk'=4] {'pts'}, dimensions={0} | all-to-all | bytes 131072 | tf_op jit(solution)/shard_map/all_to_all | solution.py:299
  65.6 0.0 collective-permute-done.10.theirs
  65.6 5.8 %shard_map.45 = f32[1536,128]{1,0:T(8,128)} custom-call(f32[128,128]{1,0:T(8,128)S(1)} %bitcast.2, f32[768,128]{1,0:T(8,128)S(1)} %get-tuple-element.28.own, f32[768,128]{1,0:T(8,128)S(1)} %collective-permute-done.10.theirs), custom_call_target="tpu_custom_call" | custom-call | bytes 1048576 | tf_op jit(solution)/shard_map/pallas_call | solution.py:47
  (3 shorter events, 0.0 us)
Async XLA Ops:
  1.6 14.9 %collective-permute-start = (bf16[128,896]{1,0:T(8,128)(2,1)}, bf16[128,896]{1,0:T(8,128)(2,1)S(1)}, u32[]{:S(2)}, u32[]{:S(2)}) collective-permute-start(bf16[128,896]{1,0:T(8,128)(2,1)} %shard_map.37.block), channel_id=1, source_target_pairs={{0,16},{4,20},{8,24},{12,28},{16,0},{20,4},{24,8},{28,12},{1,17},{... | collective-permute-start | bytes 688136 | tf_op jit(solution)/shard_map/ppermute | solution.py:37
  5.7 10.8 %collective-permute-start.1 = (bf16[128,896]{1,0:T(8,128)(2,1)}, bf16[128,896]{1,0:T(8,128)(2,1)S(1)}, u32[]{:S(2)}, u32[]{:S(2)}) collective-permute-start(bf16[128,896]{1,0:T(8,128)(2,1)} %shard_map.37.block), channel_id=1, source_target_pairs={{0,4},{4,0},{8,12},{12,8},{16,20},{20,16},{24,28},{28,24},{1,5},{5... | collective-permute-start | bytes 688136 | tf_op jit(solution)/shard_map/ppermute | solution.py:37
  7.2 10.7 %collective-permute-start.2 = (bf16[128,896]{1,0:T(8,128)(2,1)}, bf16[128,896]{1,0:T(8,128)(2,1)S(1)}, u32[]{:S(2)}, u32[]{:S(2)}) collective-permute-start(bf16[128,896]{1,0:T(8,128)(2,1)} %shard_map.37.block), channel_id=1, source_target_pairs={{0,8},{4,12},{8,0},{12,4},{16,24},{20,28},{24,16},{28,20},{1,9},{5... | collective-permute-start | bytes 688136 | tf_op jit(solution)/shard_map/ppermute | solution.py:37
  8.8 1.0 %copy-start = (bf16[128,896]{1,0:T(8,128)(2,1)S(1)}, bf16[128,896]{1,0:T(8,128)(2,1)}, u32[]{:S(2)}) copy-start(bf16[128,896]{1,0:T(8,128)(2,1)} %shard_map.37.block) | copy-start | bytes 688132
  18.0 6.0 %collective-permute-start.3 = (bf16[128,896]{1,0:T(8,128)(2,1)S(1)}, bf16[128,896]{1,0:T(8,128)(2,1)S(1)}, u32[]{:S(2)}, u32[]{:S(2)}) collective-permute-start(bf16[128,896]{1,0:T(8,128)(2,1)S(1)} %collective-permute-done.refs_0_), channel_id=1, source_target_pairs={{0,8},{4,12},{8,0},{12,4},{16,24},{20,28},{24,16},{28,20},{1,9},{5... | collective-permute-start | bytes 688136 | tf_op jit(solution)/shard_map/ppermute | solution.py:37
  18.3 6.3 %collective-permute-start.4 = (bf16[128,896]{1,0:T(8,128)(2,1)S(1)}, bf16[128,896]{1,0:T(8,128)(2,1)S(1)}, u32[]{:S(2)}, u32[]{:S(2)}) collective-permute-start(bf16[128,896]{1,0:T(8,128)(2,1)S(1)} %collective-permute-done.refs_0_), channel_id=1, source_target_pairs={{0,4},{4,0},{8,12},{12,8},{16,20},{20,16},{24,28},{28,24},{1,5},{5... | collective-permute-start | bytes 688136 | tf_op jit(solution)/shard_map/ppermute | solution.py:37
  24.6 6.0 %collective-permute-start.5 = (bf16[128,896]{1,0:T(8,128)(2,1)S(1)}, bf16[128,896]{1,0:T(8,128)(2,1)S(1)}, u32[]{:S(2)}, u32[]{:S(2)}) collective-permute-start(bf16[128,896]{1,0:T(8,128)(2,1)S(1)} %collective-permute-done.3.refs_0_), channel_id=1, source_target_pairs={{0,4},{4,0},{8,12},{12,8},{16,20},{20,16},{24,28},{28,24},{1,5},{5... | collective-permute-start | bytes 688136 | tf_op jit(solution)/shard_map/ppermute | solution.py:37
  26.0 6.0 %collective-permute-start.6 = (bf16[128,896]{1,0:T(8,128)(2,1)S(1)}, bf16[128,896]{1,0:T(8,128)(2,1)S(1)}, u32[]{:S(2)}, u32[]{:S(2)}) collective-permute-start(bf16[128,896]{1,0:T(8,128)(2,1)S(1)} %collective-permute-done.1.refs_1_), channel_id=1, source_target_pairs={{0,8},{4,12},{8,0},{12,4},{16,24},{20,28},{24,16},{28,20},{1,9},{5... | collective-permute-start | bytes 688136 | tf_op jit(solution)/shard_map/ppermute | solution.py:37
  33.2 1.8 %collective-permute-start.7 = (f32[776,128]{1,0:T(8,128)S(1)}, f32[776,128]{1,0:T(8,128)S(1)}, u32[]{:S(2)}, u32[]{:S(2)}) collective-permute-start(f32[776,128]{1,0:T(8,128)S(1)} %shard_map.42), channel_id=1, source_target_pairs={{0,1},{1,0},{2,3},{3,2},{4,5},{5,4},{6,7},{7,6},{8,9},{9,8},{10,11... | collective-permute-start | bytes 1191944 | tf_op jit(solution)/shard_map/ppermute | solution.py:37
  35.1 7.2 %collective-permute-start.8 = (bf16[800,128]{1,0:T(8,128)(2,1)S(1)}, bf16[800,128]{1,0:T(8,128)(2,1)S(1)}, u32[]{:S(2)}, u32[]{:S(2)}) collective-permute-start(bf16[800,128]{1,0:T(8,128)(2,1)S(1)} %shard_map.43.mine), channel_id=1, source_target_pairs={{0,2},{1,3},{2,0},{3,1},{4,6},{5,7},{6,4},{7,5},{8,10},{9,11},{10,... | collective-permute-start | bytes 614408 | tf_op jit(solution)/shard_map/ppermute | solution.py:37
  43.0 22.6 %collective-permute-start.10 = (f32[768,128]{1,0:T(8,128)S(1)}, f32[768,128]{1,0:T(8,128)S(1)}, u32[]{:S(2)}, u32[]{:S(2)}) collective-permute-start(f32[768,128]{1,0:T(8,128)S(1)} %get-tuple-element.28.own), channel_id=1, source_target_pairs={{0,1},{1,0},{2,3},{3,2},{4,5},{5,4},{6,7},{7,6},{8,9},{9,8},{10,11... | collective-permute-start | bytes 1179656 | tf_op jit(solution)/shard_map/ppermute | solution.py:37
  43.1 1.8 %collective-permute-start.9 = (f32[128,128]{1,0:T(8,128)S(1)}, f32[128,128]{1,0:T(8,128)S(1)}, u32[]{:S(2)}, u32[]{:S(2)}) collective-permute-start(f32[128,128]{1,0:T(8,128)S(1)} %get-tuple-element.27), channel_id=1, source_target_pairs={{0,1},{1,0},{2,3},{3,2},{4,5},{5,4},{6,7},{7,6},{8,9},{9,8},{10,11... | collective-permute-start | bytes 196616 | tf_op jit(solution)/shard_map/ppermute | solution.py:37

commit v5 on v4

--- a/solution.py
+++ b/solution.py
@@ -12,6 +12,7 @@
 LANES = 128
 TILE = 512
 PANEL = 16
+SUB = 8
 VMEM = pl.BlockSpec(memory_space=pltpu.VMEM)
 BF16 = jnp.bfloat16
 F32 = jnp.float32
@@ -58,16 +59,9 @@
     )(*operands)
 
 
-def beside_kernel(left, right, out, sems):
-    width = left.shape[1]
-    copies = [
-        pltpu.make_async_copy(left, out.at[:, :width], sems.at[0]),
-        pltpu.make_async_copy(right, out.at[:, width:], sems.at[1]),
-    ]
-    for copy in copies:
-        copy.start()
-    for copy in copies:
-        copy.wait()
+def beside_kernel(left, right, out):
+    out[:, : left.shape[1]] = left[...]
+    out[:, left.shape[1] :] = right[...]
 
 
 def meet(unit, blocks, before, total, begin=0):
@@ -143,7 +137,7 @@
     pack(jnp.concatenate([value + more, degree + plus], axis=0), half, out)
 
 
-def gram_kernel(half, mine, other, embed, gram):
+def gram_kernel(half, mine, other, embed, keep, send, gram):
     value, degree = unpack(mine, half)
     more, plus = unpack(other, half)
     projected = value + more
@@ -161,6 +155,20 @@
         precision=lax.Precision.HIGHEST,
         preferred_element_type=F32,
     )
+    some = keep.shape[0]
+    begin = lax.rem(lax.axis_index("lmk"), 2) * some
+    keep[...] = gram[pl.ds(pl.multiple_of(begin, some), some), :]
+    send[...] = gram[pl.ds(pl.multiple_of(some - begin, some), some), :]
+
+
+def parts_kernel(own, theirs, out):
+    half = own.shape[0]
+    core = lax.rem(lax.axis_index("lmk"), 2)
+    for embed, begin in ((own, core * half), (theirs, half - core * half)):
+        high, low, _ = split3(embed[...])
+        out[pl.ds(pl.multiple_of(begin, half), half), :] = jnp.concatenate(
+            [high, high, low], axis=1
+        )
 
 
 def eliminate(work, rows):
@@ -170,20 +178,26 @@
             jnp.broadcast_to(work[start + i : start + i + 1, :], (8, 2 * size))
             for i in range(PANEL)
         ]
-        block = {
-            (i, k): jnp.broadcast_to(lines[i][:, start + k : start + k + 1], (8, size))
-            for i in range(PANEL)
-            for k in range(i, PANEL)
-        }
-        for j in range(PANEL):
-            scale = lax.rsqrt(block[j, j])
-            line = lines[j] * jnp.concatenate([scale, scale], axis=1)
-            rows[start + j : start + j + 1, :] = line[:1]
-            times = {i: block[j, i] * scale for i in range(j + 1, PANEL)}
-            for i in range(j + 1, PANEL):
-                lines[i] = lines[i] - jnp.concatenate([times[i], times[i]], axis=1) * line
-                for k in range(i, PANEL):
-                    block[i, k] = block[i, k] - times[i] * times[k]
+
+        def lane(i, k):
+            return jnp.broadcast_to(lines[i][:, start + k : start + k + 1], (8, size))
+
+        for sub in range(0, PANEL, SUB):
+            inside = range(sub, sub + SUB)
+            block = {(i, k): lane(i, k) for i in inside for k in range(i, sub + SUB)}
+            for j in inside:
+                scale = lax.rsqrt(block[j, j])
+                lines[j] = lines[j] * jnp.concatenate([scale, scale], axis=1)
+                rows[start + j : start + j + 1, :] = lines[j][:1]
+                times = {
+                    i: block[j, i] * scale if i in inside else lane(j, i)
+                    for i in range(j + 1, PANEL)
+                }
+                for i, factor in times.items():
+                    lines[i] = lines[i] - jnp.concatenate([factor, factor], axis=1) * lines[j]
+                    if i in inside:
+                        for k in range(i, sub + SUB):
+                            block[i, k] = block[i, k] - factor * times[k]
         after = start + PANEL
         if after < size:
             high, mid, low = split3(rows[start:after, :])
@@ -195,23 +209,20 @@
             work[after:, :] = work[after:, :] - update[after:, :]
 
 
-def finish_kernel(points, gram, own, theirs, out, work, rows):
-    size = gram.shape[0]
-    half = own.shape[0]
-    work[:, :size] = gram[...] / points
+def finish_kernel(points, own, theirs, parts, out, work, rows):
+    some, size = own.shape
+    begin = lax.rem(lax.axis_index("lmk"), 2) * some
+    work[pl.ds(pl.multiple_of(begin, some), some), :size] = own[...] / points
+    work[pl.ds(pl.multiple_of(some - begin, some), some), :size] = theirs[...] / points
     work[:, size:] = jnp.where(eye(size), 1.0, 0.0)
     eliminate(work, rows)
-    core = lax.rem(lax.axis_index("lmk"), 2)
     high, low, _ = split3(rows[:, size:])
-    right = jnp.concatenate([high, low, high], axis=1)
-    for embed, begin in ((own, core * half), (theirs, half - core * half)):
-        high, low, _ = split3(embed[...])
-        out[pl.ds(pl.multiple_of(begin, half), half), :] = lax.dot_general(
-            jnp.concatenate([high, high, low], axis=1),
-            right,
-            (((1,), (1,)), ((), ())),
-            preferred_element_type=F32,
-        )
+    out[...] = lax.dot_general(
+        parts[...],
+        jnp.concatenate([high, low, high], axis=1),
+        (((1,), (1,)), ((), ())),
+        preferred_element_type=F32,
+    )
 
 
 def per_device(points, landmarks, eigvecs):
@@ -225,18 +236,17 @@
     shape = jax.ShapeDtypeStruct
 
     held = {
-        0: pl.pallas_call(
+        0: call_on(
             beside_kernel,
-            out_shape=shape((landmarks.shape[0], features + size), BF16),
-            in_specs=[pl.BlockSpec(memory_space=pltpu.HBM)] * 2,
-            out_specs=VMEM,
-            scratch_shapes=[pltpu.SemaphoreType.DMA((2,))],
-        )(landmarks, eigvecs)
+            shape((landmarks.shape[0], features + size), BF16),
+            (landmarks, eigvecs),
+        )
     }
     if num_pts == 8:
-        rounds = [[(0, 4), (0, 1), (0, 2)], [(4, 2), (4, 1)], [(6, 1), (1, 2)]]
+        rounds = [[(0, 4), (0, 2), (0, 1)], [(4, 2), (4, 1)], [(6, 1)]]
+        late = (1, 2)
     else:
-        rounds, order = [], [0]
+        rounds, order, late = [], [0], None
         for bit in pts_bits:
             rounds.append([(mask, bit) for mask in order])
             order = order + [mask ^ bit for mask in order]
@@ -262,11 +272,15 @@
                 flops=flops * len(ready),
             )
         ready = [mask ^ bit for mask, bit in hops]
+        if turn == 1 and late:
+            mask, bit = late
+            held[mask], total = lax.optimization_barrier((held[mask], total))
+            held[mask ^ bit] = swap(held[mask], "pts", num_pts, bit)
         if turn + 1 < len(rounds):
-            tied = list(dict.fromkeys([mask for mask, _ in rounds[turn + 1]] + ready))
+            tied = list(dict.fromkeys(ready + [mask for mask, _ in rounds[turn + 1]]))[::-1]
             *fresh, total = lax.optimization_barrier((*[held[mask] for mask in tied], total))
             held.update(zip(tied, fresh))
-    group = ready
+    group = ready + ([late[0] ^ late[1]] if late else [])
     extra = -(-(half // LANES) // 8) * 8
     send, keep = [
         call_on(
@@ -286,21 +300,24 @@
         mine = call_on(
             functools.partial(repack_kernel, half), packed, (mine, swap(mine, "lmk", num_lmk, bit))
         )
-    embed, gram = call_on(
+    embed, part, send = call_on(
         functools.partial(gram_kernel, half),
-        (shape((half, size), F32), shape((size, size), F32)),
+        (shape((half, size), F32), *[shape((size // 2, size), F32)] * 2),
         (mine, swap(mine, "lmk", num_lmk, lmk_bits[-1])),
-    )
-    gram = gram + swap(gram, "lmk", num_lmk, 1)
-    other = swap(embed, "lmk", num_lmk, 1)
-    pieces = gram.reshape(num_pts, size // num_pts, size)
-    pieces = jnp.sum(lax.all_to_all(pieces, "pts", 0, 0, tiled=False), axis=0)
-    pieces = jnp.broadcast_to(pieces, (num_pts, *pieces.shape))
-    gram = lax.all_to_all(pieces, "pts", 0, 0, tiled=False).reshape(size, size)
+        scratch=[pltpu.VMEM((size, size), F32)],
+    )
+    part = part + swap(send, "lmk", num_lmk, 1)
+    parts = call_on(
+        parts_kernel,
+        shape((num_rows, 3 * size), BF16),
+        (embed, swap(embed, "lmk", num_lmk, 1)),
+    )
+    for bit in pts_bits:
+        part = part + swap(part, "pts", num_pts, bit)
     return call_on(
         functools.partial(finish_kernel, float(num_rows * num_pts)),
         shape((num_rows, size), F32),
-        (gram, embed, other),
+        (part, swap(part, "lmk", num_lmk, 1), parts),
         scratch=[pltpu.VMEM((size, 2 * size), F32)] * 2,
     )
 

time: 71.6 us -> 64.3 us (0.90)
  blocking collectives: 20.7 us -> 0 us
  waiting for transfers between devices: 18.9 us -> 26.1 us
  starting transfers between devices: 13.2 us -> 20 us
  Pallas kernels: 17.6 us -> 16.1 us
    all_to_all x2 -> x0, blocking collectives: 20.7 us -> none  [the longest x1 11.4 us: per_device(): pieces = jnp.sum(lax.all_to_all(pieces, 'pts', 0, 0, tiled=False), axis=0)]
    ppermute x11 -> x15, waiting for transfers between devices: 18.9 us -> 26.1 us  [swap(): return lax.ppermute(value, axis, [(i, i ^ bit) for i in range(size)])]
    ppermute x11 -> x15, starting transfers between devices: 13.2 us -> 20 us  [swap(): return lax.ppermute(value, axis, [(i, i ^ bit) for i in range(size)])]
    pallas_call x1 -> x0, Pallas kernels: 1.63 us -> none  [per_device(): pl.pallas_call(beside_kernel, out_shape=shape((landmarks.shape[0], featur...]
    unnamed x2 -> x4, local copies, waits for them, and re-layouts: 0.97 us -> 1.68 us
    pallas_call x8 -> x10, Pallas kernels: 15.9 us -> 16.1 us  [call_on(): pl.pallas_call(kernel, out_shape=out, in_specs=[VMEM] * len(operands), ou...]
  transfers between devices with their start and end apart: 11 -> 15, of which waited for: 9 -> 13; matrix products, arithmetic and copies ran while one was open for 0% -> 0% of each run, Pallas kernels for 12% -> 13%
where the time goes in v5:
time: 64.3 us; the launch traced here: 64.1 us
  waiting for transfers between devices  26.1 us (41%)
  starting transfers between devices  20 us (31%)
  Pallas kernels  16.1 us (25%)
  local copies, waits for them, and re-layouts  1.68 us (3%)
    ppermute x15, waiting for transfers between devices, swap(): return lax.ppermute(value, axis, [(i, i ^ bit) for i in range(size)])  26.1 us
    ppermute x15, starting transfers between devices, swap(): return lax.ppermute(value, axis, [(i, i ^ bit) for i in range(size)])  20 us
    pallas_call x10, Pallas kernels, call_on(): pl.pallas_call(kernel, out_shape=out, in_specs=[VMEM] * len(operands), ou...  16.1 us
    unnamed x4, local copies, waits for them, and re-layouts  1.68 us
  transfers between devices with their start and end apart: 15, of which 13 were waited for; matrix products, arithmetic and copies ran while one was open for 0% of the time, Pallas kernels for 13%

profile of v5, /device:TPU:0, one launch (start us, length us, event | category | flops | bytes accessed | tf_op | source)
XLA Modules:
  0.0 64.1 jit_solution(4250858997055375986)
XLA Ops:
  0.0 0.0 copy-start
  0.0 0.9 %copy-done = bf16[128,768]{1,0:T(8,128)(2,1)S(1)} copy-done((bf16[128,768]{1,0:T(8,128)(2,1)S(1)}, bf16[128,768]{1,0:T(8,128)(2,1)}, u32[]{:S(2)}) %copy-start) | copy-done | bytes 196632
  0.9 0.0 copy-start.1
  0.9 0.8 %copy-done.1 = bf16[128,128]{1,0:T(8,128)(2,1)S(1)} copy-done((bf16[128,128]{1,0:T(8,128)(2,1)S(1)}, bf16[128,128]{1,0:T(8,128)(2,1)}, u32[]{:S(2)}) %copy-start.1) | copy-done | bytes 32792
  1.7 4.1 %collective-permute-start.2 = (bf16[128,896]{1,0:T(8,128)(2,1)S(1)}, bf16[128,896]{1,0:T(8,128)(2,1)S(1)}, u32[]{:S(2)}, u32[]{:S(2)}) collective-permute-start(bf16[128,896]{1,0:T(8,128)(2,1)S(1)} %shard_map.37.block), channel_id=1, source_target_pairs={{0,16},{4,20},{8,24},{12,28},{16,0},{20,4},{24,8},{28,12},{1,17},{... | collective-permute-start | bytes 688136 | tf_op jit(solution)/shard_map/ppermute | solution.py:38
  5.8 1.6 %collective-permute-start.1 = (bf16[128,896]{1,0:T(8,128)(2,1)S(1)}, bf16[128,896]{1,0:T(8,128)(2,1)S(1)}, u32[]{:S(2)}, u32[]{:S(2)}) collective-permute-start(bf16[128,896]{1,0:T(8,128)(2,1)S(1)} %shard_map.37.block), channel_id=1, source_target_pairs={{0,8},{4,12},{8,0},{12,4},{16,24},{20,28},{24,16},{28,20},{1,9},{5... | collective-permute-start | bytes 688136 | tf_op jit(solution)/shard_map/ppermute | solution.py:38
  7.4 1.5 %collective-permute-start = (bf16[128,896]{1,0:T(8,128)(2,1)S(1)}, bf16[128,896]{1,0:T(8,128)(2,1)S(1)}, u32[]{:S(2)}, u32[]{:S(2)}) collective-permute-start(bf16[128,896]{1,0:T(8,128)(2,1)S(1)} %shard_map.37.block), channel_id=1, source_target_pairs={{0,4},{4,0},{8,12},{12,8},{16,20},{20,16},{24,28},{28,24},{1,5},{5... | collective-permute-start | bytes 688136 | tf_op jit(solution)/shard_map/ppermute | solution.py:38
  8.9 3.1 %shard_map.38 = (bf16[1536,768]{1,0:T(8,128)(2,1)S(1)}, f32[1536,256]{1,0:T(8,128)S(1)}) custom-call(bf16[1536,768]{1,0:T(8,128)(2,1)} %points.1, bf16[128,896]{1,0:T(8,128)(2,1)S(1)} %shard_map.37.block), custom_call_target="tpu_custom_call" | custom-call | flops 1610612736 | bytes 1048576 | tf_op jit(solution)/shard_map/pallas_call | solution.py:48
  12.0 4.5 %collective-permute-done.2.refs_0_ = bf16[128,896]{1,0:T(8,128)(2,1)S(1)} collective-permute-done((bf16[128,896]{1,0:T(8,128)(2,1)S(1)}, bf16[128,896]{1,0:T(8,128)(2,1)S(1)}, u32[]{:S(2)}, u32[]{:S(2)}) %collective-permute-start.2) | collective-permute-done | bytes 229408 | tf_op jit(solution)/shard_map/ppermute | solution.py:38
  16.4 0.2 collective-permute-done.1.refs_1_
  16.6 0.0 collective-permute-done.refs_2_
  16.6 1.5 %collective-permute-start.4 = (bf16[128,896]{1,0:T(8,128)(2,1)S(1)}, bf16[128,896]{1,0:T(8,128)(2,1)S(1)}, u32[]{:S(2)}, u32[]{:S(2)}) collective-permute-start(bf16[128,896]{1,0:T(8,128)(2,1)S(1)} %collective-permute-done.2.refs_0_), channel_id=1, source_target_pairs={{0,8},{4,12},{8,0},{12,4},{16,24},{20,28},{24,16},{28,20},{1,9},{5... | collective-permute-start | bytes 688136 | tf_op jit(solution)/shard_map/ppermute | solution.py:38
  18.1 1.5 %collective-permute-start.3 = (bf16[128,896]{1,0:T(8,128)(2,1)S(1)}, bf16[128,896]{1,0:T(8,128)(2,1)S(1)}, u32[]{:S(2)}, u32[]{:S(2)}) collective-permute-start(bf16[128,896]{1,0:T(8,128)(2,1)S(1)} %collective-permute-done.2.refs_0_), channel_id=1, source_target_pairs={{0,4},{4,0},{8,12},{12,8},{16,20},{20,16},{24,28},{28,24},{1,5},{5... | collective-permute-start | bytes 688136 | tf_op jit(solution)/shard_map/ppermute | solution.py:38
  19.6 2.3 %shard_map.39.refs_2_ = f32[1536,256]{1,0:T(8,128)S(1)} custom-call(bf16[1536,768]{1,0:T(8,128)(2,1)S(1)} %get-tuple-element.19.unit, bf16[128,896]{1,0:T(8,128)(2,1)S(1)} %collective-permute-done.2.refs_0_, bf16[128,896]{1,0:T(8,128)(2,1)S(1)} %collective-permute-done.1.refs_1_, ...), custom_call_target="tpu_custom_call", output_to_operand_aliasing={{}: (4, {})} | custom-call | flops 4831838208 | bytes 1048576 | tf_op jit(solution)/shard_map/pallas_call | solution.py:48
  21.9 0.7 %collective-permute-start.6 = (bf16[128,896]{1,0:T(8,128)(2,1)S(1)}, bf16[128,896]{1,0:T(8,128)(2,1)S(1)}, u32[]{:S(2)}, u32[]{:S(2)}) collective-permute-start(bf16[128,896]{1,0:T(8,128)(2,1)S(1)} %collective-permute-done.refs_2_), channel_id=1, source_target_pairs={{0,8},{4,12},{8,0},{12,4},{16,24},{20,28},{24,16},{28,20},{1,9},{5... | collective-permute-start | bytes 688136 | tf_op jit(solution)/shard_map/ppermute | solution.py:38
  22.6 0.7 %collective-permute-done.4.refs_0_ = bf16[128,896]{1,0:T(8,128)(2,1)S(1)} collective-permute-done((bf16[128,896]{1,0:T(8,128)(2,1)S(1)}, bf16[128,896]{1,0:T(8,128)(2,1)S(1)}, u32[]{:S(2)}, u32[]{:S(2)}) %collective-permute-start.4) | collective-permute-done | bytes 229408 | tf_op jit(solution)/shard_map/ppermute | solution.py:38
  23.3 1.0 %collective-permute-done.3.refs_1_ = bf16[128,896]{1,0:T(8,128)(2,1)S(1)} collective-permute-done((bf16[128,896]{1,0:T(8,128)(2,1)S(1)}, bf16[128,896]{1,0:T(8,128)(2,1)S(1)}, u32[]{:S(2)}, u32[]{:S(2)}) %collective-permute-start.3) | collective-permute-done | bytes 229408 | tf_op jit(solution)/shard_map/ppermute | solution.py:38
  24.3 1.5 %collective-permute-start.5 = (bf16[128,896]{1,0:T(8,128)(2,1)S(1)}, bf16[128,896]{1,0:T(8,128)(2,1)S(1)}, u32[]{:S(2)}, u32[]{:S(2)}) collective-permute-start(bf16[128,896]{1,0:T(8,128)(2,1)S(1)} %collective-permute-done.4.refs_0_), channel_id=1, source_target_pairs={{0,4},{4,0},{8,12},{12,8},{16,20},{20,16},{24,28},{28,24},{1,5},{5... | collective-permute-start | bytes 688136 | tf_op jit(solution)/shard_map/ppermute | solution.py:38
  25.8 1.7 %shard_map.40.refs_2_ = f32[1536,256]{1,0:T(8,128)S(1)} custom-call(bf16[1536,768]{1,0:T(8,128)(2,1)S(1)} %get-tuple-element.19.unit, bf16[128,896]{1,0:T(8,128)(2,1)S(1)} %collective-permute-done.4.refs_0_, bf16[128,896]{1,0:T(8,128)(2,1)S(1)} %collective-permute-done.3.refs_1_, f32[1536,256]{1,0:T(8,128)S(1)} %shard_map.39.refs_2_), custom_call_target="tpu_custom_call", output_to_operand_aliasing={{}: (3, {})} | custom-call | flops 3221225472 | bytes 1048576 | tf_op jit(solution)/shard_map/pallas_call | solution.py:48
  27.5 0.6 collective-permute-done.6.refs_1_
  28.1 2.2 %collective-permute-done.5.refs_0_ = bf16[128,896]{1,0:T(8,128)(2,1)S(1)} collective-permute-done((bf16[128,896]{1,0:T(8,128)(2,1)S(1)}, bf16[128,896]{1,0:T(8,128)(2,1)S(1)}, u32[]{:S(2)}, u32[]{:S(2)}) %collective-permute-start.5) | collective-permute-done | bytes 229408 | tf_op jit(solution)/shard_map/ppermute | solution.py:38
  30.3 1.2 %shard_map.42 = f32[776,128]{1,0:T(8,128)S(1)} custom-call(bf16[1536,768]{1,0:T(8,128)(2,1)S(1)} %get-tuple-element.19.unit, bf16[128,896]{1,0:T(8,128)(2,1)S(1)} %collective-permute-done.5.refs_0_, bf16[128,896]{1,0:T(8,128)(2,1)S(1)} %collective-permute-done.6.refs_1_, f32[1536,256]{1,0:T(8,128)S(1)} %shard_map.40.refs_2_), custom_call_target="tpu_custom_call" | custom-call | flops 1610612736 | bytes 1048576 | tf_op jit(solution)/shard_map/pallas_call | solution.py:48
  31.5 0.1 collective-permute-start.7
  31.6 1.2 %shard_map.41.mine = f32[776,128]{1,0:T(8,128)S(1)} custom-call(bf16[1536,768]{1,0:T(8,128)(2,1)S(1)} %get-tuple-element.19.unit, bf16[128,896]{1,0:T(8,128)(2,1)S(1)} %collective-permute-done.5.refs_0_, bf16[128,896]{1,0:T(8,128)(2,1)S(1)} %collective-permute-done.6.refs_1_, f32[1536,256]{1,0:T(8,128)S(1)} %shard_map.40.refs_2_), custom_call_target="tpu_custom_call" | custom-call | flops 1610612736 | bytes 1048576 | tf_op jit(solution)/shard_map/pallas_call | solution.py:48
  32.7 0.6 collective-permute-done.7.other
  33.3 0.1 shard_map.43.mine
  33.4 1.6 %collective-permute-start.8 = (bf16[800,128]{1,0:T(8,128)(2,1)S(1)}, bf16[800,128]{1,0:T(8,128)(2,1)S(1)}, u32[]{:S(2)}, u32[]{:S(2)}) collective-permute-start(bf16[800,128]{1,0:T(8,128)(2,1)S(1)} %shard_map.43.mine), channel_id=1, source_target_pairs={{0,2},{1,3},{2,0},{3,1},{4,6},{5,7},{6,4},{7,5},{8,10},{9,11},{10,... | collective-permute-start | bytes 614408 | tf_op jit(solution)/shard_map/ppermute | solution.py:38
  34.9 5.6 %collective-permute-done.8.other = bf16[800,128]{1,0:T(8,128)(2,1)S(1)} collective-permute-done((bf16[800,128]{1,0:T(8,128)(2,1)S(1)}, bf16[800,128]{1,0:T(8,128)(2,1)S(1)}, u32[]{:S(2)}, u32[]{:S(2)}) %collective-permute-start.8) | collective-permute-done | bytes 204832 | tf_op jit(solution)/shard_map/ppermute | solution.py:38
  40.5 0.7 %shard_map.44 = (f32[768,128]{1,0:T(8,128)S(1)}, f32[64,128]{1,0:T(8,128)S(1)}, f32[64,128]{1,0:T(8,128)S(1)}) custom-call(bf16[800,128]{1,0:T(8,128)(2,1)S(1)} %shard_map.43.mine, bf16[800,128]{1,0:T(8,128)(2,1)S(1)} %collective-permute-done.8.other), custom_call_target="tpu_custom_call" | custom-call | bytes 1048576 | tf_op jit(solution)/shard_map/pallas_call | solution.py:48
  41.3 0.1 collective-permute-start.14
  41.3 0.5 collective-permute-start.9
  41.8 1.3 %collective-permute-done.9 = f32[64,128]{1,0:T(8,128)S(1)} collective-permute-done((f32[64,128]{1,0:T(8,128)S(1)}, f32[64,128]{1,0:T(8,128)S(1)}, u32[]{:S(2)}, u32[]{:S(2)}) %collective-permute-start.9) | collective-permute-done | bytes 32800 | tf_op jit(solution)/shard_map/ppermute | solution.py:38
  43.1 3.7 %collective-permute-start.10 = (f32[64,128]{1,0:T(8,128)S(1)}, f32[64,128]{1,0:T(8,128)S(1)}, u32[]{:S(2)}, u32[]{:S(2)}) collective-permute-start(f32[64,128]{1,0:T(8,128)S(1)} %add.12), channel_id=1, source_target_pairs={{0,16},{4,20},{8,24},{12,28},{16,0},{20,4},{24,8},{28,12},{1,17},{... | collective-permute-start | bytes 98312 | tf_op jit(solution)/shard_map/ppermute | solution.py:38
  46.8 2.4 %collective-permute-done.10 = f32[64,128]{1,0:T(8,128)S(1)} collective-permute-done((f32[64,128]{1,0:T(8,128)S(1)}, f32[64,128]{1,0:T(8,128)S(1)}, u32[]{:S(2)}, u32[]{:S(2)}) %collective-permute-start.10) | collective-permute-done | bytes 32800 | tf_op jit(solution)/shard_map/ppermute | solution.py:38
  49.2 0.4 collective-permute-start.11
  49.6 3.5 %collective-permute-done.11 = f32[64,128]{1,0:T(8,128)S(1)} collective-permute-done((f32[64,128]{1,0:T(8,128)S(1)}, f32[64,128]{1,0:T(8,128)S(1)}, u32[]{:S(2)}, u32[]{:S(2)}) %collective-permute-start.11) | collective-permute-done | bytes 32800 | tf_op jit(solution)/shard_map/ppermute | solution.py:38
  53.1 1.3 %collective-permute-start.12 = (f32[64,128]{1,0:T(8,128)S(1)}, f32[64,128]{1,0:T(8,128)S(1)}, u32[]{:S(2)}, u32[]{:S(2)}) collective-permute-start(f32[64,128]{1,0:T(8,128)S(1)} %add.14), channel_id=1, source_target_pairs={{0,4},{4,0},{8,12},{12,8},{16,20},{20,16},{24,28},{28,24},{1,5},{5... | collective-permute-start | bytes 98312 | tf_op jit(solution)/shard_map/ppermute | solution.py:38
  54.5 2.6 %collective-permute-done.12 = f32[64,128]{1,0:T(8,128)S(1)} collective-permute-done((f32[64,128]{1,0:T(8,128)S(1)}, f32[64,128]{1,0:T(8,128)S(1)}, u32[]{:S(2)}, u32[]{:S(2)}) %collective-permute-start.12) | collective-permute-done | bytes 32800 | tf_op jit(solution)/shard_map/ppermute | solution.py:38
  57.1 0.0 collective-permute-start.13
  57.1 0.0 collective-permute-done.14.theirs
  57.1 0.1 shard_map.45.parts
  57.2 1.0 %collective-permute-done.13.theirs = f32[64,128]{1,0:T(8,128)S(1)} collective-permute-done((f32[64,128]{1,0:T(8,128)S(1)}, f32[64,128]{1,0:T(8,128)S(1)}, u32[]{:S(2)}, u32[]{:S(2)}) %collective-permute-start.13) | collective-permute-done | bytes 32800 | tf_op jit(solution)/shard_map/ppermute | solution.py:38
  58.3 5.8 %shard_map.46 = f32[1536,128]{1,0:T(8,128)} custom-call(f32[64,128]{1,0:T(8,128)S(1)} %add.15.own, f32[64,128]{1,0:T(8,128)S(1)} %collective-permute-done.13.theirs, bf16[1536,384]{1,0:T(8,128)(2,1)S(1)} %shard_map.45.parts), custom_call_target="tpu_custom_call" | custom-call | bytes 1048576 | tf_op jit(solution)/shard_map/pallas_call | solution.py:48
  (5 shorter events, 0.0 us)
Async XLA Ops:
  0.0 0.9 %copy-start = (bf16[128,768]{1,0:T(8,128)(2,1)S(1)}, bf16[128,768]{1,0:T(8,128)(2,1)}, u32[]{:S(2)}) copy-start(bf16[128,768]{1,0:T(8,128)(2,1)} %left.1) | copy-start | bytes 589828
  0.9 0.8 %copy-start.1 = (bf16[128,128]{1,0:T(8,128)(2,1)S(1)}, bf16[128,128]{1,0:T(8,128)(2,1)}, u32[]{:S(2)}) copy-start(bf16[128,128]{1,0:T(8,128)(2,1)} %right.1) | copy-start | bytes 98308
  1.7 14.7 %collective-permute-start.2 = (bf16[128,896]{1,0:T(8,128)(2,1)S(1)}, bf16[128,896]{1,0:T(8,128)(2,1)S(1)}, u32[]{:S(2)}, u32[]{:S(2)}) collective-permute-start(bf16[128,896]{1,0:T(8,128)(2,1)S(1)} %shard_map.37.block), channel_id=1, source_target_pairs={{0,16},{4,20},{8,24},{12,28},{16,0},{20,4},{24,8},{28,12},{1,17},{... | collective-permute-start | bytes 688136 | tf_op jit(solution)/shard_map/ppermute | solution.py:38
  5.8 10.8 %collective-permute-start.1 = (bf16[128,896]{1,0:T(8,128)(2,1)S(1)}, bf16[128,896]{1,0:T(8,128)(2,1)S(1)}, u32[]{:S(2)}, u32[]{:S(2)}) collective-permute-start(bf16[128,896]{1,0:T(8,128)(2,1)S(1)} %shard_map.37.block), channel_id=1, source_target_pairs={{0,8},{4,12},{8,0},{12,4},{16,24},{20,28},{24,16},{28,20},{1,9},{5... | collective-permute-start | bytes 688136 | tf_op jit(solution)/shard_map/ppermute | solution.py:38
  7.4 9.2 %collective-permute-start = (bf16[128,896]{1,0:T(8,128)(2,1)S(1)}, bf16[128,896]{1,0:T(8,128)(2,1)S(1)}, u32[]{:S(2)}, u32[]{:S(2)}) collective-permute-start(bf16[128,896]{1,0:T(8,128)(2,1)S(1)} %shard_map.37.block), channel_id=1, source_target_pairs={{0,4},{4,0},{8,12},{12,8},{16,20},{20,16},{24,28},{28,24},{1,5},{5... | collective-permute-start | bytes 688136 | tf_op jit(solution)/shard_map/ppermute | solution.py:38
  16.6 6.7 %collective-permute-start.4 = (bf16[128,896]{1,0:T(8,128)(2,1)S(1)}, bf16[128,896]{1,0:T(8,128)(2,1)S(1)}, u32[]{:S(2)}, u32[]{:S(2)}) collective-permute-start(bf16[128,896]{1,0:T(8,128)(2,1)S(1)} %collective-permute-done.2.refs_0_), channel_id=1, source_target_pairs={{0,8},{4,12},{8,0},{12,4},{16,24},{20,28},{24,16},{28,20},{1,9},{5... | collective-permute-start | bytes 688136 | tf_op jit(solution)/shard_map/ppermute | solution.py:38
  18.1 6.2 %collective-permute-start.3 = (bf16[128,896]{1,0:T(8,128)(2,1)S(1)}, bf16[128,896]{1,0:T(8,128)(2,1)S(1)}, u32[]{:S(2)}, u32[]{:S(2)}) collective-permute-start(bf16[128,896]{1,0:T(8,128)(2,1)S(1)} %collective-permute-done.2.refs_0_), channel_id=1, source_target_pairs={{0,4},{4,0},{8,12},{12,8},{16,20},{20,16},{24,28},{28,24},{1,5},{5... | collective-permute-start | bytes 688136 | tf_op jit(solution)/shard_map/ppermute | solution.py:38
  21.9 6.2 %collective-permute-start.6 = (bf16[128,896]{1,0:T(8,128)(2,1)S(1)}, bf16[128,896]{1,0:T(8,128)(2,1)S(1)}, u32[]{:S(2)}, u32[]{:S(2)}) collective-permute-start(bf16[128,896]{1,0:T(8,128)(2,1)S(1)} %collective-permute-done.refs_2_), channel_id=1, source_target_pairs={{0,8},{4,12},{8,0},{12,4},{16,24},{20,28},{24,16},{28,20},{1,9},{5... | collective-permute-start | bytes 688136 | tf_op jit(solution)/shard_map/ppermute | solution.py:38
  24.3 6.0 %collective-permute-start.5 = (bf16[128,896]{1,0:T(8,128)(2,1)S(1)}, bf16[128,896]{1,0:T(8,128)(2,1)S(1)}, u32[]{:S(2)}, u32[]{:S(2)}) collective-permute-start(bf16[128,896]{1,0:T(8,128)(2,1)S(1)} %collective-permute-done.4.refs_0_), channel_id=1, source_target_pairs={{0,4},{4,0},{8,12},{12,8},{16,20},{20,16},{24,28},{28,24},{1,5},{5... | collective-permute-start | bytes 688136 | tf_op jit(solution)/shard_map/ppermute | solution.py:38
  31.5 1.8 %collective-permute-start.7 = (f32[776,128]{1,0:T(8,128)S(1)}, f32[776,128]{1,0:T(8,128)S(1)}, u32[]{:S(2)}, u32[]{:S(2)}) collective-permute-start(f32[776,128]{1,0:T(8,128)S(1)} %shard_map.42), channel_id=1, source_target_pairs={{0,1},{1,0},{2,3},{3,2},{4,5},{5,4},{6,7},{7,6},{8,9},{9,8},{10,11... | collective-permute-start | bytes 1191944 | tf_op jit(solution)/shard_map/ppermute | solution.py:38
  33.4 7.2 %collective-permute-start.8 = (bf16[800,128]{1,0:T(8,128)(2,1)S(1)}, bf16[800,128]{1,0:T(8,128)(2,1)S(1)}, u32[]{:S(2)}, u32[]{:S(2)}) collective-permute-start(bf16[800,128]{1,0:T(8,128)(2,1)S(1)} %shard_map.43.mine), channel_id=1, source_target_pairs={{0,2},{1,3},{2,0},{3,1},{4,6},{5,7},{6,4},{7,5},{8,10},{9,11},{10,... | collective-permute-start | bytes 614408 | tf_op jit(solution)/shard_map/ppermute | solution.py:38
  41.3 15.8 %collective-permute-start.14 = (f32[768,128]{1,0:T(8,128)S(1)}, f32[768,128]{1,0:T(8,128)S(1)}, u32[]{:S(2)}, u32[]{:S(2)}) collective-permute-start(f32[768,128]{1,0:T(8,128)S(1)} %get-tuple-element.32.own), channel_id=1, source_target_pairs={{0,1},{1,0},{2,3},{3,2},{4,5},{5,4},{6,7},{7,6},{8,9},{9,8},{10,11... | collective-permute-start | bytes 1179656 | tf_op jit(solution)/shard_map/ppermute | solution.py:38
  41.3 1.8 %collective-permute-start.9 = (f32[64,128]{1,0:T(8,128)S(1)}, f32[64,128]{1,0:T(8,128)S(1)}, u32[]{:S(2)}, u32[]{:S(2)}) collective-permute-start(f32[64,128]{1,0:T(8,128)S(1)} %get-tuple-element.31), channel_id=1, source_target_pairs={{0,1},{1,0},{2,3},{3,2},{4,5},{5,4},{6,7},{7,6},{8,9},{9,8},{10,11... | collective-permute-start | bytes 98312 | tf_op jit(solution)/shard_map/ppermute | solution.py:38
  43.1 6.1 %collective-permute-start.10 = (f32[64,128]{1,0:T(8,128)S(1)}, f32[64,128]{1,0:T(8,128)S(1)}, u32[]{:S(2)}, u32[]{:S(2)}) collective-permute-start(f32[64,128]{1,0:T(8,128)S(1)} %add.12), channel_id=1, source_target_pairs={{0,16},{4,20},{8,24},{12,28},{16,0},{20,4},{24,8},{28,12},{1,17},{... | collective-permute-start | bytes 98312 | tf_op jit(solution)/shard_map/ppermute | solution.py:38
  49.2 3.9 %collective-permute-start.11 = (f32[64,128]{1,0:T(8,128)S(1)}, f32[64,128]{1,0:T(8,128)S(1)}, u32[]{:S(2)}, u32[]{:S(2)}) collective-permute-start(f32[64,128]{1,0:T(8,128)S(1)} %add.13), channel_id=1, source_target_pairs={{0,8},{4,12},{8,0},{12,4},{16,24},{20,28},{24,16},{28,20},{1,9},{5... | collective-permute-start | bytes 98312 | tf_op jit(solution)/shard_map/ppermute | solution.py:38
  53.1 3.9 %collective-permute-start.12 = (f32[64,128]{1,0:T(8,128)S(1)}, f32[64,128]{1,0:T(8,128)S(1)}, u32[]{:S(2)}, u32[]{:S(2)}) collective-permute-start(f32[64,128]{1,0:T(8,128)S(1)} %add.14), channel_id=1, source_target_pairs={{0,4},{4,0},{8,12},{12,8},{16,20},{20,16},{24,28},{28,24},{1,5},{5... | collective-permute-start | bytes 98312 | tf_op jit(solution)/shard_map/ppermute | solution.py:38
  57.1 1.2 %collective-permute-start.13 = (f32[64,128]{1,0:T(8,128)S(1)}, f32[64,128]{1,0:T(8,128)S(1)}, u32[]{:S(2)}, u32[]{:S(2)}) collective-permute-start(f32[64,128]{1,0:T(8,128)S(1)} %add.15.own), channel_id=1, source_target_pairs={{0,1},{1,0},{2,3},{3,2},{4,5},{5,4},{6,7},{7,6},{8,9},{9,8},{10,11... | collective-permute-start | bytes 98312 | tf_op jit(solution)/shard_map/ppermute | solution.py:38

commit v6 on v5

--- a/solution.py
+++ b/solution.py
@@ -11,8 +11,7 @@
 kernel_gain = 16.0
 LANES = 128
 TILE = 512
-PANEL = 16
-SUB = 8
+PANEL = 8
 VMEM = pl.BlockSpec(memory_space=pltpu.VMEM)
 BF16 = jnp.bfloat16
 F32 = jnp.float32
@@ -48,8 +47,8 @@
     return pl.pallas_call(
         kernel,
         out_shape=out,
-        in_specs=[VMEM] * len(operands),
-        out_specs=jax.tree.map(lambda _: VMEM, out),
+        in_specs=[rest.get("in_specs", VMEM)] * len(operands),
+        out_specs=rest.get("out_specs", jax.tree.map(lambda _: VMEM, out)),
         scratch_shapes=rest.get("scratch", ()),
         input_output_aliases=rest.get("aliases", {}),
         cost_estimate=pl.CostEstimate(
@@ -59,9 +58,18 @@
     )(*operands)
 
 
-def beside_kernel(left, right, out):
-    out[:, : left.shape[1]] = left[...]
-    out[:, left.shape[1] :] = right[...]
+def beside_kernel(left, right, out, sems):
+    width = left.shape[1]
+    copies = [pltpu.make_async_copy(right, out.at[:, width:], sems.at[0])]
+    for start in range(0, left.shape[0], 16):
+        rows = pl.ds(start, 16)
+        copies.append(
+            pltpu.make_async_copy(left.at[rows], out.at[rows, :width], sems.at[len(copies)])
+        )
+    for copy in copies:
+        copy.start()
+    for copy in copies:
+        copy.wait()
 
 
 def meet(unit, blocks, before, total, begin=0):
@@ -173,43 +181,53 @@
 
 def eliminate(work, rows):
     size = work.shape[0]
-    for start in range(0, size, PANEL):
-        lines = [
+
+    def load(start):
+        return [
             jnp.broadcast_to(work[start + i : start + i + 1, :], (8, 2 * size))
             for i in range(PANEL)
         ]
 
+    def twice(value):
+        return jnp.concatenate([value, value], axis=1)
+
+    lines = load(0)
+    for start in range(0, size, PANEL):
+        ahead = load(start + PANEL) if start + PANEL < size else []
+
         def lane(i, k):
             return jnp.broadcast_to(lines[i][:, start + k : start + k + 1], (8, size))
 
-        for sub in range(0, PANEL, SUB):
-            inside = range(sub, sub + SUB)
-            block = {(i, k): lane(i, k) for i in inside for k in range(i, sub + SUB)}
-            for j in inside:
-                scale = lax.rsqrt(block[j, j])
-                lines[j] = lines[j] * jnp.concatenate([scale, scale], axis=1)
-                rows[start + j : start + j + 1, :] = lines[j][:1]
-                times = {
-                    i: block[j, i] * scale if i in inside else lane(j, i)
-                    for i in range(j + 1, PANEL)
-                }
-                for i, factor in times.items():
-                    lines[i] = lines[i] - jnp.concatenate([factor, factor], axis=1) * lines[j]
-                    if i in inside:
-                        for k in range(i, sub + SUB):
-                            block[i, k] = block[i, k] - factor * times[k]
-        after = start + PANEL
-        if after < size:
-            high, mid, low = split3(rows[start:after, :])
+        block = {(i, k): lane(i, k) for i in range(PANEL) for k in range(i, PANEL)}
+        for j in range(PANEL):
+            scale = lax.rsqrt(block[j, j])
+            lines[j] = lines[j] * twice(scale)
+            rows[start + j : start + j + 1, :] = lines[j][:1]
+            times = {i: block[j, i] * scale for i in range(j + 1, PANEL)}
+            for i, factor in times.items():
+                lines[i] = lines[i] - twice(factor) * lines[j]
+                for k in range(i, PANEL):
+                    block[i, k] = block[i, k] - factor * times[k]
+            for i in range(len(ahead)):
+                ahead[i] = ahead[i] - twice(lane(j, PANEL + i)) * lines[j]
+        behind = start + 2 * PANEL
+        if behind < size:
+            high, mid, low = [
+                part.astype(F32) for part in split3(rows[start : start + PANEL, :])
+            ]
             left = jnp.concatenate([high, high, mid, high, low, mid], axis=0)[:, :size]
             right = jnp.concatenate([high, mid, high, low, high, mid], axis=0)
             update = lax.dot_general(
-                left, right, (((0,), (0,)), ((), ())), preferred_element_type=F32
+                left.astype(BF16),
+                right.astype(BF16),
+                (((0,), (0,)), ((), ())),
+                preferred_element_type=F32,
             )
-            work[after:, :] = work[after:, :] - update[after:, :]
-
-
-def finish_kernel(points, own, theirs, parts, out, work, rows):
+            work[behind:, :] = work[behind:, :] - update[behind:, :]
+        lines = ahead
+
+
+def finish_kernel(points, own, theirs, parts, out, work, rows, result, sems):
     some, size = own.shape
     begin = lax.rem(lax.axis_index("lmk"), 2) * some
     work[pl.ds(pl.multiple_of(begin, some), some), :size] = own[...] / points
@@ -217,12 +235,19 @@
     work[:, size:] = jnp.where(eye(size), 1.0, 0.0)
     eliminate(work, rows)
     high, low, _ = split3(rows[:, size:])
-    out[...] = lax.dot_general(
-        parts[...],
-        jnp.concatenate([high, low, high], axis=1),
-        (((1,), (1,)), ((), ())),
-        preferred_element_type=F32,
-    )
+    right = jnp.concatenate([high, low, high], axis=1)
+    copies = []
+    for start in range(0, parts.shape[0], TILE):
+        lines = pl.ds(start, min(TILE, parts.shape[0] - start))
+        result[lines, :] = lax.dot_general(
+            parts[lines, :], right, (((1,), (1,)), ((), ())), preferred_element_type=F32
+        )
+        copies.append(
+            pltpu.make_async_copy(result.at[lines], out.at[lines], sems.at[len(copies)])
+        )
+        copies[-1].start()
+    for copy in copies:
+        copy.wait()
 
 
 def per_device(points, landmarks, eigvecs):
@@ -240,6 +265,8 @@
             beside_kernel,
             shape((landmarks.shape[0], features + size), BF16),
             (landmarks, eigvecs),
+            scratch=[pltpu.SemaphoreType.DMA((1 + landmarks.shape[0] // 16,))],
+            in_specs=pl.BlockSpec(memory_space=pltpu.HBM),
         )
     }
     if num_pts == 8:
@@ -312,13 +339,17 @@
         shape((num_rows, 3 * size), BF16),
         (embed, swap(embed, "lmk", num_lmk, 1)),
     )
-    for bit in pts_bits:
-        part = part + swap(part, "pts", num_pts, bit)
+    part = lax.psum(part, "pts")
     return call_on(
         functools.partial(finish_kernel, float(num_rows * num_pts)),
         shape((num_rows, size), F32),
         (part, swap(part, "lmk", num_lmk, 1), parts),
-        scratch=[pltpu.VMEM((size, 2 * size), F32)] * 2,
+        scratch=[
+            *[pltpu.VMEM((size, 2 * size), F32)] * 2,
+            pltpu.VMEM((num_rows, size), F32),
+            pltpu.SemaphoreType.DMA((-(-num_rows // TILE),)),
+        ],
+        out_specs=pl.BlockSpec(memory_space=pltpu.HBM),
     )
 
 

time: 64.3 us -> 87.7 us (1.36)
  blocking collectives: 0 us -> 37.8 us
  waiting for transfers between devices: 26.1 us -> 17.7 us
  starting transfers between devices: 20 us -> 14.5 us
    psum x0 -> x1, blocking collectives: none -> 37.8 us  [per_device(): part = lax.psum(part, 'pts')]
    ppermute x15 -> x12, waiting for transfers between devices: 26.1 us -> 17.7 us  [swap(): return lax.ppermute(value, axis, [(i, i ^ bit) for i in range(size)])]
    ppermute x15 -> x12, starting transfers between devices: 20 us -> 14.5 us  [swap(): return lax.ppermute(value, axis, [(i, i ^ bit) for i in range(size)])]
  transfers between devices with their start and end apart: 15 -> 12, of which waited for: 13 -> 10; matrix products, arithmetic and copies ran while one was open for 0% -> 0% of each run, Pallas kernels for 13% -> 10%
where the time goes in v6:
time: 87.7 us; the launch traced here: 87.5 us
  blocking collectives  37.8 us (43%)
  waiting for transfers between devices  17.7 us (20%)
  Pallas kernels  15.7 us (18%)
  starting transfers between devices  14.5 us (17%)
  local copies, waits for them, and re-layouts  1.68 us (2%)
    psum x1, blocking collectives, per_device(): part = lax.psum(part, 'pts')  37.8 us
    ppermute x12, waiting for transfers between devices, swap(): return lax.ppermute(value, axis, [(i, i ^ bit) for i in range(size)])  17.7 us
    pallas_call x10, Pallas kernels, call_on(): pl.pallas_call(kernel, out_shape=out, in_specs=[rest.get('in_specs', VMEM...  15.7 us
    ppermute x12, starting transfers between devices, swap(): return lax.ppermute(value, axis, [(i, i ^ bit) for i in range(size)])  14.5 us
  transfers between devices with their start and end apart: 12, of which 10 were waited for; matrix products, arithmetic and copies ran while one was open for 0% of the time, Pallas kernels for 10%

profile of v6, /device:TPU:0, one launch (start us, length us, event | category | flops | bytes accessed | tf_op | source)
XLA Modules:
  0.0 87.5 jit_solution(15004993258037295961)
XLA Ops:
  0.0 0.0 copy-start
  0.0 0.9 %copy-done = bf16[128,768]{1,0:T(8,128)(2,1)S(1)} copy-done((bf16[128,768]{1,0:T(8,128)(2,1)S(1)}, bf16[128,768]{1,0:T(8,128)(2,1)}, u32[]{:S(2)}) %copy-start) | copy-done | bytes 196632
  0.9 0.0 copy-start.1
  0.9 0.8 copy-done.1
  1.7 0.2 shard_map.37.block
  1.9 4.1 %collective-permute-start.2 = (bf16[128,896]{1,0:T(8,128)(2,1)S(1)}, bf16[128,896]{1,0:T(8,128)(2,1)S(1)}, u32[]{:S(2)}, u32[]{:S(2)}) collective-permute-start(bf16[128,896]{1,0:T(8,128)(2,1)S(1)} %shard_map.37.block), channel_id=1, source_target_pairs={{0,16},{4,20},{8,24},{12,28},{16,0},{20,4},{24,8},{28,12},{1,17},{... | collective-permute-start | bytes 688136 | tf_op jit(solution)/shard_map/ppermute | solution.py:37
  6.0 1.6 %collective-permute-start.1 = (bf16[128,896]{1,0:T(8,128)(2,1)S(1)}, bf16[128,896]{1,0:T(8,128)(2,1)S(1)}, u32[]{:S(2)}, u32[]{:S(2)}) collective-permute-start(bf16[128,896]{1,0:T(8,128)(2,1)S(1)} %shard_map.37.block), channel_id=1, source_target_pairs={{0,8},{4,12},{8,0},{12,4},{16,24},{20,28},{24,16},{28,20},{1,9},{5... | collective-permute-start | bytes 688136 | tf_op jit(solution)/shard_map/ppermute | solution.py:37
  7.6 1.5 %collective-permute-start = (bf16[128,896]{1,0:T(8,128)(2,1)S(1)}, bf16[128,896]{1,0:T(8,128)(2,1)S(1)}, u32[]{:S(2)}, u32[]{:S(2)}) collective-permute-start(bf16[128,896]{1,0:T(8,128)(2,1)S(1)} %shard_map.37.block), channel_id=1, source_target_pairs={{0,4},{4,0},{8,12},{12,8},{16,20},{20,16},{24,28},{28,24},{1,5},{5... | collective-permute-start | bytes 688136 | tf_op jit(solution)/shard_map/ppermute | solution.py:37
  9.1 3.1 %shard_map.38 = (bf16[1536,768]{1,0:T(8,128)(2,1)S(1)}, f32[1536,256]{1,0:T(8,128)S(1)}) custom-call(bf16[1536,768]{1,0:T(8,128)(2,1)} %points.1, bf16[128,896]{1,0:T(8,128)(2,1)S(1)} %shard_map.37.block), custom_call_target="tpu_custom_call" | custom-call | flops 1610612736 | bytes 1048576 | tf_op jit(solution)/shard_map/pallas_call | solution.py:47
  12.2 4.5 %collective-permute-done.2.refs_0_ = bf16[128,896]{1,0:T(8,128)(2,1)S(1)} collective-permute-done((bf16[128,896]{1,0:T(8,128)(2,1)S(1)}, bf16[128,896]{1,0:T(8,128)(2,1)S(1)}, u32[]{:S(2)}, u32[]{:S(2)}) %collective-permute-start.2) | collective-permute-done | bytes 229408 | tf_op jit(solution)/shard_map/ppermute | solution.py:37
  16.6 0.2 collective-permute-done.1.refs_1_
  16.8 0.0 collective-permute-done.refs_2_
  16.8 1.5 %collective-permute-start.4 = (bf16[128,896]{1,0:T(8,128)(2,1)S(1)}, bf16[128,896]{1,0:T(8,128)(2,1)S(1)}, u32[]{:S(2)}, u32[]{:S(2)}) collective-permute-start(bf16[128,896]{1,0:T(8,128)(2,1)S(1)} %collective-permute-done.2.refs_0_), channel_id=1, source_target_pairs={{0,8},{4,12},{8,0},{12,4},{16,24},{20,28},{24,16},{28,20},{1,9},{5... | collective-permute-start | bytes 688136 | tf_op jit(solution)/shard_map/ppermute | solution.py:37
  18.3 1.5 %collective-permute-start.3 = (bf16[128,896]{1,0:T(8,128)(2,1)S(1)}, bf16[128,896]{1,0:T(8,128)(2,1)S(1)}, u32[]{:S(2)}, u32[]{:S(2)}) collective-permute-start(bf16[128,896]{1,0:T(8,128)(2,1)S(1)} %collective-permute-done.2.refs_0_), channel_id=1, source_target_pairs={{0,4},{4,0},{8,12},{12,8},{16,20},{20,16},{24,28},{28,24},{1,5},{5... | collective-permute-start | bytes 688136 | tf_op jit(solution)/shard_map/ppermute | solution.py:37
  19.8 2.3 %shard_map.39.refs_2_ = f32[1536,256]{1,0:T(8,128)S(1)} custom-call(bf16[1536,768]{1,0:T(8,128)(2,1)S(1)} %get-tuple-element.19.unit, bf16[128,896]{1,0:T(8,128)(2,1)S(1)} %collective-permute-done.2.refs_0_, bf16[128,896]{1,0:T(8,128)(2,1)S(1)} %collective-permute-done.1.refs_1_, ...), custom_call_target="tpu_custom_call", output_to_operand_aliasing={{}: (4, {})} | custom-call | flops 4831838208 | bytes 1048576 | tf_op jit(solution)/shard_map/pallas_call | solution.py:47
  22.1 0.7 collective-permute-start.6
  22.8 0.7 collective-permute-done.4.refs_0_
  23.5 1.0 %collective-permute-done.3.refs_1_ = bf16[128,896]{1,0:T(8,128)(2,1)S(1)} collective-permute-done((bf16[128,896]{1,0:T(8,128)(2,1)S(1)}, bf16[128,896]{1,0:T(8,128)(2,1)S(1)}, u32[]{:S(2)}, u32[]{:S(2)}) %collective-permute-start.3) | collective-permute-done | bytes 229408 | tf_op jit(solution)/shard_map/ppermute | solution.py:37
  24.5 1.5 %collective-permute-start.5 = (bf16[128,896]{1,0:T(8,128)(2,1)S(1)}, bf16[128,896]{1,0:T(8,128)(2,1)S(1)}, u32[]{:S(2)}, u32[]{:S(2)}) collective-permute-start(bf16[128,896]{1,0:T(8,128)(2,1)S(1)} %collective-permute-done.4.refs_0_), channel_id=1, source_target_pairs={{0,4},{4,0},{8,12},{12,8},{16,20},{20,16},{24,28},{28,24},{1,5},{5... | collective-permute-start | bytes 688136 | tf_op jit(solution)/shard_map/ppermute | solution.py:37
  26.0 1.7 %shard_map.40.refs_2_ = f32[1536,256]{1,0:T(8,128)S(1)} custom-call(bf16[1536,768]{1,0:T(8,128)(2,1)S(1)} %get-tuple-element.19.unit, bf16[128,896]{1,0:T(8,128)(2,1)S(1)} %collective-permute-done.4.refs_0_, bf16[128,896]{1,0:T(8,128)(2,1)S(1)} %collective-permute-done.3.refs_1_, f32[1536,256]{1,0:T(8,128)S(1)} %shard_map.39.refs_2_), custom_call_target="tpu_custom_call", output_to_operand_aliasing={{}: (3, {})} | custom-call | flops 3221225472 | bytes 1048576 | tf_op jit(solution)/shard_map/pallas_call | solution.py:47
  27.7 0.6 collective-permute-done.6.refs_1_
  28.3 2.2 %collective-permute-done.5.refs_0_ = bf16[128,896]{1,0:T(8,128)(2,1)S(1)} collective-permute-done((bf16[128,896]{1,0:T(8,128)(2,1)S(1)}, bf16[128,896]{1,0:T(8,128)(2,1)S(1)}, u32[]{:S(2)}, u32[]{:S(2)}) %collective-permute-start.5) | collective-permute-done | bytes 229408 | tf_op jit(solution)/shard_map/ppermute | solution.py:37
  30.5 1.2 %shard_map.42 = f32[776,128]{1,0:T(8,128)S(1)} custom-call(bf16[1536,768]{1,0:T(8,128)(2,1)S(1)} %get-tuple-element.19.unit, bf16[128,896]{1,0:T(8,128)(2,1)S(1)} %collective-permute-done.5.refs_0_, bf16[128,896]{1,0:T(8,128)(2,1)S(1)} %collective-permute-done.6.refs_1_, f32[1536,256]{1,0:T(8,128)S(1)} %shard_map.40.refs_2_), custom_call_target="tpu_custom_call" | custom-call | flops 1610612736 | bytes 1048576 | tf_op jit(solution)/shard_map/pallas_call | solution.py:47
  31.7 0.1 collective-permute-start.7
  31.8 1.2 %shard_map.41.mine = f32[776,128]{1,0:T(8,128)S(1)} custom-call(bf16[1536,768]{1,0:T(8,128)(2,1)S(1)} %get-tuple-element.19.unit, bf16[128,896]{1,0:T(8,128)(2,1)S(1)} %collective-permute-done.5.refs_0_, bf16[128,896]{1,0:T(8,128)(2,1)S(1)} %collective-permute-done.6.refs_1_, f32[1536,256]{1,0:T(8,128)S(1)} %shard_map.40.refs_2_), custom_call_target="tpu_custom_call" | custom-call | flops 1610612736 | bytes 1048576 | tf_op jit(solution)/shard_map/pallas_call | solution.py:47
  32.9 0.6 collective-permute-done.7.other
  33.5 0.1 shard_map.43.mine
  33.6 1.6 %collective-permute-start.8 = (bf16[800,128]{1,0:T(8,128)(2,1)S(1)}, bf16[800,128]{1,0:T(8,128)(2,1)S(1)}, u32[]{:S(2)}, u32[]{:S(2)}) collective-permute-start(bf16[800,128]{1,0:T(8,128)(2,1)S(1)} %shard_map.43.mine), channel_id=1, source_target_pairs={{0,2},{1,3},{2,0},{3,1},{4,6},{5,7},{6,4},{7,5},{8,10},{9,11},{10,... | collective-permute-start | bytes 614408 | tf_op jit(solution)/shard_map/ppermute | solution.py:37
  35.2 5.6 %collective-permute-done.8.other = bf16[800,128]{1,0:T(8,128)(2,1)S(1)} collective-permute-done((bf16[800,128]{1,0:T(8,128)(2,1)S(1)}, bf16[800,128]{1,0:T(8,128)(2,1)S(1)}, u32[]{:S(2)}, u32[]{:S(2)}) %collective-permute-start.8) | collective-permute-done | bytes 204832 | tf_op jit(solution)/shard_map/ppermute | solution.py:37
  40.8 0.7 shard_map.44
  41.5 0.1 collective-permute-start.11
  41.5 0.5 collective-permute-start.9
  42.0 1.3 %collective-permute-done.9 = f32[64,128]{1,0:T(8,128)S(1)} collective-permute-done((f32[64,128]{1,0:T(8,128)S(1)}, f32[64,128]{1,0:T(8,128)S(1)}, u32[]{:S(2)}, u32[]{:S(2)}) %collective-permute-start.9) | collective-permute-done | bytes 32800 | tf_op jit(solution)/shard_map/ppermute | solution.py:37
  43.3 37.8 %psum.7.own = f32[64,128]{1,0:T(8,128)S(1)} all-reduce(f32[64,128]{1,0:T(8,128)S(1)} %add.5), channel_id=1, replica_groups=mesh['pts'=8,'lmk'=4] {'pts'}, use_global_device_ids=true, to_apply=%region_0.0 | all-reduce | flops 8192 | bytes 65536 | tf_op jit(solution)/shard_map/psum | solution.py:342
  81.1 0.0 collective-permute-start.10
  81.1 0.0 collective-permute-done.11.theirs
  81.1 0.1 shard_map.45.parts
  81.3 1.1 %collective-permute-done.10.theirs = f32[64,128]{1,0:T(8,128)S(1)} collective-permute-done((f32[64,128]{1,0:T(8,128)S(1)}, f32[64,128]{1,0:T(8,128)S(1)}, u32[]{:S(2)}, u32[]{:S(2)}) %collective-permute-start.10) | collective-permute-done | bytes 32800 | tf_op jit(solution)/shard_map/ppermute | solution.py:37
  82.3 5.2 %shard_map.46 = f32[1536,128]{1,0:T(8,128)} custom-call(f32[64,128]{1,0:T(8,128)S(1)} %psum.7.own, f32[64,128]{1,0:T(8,128)S(1)} %collective-permute-done.10.theirs, bf16[1536,384]{1,0:T(8,128)(2,1)S(1)} %shard_map.45.parts), custom_call_target="tpu_custom_call" | custom-call | bytes 1048576 | tf_op jit(solution)/shard_map/pallas_call | solution.py:47
  (1 shorter events, 0.0 us)
Async XLA Ops:
  0.0 0.9 %copy-start = (bf16[128,768]{1,0:T(8,128)(2,1)S(1)}, bf16[128,768]{1,0:T(8,128)(2,1)}, u32[]{:S(2)}) copy-start(bf16[128,768]{1,0:T(8,128)(2,1)} %left.1) | copy-start | bytes 589828
  0.9 0.8 copy-start.1
  1.9 14.7 %collective-permute-start.2 = (bf16[128,896]{1,0:T(8,128)(2,1)S(1)}, bf16[128,896]{1,0:T(8,128)(2,1)S(1)}, u32[]{:S(2)}, u32[]{:S(2)}) collective-permute-start(bf16[128,896]{1,0:T(8,128)(2,1)S(1)} %shard_map.37.block), channel_id=1, source_target_pairs={{0,16},{4,20},{8,24},{12,28},{16,0},{20,4},{24,8},{28,12},{1,17},{... | collective-permute-start | bytes 688136 | tf_op jit(solution)/shard_map/ppermute | solution.py:37
  6.0 10.8 %collective-permute-start.1 = (bf16[128,896]{1,0:T(8,128)(2,1)S(1)}, bf16[128,896]{1,0:T(8,128)(2,1)S(1)}, u32[]{:S(2)}, u32[]{:S(2)}) collective-permute-start(bf16[128,896]{1,0:T(8,128)(2,1)S(1)} %shard_map.37.block), channel_id=1, source_target_pairs={{0,8},{4,12},{8,0},{12,4},{16,24},{20,28},{24,16},{28,20},{1,9},{5... | collective-permute-start | bytes 688136 | tf_op jit(solution)/shard_map/ppermute | solution.py:37
  7.6 9.2 %collective-permute-start = (bf16[128,896]{1,0:T(8,128)(2,1)S(1)}, bf16[128,896]{1,0:T(8,128)(2,1)S(1)}, u32[]{:S(2)}, u32[]{:S(2)}) collective-permute-start(bf16[128,896]{1,0:T(8,128)(2,1)S(1)} %shard_map.37.block), channel_id=1, source_target_pairs={{0,4},{4,0},{8,12},{12,8},{16,20},{20,16},{24,28},{28,24},{1,5},{5... | collective-permute-start | bytes 688136 | tf_op jit(solution)/shard_map/ppermute | solution.py:37
  16.8 6.7 %collective-permute-start.4 = (bf16[128,896]{1,0:T(8,128)(2,1)S(1)}, bf16[128,896]{1,0:T(8,128)(2,1)S(1)}, u32[]{:S(2)}, u32[]{:S(2)}) collective-permute-start(bf16[128,896]{1,0:T(8,128)(2,1)S(1)} %collective-permute-done.2.refs_0_), channel_id=1, source_target_pairs={{0,8},{4,12},{8,0},{12,4},{16,24},{20,28},{24,16},{28,20},{1,9},{5... | collective-permute-start | bytes 688136 | tf_op jit(solution)/shard_map/ppermute | solution.py:37
  18.3 6.2 %collective-permute-start.3 = (bf16[128,896]{1,0:T(8,128)(2,1)S(1)}, bf16[128,896]{1,0:T(8,128)(2,1)S(1)}, u32[]{:S(2)}, u32[]{:S(2)}) collective-permute-start(bf16[128,896]{1,0:T(8,128)(2,1)S(1)} %collective-permute-done.2.refs_0_), channel_id=1, source_target_pairs={{0,4},{4,0},{8,12},{12,8},{16,20},{20,16},{24,28},{28,24},{1,5},{5... | collective-permute-start | bytes 688136 | tf_op jit(solution)/shard_map/ppermute | solution.py:37
  22.1 6.2 %collective-permute-start.6 = (bf16[128,896]{1,0:T(8,128)(2,1)S(1)}, bf16[128,896]{1,0:T(8,128)(2,1)S(1)}, u32[]{:S(2)}, u32[]{:S(2)}) collective-permute-start(bf16[128,896]{1,0:T(8,128)(2,1)S(1)} %collective-permute-done.refs_2_), channel_id=1, source_target_pairs={{0,8},{4,12},{8,0},{12,4},{16,24},{20,28},{24,16},{28,20},{1,9},{5... | collective-permute-start | bytes 688136 | tf_op jit(solution)/shard_map/ppermute | solution.py:37
  24.5 6.0 %collective-permute-start.5 = (bf16[128,896]{1,0:T(8,128)(2,1)S(1)}, bf16[128,896]{1,0:T(8,128)(2,1)S(1)}, u32[]{:S(2)}, u32[]{:S(2)}) collective-permute-start(bf16[128,896]{1,0:T(8,128)(2,1)S(1)} %collective-permute-done.4.refs_0_), channel_id=1, source_target_pairs={{0,4},{4,0},{8,12},{12,8},{16,20},{20,16},{24,28},{28,24},{1,5},{5... | collective-permute-start | bytes 688136 | tf_op jit(solution)/shard_map/ppermute | solution.py:37
  31.7 1.8 %collective-permute-start.7 = (f32[776,128]{1,0:T(8,128)S(1)}, f32[776,128]{1,0:T(8,128)S(1)}, u32[]{:S(2)}, u32[]{:S(2)}) collective-permute-start(f32[776,128]{1,0:T(8,128)S(1)} %shard_map.42), channel_id=1, source_target_pairs={{0,1},{1,0},{2,3},{3,2},{4,5},{5,4},{6,7},{7,6},{8,9},{9,8},{10,11... | collective-permute-start | bytes 1191944 | tf_op jit(solution)/shard_map/ppermute | solution.py:37
  33.6 7.2 %collective-permute-start.8 = (bf16[800,128]{1,0:T(8,128)(2,1)S(1)}, bf16[800,128]{1,0:T(8,128)(2,1)S(1)}, u32[]{:S(2)}, u32[]{:S(2)}) collective-permute-start(bf16[800,128]{1,0:T(8,128)(2,1)S(1)} %shard_map.43.mine), channel_id=1, source_target_pairs={{0,2},{1,3},{2,0},{3,1},{4,6},{5,7},{6,4},{7,5},{8,10},{9,11},{10,... | collective-permute-start | bytes 614408 | tf_op jit(solution)/shard_map/ppermute | solution.py:37
  41.5 39.6 %collective-permute-start.11 = (f32[768,128]{1,0:T(8,128)S(1)}, f32[768,128]{1,0:T(8,128)S(1)}, u32[]{:S(2)}, u32[]{:S(2)}) collective-permute-start(f32[768,128]{1,0:T(8,128)S(1)} %get-tuple-element.32.own), channel_id=1, source_target_pairs={{0,1},{1,0},{2,3},{3,2},{4,5},{5,4},{6,7},{7,6},{8,9},{9,8},{10,11... | collective-permute-start | bytes 1179656 | tf_op jit(solution)/shard_map/ppermute | solution.py:37
  41.5 1.8 %collective-permute-start.9 = (f32[64,128]{1,0:T(8,128)S(1)}, f32[64,128]{1,0:T(8,128)S(1)}, u32[]{:S(2)}, u32[]{:S(2)}) collective-permute-start(f32[64,128]{1,0:T(8,128)S(1)} %get-tuple-element.31), channel_id=1, source_target_pairs={{0,1},{1,0},{2,3},{3,2},{4,5},{5,4},{6,7},{7,6},{8,9},{9,8},{10,11... | collective-permute-start | bytes 98312 | tf_op jit(solution)/shard_map/ppermute | solution.py:37
  81.1 1.2 %collective-permute-start.10 = (f32[64,128]{1,0:T(8,128)S(1)}, f32[64,128]{1,0:T(8,128)S(1)}, u32[]{:S(2)}, u32[]{:S(2)}) collective-permute-start(f32[64,128]{1,0:T(8,128)S(1)} %psum.7.own), channel_id=1, source_target_pairs={{0,1},{1,0},{2,3},{3,2},{4,5},{5,4},{6,7},{7,6},{8,9},{9,8},{10,11... | collective-permute-start | bytes 98312 | tf_op jit(solution)/shard_map/ppermute | solution.py:37

commit v7 on v6

--- a/solution.py
+++ b/solution.py
@@ -261,13 +261,13 @@
     shape = jax.ShapeDtypeStruct
 
     held = {
-        0: call_on(
+        0: pl.pallas_call(
             beside_kernel,
-            shape((landmarks.shape[0], features + size), BF16),
-            (landmarks, eigvecs),
-            scratch=[pltpu.SemaphoreType.DMA((1 + landmarks.shape[0] // 16,))],
-            in_specs=pl.BlockSpec(memory_space=pltpu.HBM),
-        )
+            out_shape=shape((landmarks.shape[0], features + size), BF16),
+            in_specs=[pl.BlockSpec(memory_space=pltpu.HBM)] * 2,
+            out_specs=VMEM,
+            scratch_shapes=[pltpu.SemaphoreType.DMA((1 + landmarks.shape[0] // 16,))],
+        )(landmarks, eigvecs)
     }
     if num_pts == 8:
         rounds = [[(0, 4), (0, 2), (0, 1)], [(4, 2), (4, 1)], [(6, 1)]]
@@ -279,6 +279,16 @@
             order = order + [mask ^ bit for mask in order]
 
     flops = 8 * num_rows * landmarks.shape[0] * (features + 2 * size)
+
+    def more(total, masks):
+        return call_on(
+            functools.partial(next_kernel, len(masks)),
+            shape((num_rows, 2 * size), F32),
+            (unit, *[held[mask] for mask in masks], total),
+            aliases={len(masks) + 1: 0},
+            flops=flops * len(masks),
+        )
+
     ready, unit, total = [0], None, None
     for turn, hops in enumerate(rounds):
         for mask, bit in hops:
@@ -291,23 +301,20 @@
                 flops=flops,
             )
         else:
-            total = call_on(
-                functools.partial(next_kernel, len(ready)),
-                shape((num_rows, 2 * size), F32),
-                (unit, *[held[mask] for mask in ready], total),
-                aliases={len(ready) + 1: 0},
-                flops=flops * len(ready),
-            )
+            total = more(total, ready)
         ready = [mask ^ bit for mask, bit in hops]
         if turn == 1 and late:
             mask, bit = late
             held[mask], total = lax.optimization_barrier((held[mask], total))
             held[mask ^ bit] = swap(held[mask], "pts", num_pts, bit)
         if turn + 1 < len(rounds):
-            tied = list(dict.fromkeys(ready + [mask for mask, _ in rounds[turn + 1]]))[::-1]
+            sources = [mask for mask, _ in rounds[turn + 1]]
+            tied = list(dict.fromkeys(ready + sources))[::-1]
             *fresh, total = lax.optimization_barrier((*[held[mask] for mask in tied], total))
             held.update(zip(tied, fresh))
-    group = ready + ([late[0] ^ late[1]] if late else [])
+    if late:
+        total = more(total, [late[0] ^ late[1]])
+    group = ready
     extra = -(-(half // LANES) // 8) * 8
     send, keep = [
         call_on(
@@ -339,7 +346,12 @@
         shape((num_rows, 3 * size), BF16),
         (embed, swap(embed, "lmk", num_lmk, 1)),
     )
-    part = lax.psum(part, "pts")
+    if num_pts == 8:
+        pair = part + swap(part, "pts", num_pts, 1)
+        part = pair + (swap(part, "pts", num_pts, 2) + swap(part, "pts", num_pts, 3))
+        pts_bits = [4]
+    for bit in pts_bits:
+        part = part + swap(part, "pts", num_pts, bit)
     return call_on(
         functools.partial(finish_kernel, float(num_rows * num_pts)),
         shape((num_rows, size), F32),

time: 87.7 us -> 62.1 us (0.71)
  blocking collectives: 37.8 us -> 0 us
  starting transfers between devices: 14.5 us -> 21.8 us
  waiting for transfers between devices: 17.7 us -> 21.2 us
  Pallas kernels: 15.7 us -> 17.7 us
    psum x1 -> x0, blocking collectives: 37.8 us -> none  [per_device(): part = lax.psum(part, 'pts')]
    ppermute x12 -> x16, starting transfers between devices: 14.5 us -> 21.8 us  [swap(): return lax.ppermute(value, axis, [(i, i ^ bit) for i in range(size)])]
    ppermute x12 -> x16, waiting for transfers between devices: 17.7 us -> 21.2 us  [swap(): return lax.ppermute(value, axis, [(i, i ^ bit) for i in range(size)])]
    pallas_call x0 -> x1, Pallas kernels: none -> 1.64 us  [per_device(): pl.pallas_call(beside_kernel, out_shape=shape((landmarks.shape[0], featur...]
  transfers between devices with their start and end apart: 12 -> 16, of which waited for: 10 -> 13; matrix products, arithmetic and copies ran while one was open for 0% -> 0% of each run, Pallas kernels for 10% -> 15%
where the time goes in v7:
time: 62.1 us; the launch traced here: 61.9 us
  starting transfers between devices  21.8 us (35%)
  waiting for transfers between devices  21.2 us (34%)
  Pallas kernels  17.7 us (29%)
  local copies, waits for them, and re-layouts  0.97 us (2%)
    ppermute x16, starting transfers between devices, swap(): return lax.ppermute(value, axis, [(i, i ^ bit) for i in range(size)])  21.8 us
    ppermute x16, waiting for transfers between devices, swap(): return lax.ppermute(value, axis, [(i, i ^ bit) for i in range(size)])  21.2 us
    pallas_call x10, Pallas kernels, call_on(): pl.pallas_call(kernel, out_shape=out, in_specs=[rest.get('in_specs', VMEM...  16.1 us
    pallas_call x1, Pallas kernels, per_device(): pl.pallas_call(beside_kernel, out_shape=shape((landmarks.shape[0], featur...  1.64 us
  transfers between devices with their start and end apart: 16, of which 13 were waited for; matrix products, arithmetic and copies ran while one was open for 0% of the time, Pallas kernels for 15%

profile of v7, /device:TPU:0, one launch (start us, length us, event | category | flops | bytes accessed | tf_op | source)
XLA Modules:
  0.0 61.9 jit_solution(3990913808187812909)
XLA Ops:
  0.0 1.6 %shard_map.37.block = bf16[128,896]{1,0:T(8,128)(2,1)} custom-call(bf16[128,768]{1,0:T(8,128)(2,1)} %left.1, bf16[128,128]{1,0:T(8,128)(2,1)} %right.1), custom_call_target="tpu_custom_call" | custom-call | tf_op jit(solution)/shard_map/pallas_call | solution.py:264
  1.7 4.1 %collective-permute-start.2 = (bf16[128,896]{1,0:T(8,128)(2,1)}, bf16[128,896]{1,0:T(8,128)(2,1)S(1)}, u32[]{:S(2)}, u32[]{:S(2)}) collective-permute-start(bf16[128,896]{1,0:T(8,128)(2,1)} %shard_map.37.block), channel_id=1, source_target_pairs={{0,16},{4,20},{8,24},{12,28},{16,0},{20,4},{24,8},{28,12},{1,17},{... | collective-permute-start | bytes 688136 | tf_op jit(solution)/shard_map/ppermute | solution.py:37
  5.8 1.6 %collective-permute-start.1 = (bf16[128,896]{1,0:T(8,128)(2,1)}, bf16[128,896]{1,0:T(8,128)(2,1)S(1)}, u32[]{:S(2)}, u32[]{:S(2)}) collective-permute-start(bf16[128,896]{1,0:T(8,128)(2,1)} %shard_map.37.block), channel_id=1, source_target_pairs={{0,8},{4,12},{8,0},{12,4},{16,24},{20,28},{24,16},{28,20},{1,9},{5... | collective-permute-start | bytes 688136 | tf_op jit(solution)/shard_map/ppermute | solution.py:37
  7.3 1.5 %collective-permute-start = (bf16[128,896]{1,0:T(8,128)(2,1)}, bf16[128,896]{1,0:T(8,128)(2,1)S(1)}, u32[]{:S(2)}, u32[]{:S(2)}) collective-permute-start(bf16[128,896]{1,0:T(8,128)(2,1)} %shard_map.37.block), channel_id=1, source_target_pairs={{0,4},{4,0},{8,12},{12,8},{16,20},{20,16},{24,28},{28,24},{1,5},{5... | collective-permute-start | bytes 688136 | tf_op jit(solution)/shard_map/ppermute | solution.py:37
  8.8 0.0 copy-start
  8.8 1.0 %copy-done = bf16[128,896]{1,0:T(8,128)(2,1)S(1)} copy-done((bf16[128,896]{1,0:T(8,128)(2,1)S(1)}, bf16[128,896]{1,0:T(8,128)(2,1)}, u32[]{:S(2)}) %copy-start) | copy-done | bytes 229400
  9.8 3.1 %shard_map.38 = (bf16[1536,768]{1,0:T(8,128)(2,1)S(1)}, f32[1536,256]{1,0:T(8,128)S(1)}) custom-call(bf16[1536,768]{1,0:T(8,128)(2,1)} %points.1, bf16[128,896]{1,0:T(8,128)(2,1)S(1)} %copy-done), custom_call_target="tpu_custom_call" | custom-call | flops 1610612736 | bytes 1048576 | tf_op jit(solution)/shard_map/pallas_call | solution.py:47
  12.9 3.7 %collective-permute-done.2.refs_0_ = bf16[128,896]{1,0:T(8,128)(2,1)S(1)} collective-permute-done((bf16[128,896]{1,0:T(8,128)(2,1)}, bf16[128,896]{1,0:T(8,128)(2,1)S(1)}, u32[]{:S(2)}, u32[]{:S(2)}) %collective-permute-start.2) | collective-permute-done | bytes 229408 | tf_op jit(solution)/shard_map/ppermute | solution.py:37
  16.6 0.2 collective-permute-done.1.refs_1_
  16.8 0.0 collective-permute-done.refs_2_
  16.8 1.5 %collective-permute-start.4 = (bf16[128,896]{1,0:T(8,128)(2,1)S(1)}, bf16[128,896]{1,0:T(8,128)(2,1)S(1)}, u32[]{:S(2)}, u32[]{:S(2)}) collective-permute-start(bf16[128,896]{1,0:T(8,128)(2,1)S(1)} %collective-permute-done.2.refs_0_), channel_id=1, source_target_pairs={{0,8},{4,12},{8,0},{12,4},{16,24},{20,28},{24,16},{28,20},{1,9},{5... | collective-permute-start | bytes 688136 | tf_op jit(solution)/shard_map/ppermute | solution.py:37
  18.3 1.5 %collective-permute-start.3 = (bf16[128,896]{1,0:T(8,128)(2,1)S(1)}, bf16[128,896]{1,0:T(8,128)(2,1)S(1)}, u32[]{:S(2)}, u32[]{:S(2)}) collective-permute-start(bf16[128,896]{1,0:T(8,128)(2,1)S(1)} %collective-permute-done.2.refs_0_), channel_id=1, source_target_pairs={{0,4},{4,0},{8,12},{12,8},{16,20},{20,16},{24,28},{28,24},{1,5},{5... | collective-permute-start | bytes 688136 | tf_op jit(solution)/shard_map/ppermute | solution.py:37
  19.8 2.3 %shard_map.39.refs_2_ = f32[1536,256]{1,0:T(8,128)S(1)} custom-call(bf16[1536,768]{1,0:T(8,128)(2,1)S(1)} %get-tuple-element.19.unit, bf16[128,896]{1,0:T(8,128)(2,1)S(1)} %collective-permute-done.2.refs_0_, bf16[128,896]{1,0:T(8,128)(2,1)S(1)} %collective-permute-done.1.refs_1_, ...), custom_call_target="tpu_custom_call", output_to_operand_aliasing={{}: (4, {})} | custom-call | flops 4831838208 | bytes 1048576 | tf_op jit(solution)/shard_map/pallas_call | solution.py:47
  22.1 0.7 %collective-permute-start.6 = (bf16[128,896]{1,0:T(8,128)(2,1)S(1)}, bf16[128,896]{1,0:T(8,128)(2,1)S(1)}, u32[]{:S(2)}, u32[]{:S(2)}) collective-permute-start(bf16[128,896]{1,0:T(8,128)(2,1)S(1)} %collective-permute-done.refs_2_), channel_id=1, source_target_pairs={{0,8},{4,12},{8,0},{12,4},{16,24},{20,28},{24,16},{28,20},{1,9},{5... | collective-permute-start | bytes 688136 | tf_op jit(solution)/shard_map/ppermute | solution.py:37
  22.7 0.9 %collective-permute-done.4.refs_0_ = bf16[128,896]{1,0:T(8,128)(2,1)S(1)} collective-permute-done((bf16[128,896]{1,0:T(8,128)(2,1)S(1)}, bf16[128,896]{1,0:T(8,128)(2,1)S(1)}, u32[]{:S(2)}, u32[]{:S(2)}) %collective-permute-start.4) | collective-permute-done | bytes 229408 | tf_op jit(solution)/shard_map/ppermute | solution.py:37
  23.6 1.0 %collective-permute-done.3.refs_1_ = bf16[128,896]{1,0:T(8,128)(2,1)S(1)} collective-permute-done((bf16[128,896]{1,0:T(8,128)(2,1)S(1)}, bf16[128,896]{1,0:T(8,128)(2,1)S(1)}, u32[]{:S(2)}, u32[]{:S(2)}) %collective-permute-start.3) | collective-permute-done | bytes 229408 | tf_op jit(solution)/shard_map/ppermute | solution.py:37
  24.6 1.5 %collective-permute-start.5 = (bf16[128,896]{1,0:T(8,128)(2,1)S(1)}, bf16[128,896]{1,0:T(8,128)(2,1)S(1)}, u32[]{:S(2)}, u32[]{:S(2)}) collective-permute-start(bf16[128,896]{1,0:T(8,128)(2,1)S(1)} %collective-permute-done.4.refs_0_), channel_id=1, source_target_pairs={{0,4},{4,0},{8,12},{12,8},{16,20},{20,16},{24,28},{28,24},{1,5},{5... | collective-permute-start | bytes 688136 | tf_op jit(solution)/shard_map/ppermute | solution.py:37
  26.1 1.7 %shard_map.40.refs_1_ = f32[1536,256]{1,0:T(8,128)S(1)} custom-call(bf16[1536,768]{1,0:T(8,128)(2,1)S(1)} %get-tuple-element.19.unit, bf16[128,896]{1,0:T(8,128)(2,1)S(1)} %collective-permute-done.4.refs_0_, bf16[128,896]{1,0:T(8,128)(2,1)S(1)} %collective-permute-done.3.refs_1_, f32[1536,256]{1,0:T(8,128)S(1)} %shard_map.39.refs_2_), custom_call_target="tpu_custom_call", output_to_operand_aliasing={{}: (3, {})} | custom-call | flops 3221225472 | bytes 1048576 | tf_op jit(solution)/shard_map/pallas_call | solution.py:47
  27.8 0.5 collective-permute-done.6.refs_0_
  28.2 1.3 %shard_map.41.refs_1_ = f32[1536,256]{1,0:T(8,128)S(1)} custom-call(bf16[1536,768]{1,0:T(8,128)(2,1)S(1)} %get-tuple-element.19.unit, bf16[128,896]{1,0:T(8,128)(2,1)S(1)} %collective-permute-done.6.refs_0_, f32[1536,256]{1,0:T(8,128)S(1)} %shard_map.40.refs_1_), custom_call_target="tpu_custom_call", output_to_operand_aliasing={{}: (2, {})} | custom-call | flops 1610612736 | bytes 1048576 | tf_op jit(solution)/shard_map/pallas_call | solution.py:47
  29.5 1.1 %collective-permute-done.5.refs_0_ = bf16[128,896]{1,0:T(8,128)(2,1)S(1)} collective-permute-done((bf16[128,896]{1,0:T(8,128)(2,1)S(1)}, bf16[128,896]{1,0:T(8,128)(2,1)S(1)}, u32[]{:S(2)}, u32[]{:S(2)}) %collective-permute-start.5) | collective-permute-done | bytes 229408 | tf_op jit(solution)/shard_map/ppermute | solution.py:37
  30.6 0.9 %shard_map.43 = f32[776,128]{1,0:T(8,128)S(1)} custom-call(bf16[1536,768]{1,0:T(8,128)(2,1)S(1)} %get-tuple-element.19.unit, bf16[128,896]{1,0:T(8,128)(2,1)S(1)} %collective-permute-done.5.refs_0_, f32[1536,256]{1,0:T(8,128)S(1)} %shard_map.41.refs_1_), custom_call_target="tpu_custom_call" | custom-call | flops 805306368 | bytes 1048576 | tf_op jit(solution)/shard_map/pallas_call | solution.py:47
  31.5 0.1 collective-permute-start.7
  31.5 0.9 %shard_map.42.mine = f32[776,128]{1,0:T(8,128)S(1)} custom-call(bf16[1536,768]{1,0:T(8,128)(2,1)S(1)} %get-tuple-element.19.unit, bf16[128,896]{1,0:T(8,128)(2,1)S(1)} %collective-permute-done.5.refs_0_, f32[1536,256]{1,0:T(8,128)S(1)} %shard_map.41.refs_1_), custom_call_target="tpu_custom_call" | custom-call | flops 805306368 | bytes 1048576 | tf_op jit(solution)/shard_map/pallas_call | solution.py:47
  32.4 0.8 %collective-permute-done.7.other = f32[776,128]{1,0:T(8,128)S(1)} collective-permute-done((f32[776,128]{1,0:T(8,128)S(1)}, f32[776,128]{1,0:T(8,128)S(1)}, u32[]{:S(2)}, u32[]{:S(2)}) %collective-permute-start.7) | collective-permute-done | bytes 397344 | tf_op jit(solution)/shard_map/ppermute | solution.py:37
  33.3 1.6 %collective-permute-start.8 = (bf16[800,128]{1,0:T(8,128)(2,1)S(1)}, bf16[800,128]{1,0:T(8,128)(2,1)S(1)}, u32[]{:S(2)}, u32[]{:S(2)}) collective-permute-start(bf16[800,128]{1,0:T(8,128)(2,1)S(1)} %shard_map.44.mine), channel_id=1, source_target_pairs={{0,2},{1,3},{2,0},{3,1},{4,6},{5,7},{6,4},{7,5},{8,10},{9,11},{10,... | collective-permute-start | bytes 614408 | tf_op jit(solution)/shard_map/ppermute | solution.py:37
  34.9 5.6 %collective-permute-done.8.other = bf16[800,128]{1,0:T(8,128)(2,1)S(1)} collective-permute-done((bf16[800,128]{1,0:T(8,128)(2,1)S(1)}, bf16[800,128]{1,0:T(8,128)(2,1)S(1)}, u32[]{:S(2)}, u32[]{:S(2)}) %collective-permute-start.8) | collective-permute-done | bytes 204832 | tf_op jit(solution)/shard_map/ppermute | solution.py:37
  40.5 0.7 %shard_map.45 = (f32[768,128]{1,0:T(8,128)S(1)}, f32[64,128]{1,0:T(8,128)S(1)}, f32[64,128]{1,0:T(8,128)S(1)}) custom-call(bf16[800,128]{1,0:T(8,128)(2,1)S(1)} %shard_map.44.mine, bf16[800,128]{1,0:T(8,128)(2,1)S(1)} %collective-permute-done.8.other), custom_call_target="tpu_custom_call" | custom-call | bytes 1048576 | tf_op jit(solution)/shard_map/pallas_call | solution.py:47
  41.2 0.1 collective-permute-start.15
  41.3 0.5 collective-permute-start.9
  41.8 1.3 %collective-permute-done.9 = f32[64,128]{1,0:T(8,128)S(1)} collective-permute-done((f32[64,128]{1,0:T(8,128)S(1)}, f32[64,128]{1,0:T(8,128)S(1)}, u32[]{:S(2)}, u32[]{:S(2)}) %collective-permute-start.9) | collective-permute-done | bytes 32800 | tf_op jit(solution)/shard_map/ppermute | solution.py:37
  43.0 3.2 %collective-permute-start.12 = (f32[64,128]{1,0:T(8,128)S(1)}, f32[64,128]{1,0:T(8,128)S(1)}, u32[]{:S(2)}, u32[]{:S(2)}) collective-permute-start(f32[64,128]{1,0:T(8,128)S(1)} %add.15), channel_id=1, source_target_pairs={{0,12},{4,8},{8,4},{12,0},{16,28},{20,24},{24,20},{28,16},{1,13},{... | collective-permute-start | bytes 98312 | tf_op jit(solution)/shard_map/ppermute | solution.py:37
  46.2 0.0 collective-permute-start.11
  46.2 0.6 %collective-permute-start.10 = (f32[64,128]{1,0:T(8,128)S(1)}, f32[64,128]{1,0:T(8,128)S(1)}, u32[]{:S(2)}, u32[]{:S(2)}) collective-permute-start(f32[64,128]{1,0:T(8,128)S(1)} %add.15), channel_id=1, source_target_pairs={{0,4},{4,0},{8,12},{12,8},{16,20},{20,16},{24,28},{28,24},{1,5},{5... | collective-permute-start | bytes 98312 | tf_op jit(solution)/shard_map/ppermute | solution.py:37
  46.8 1.3 %collective-permute-done.12 = f32[64,128]{1,0:T(8,128)S(1)} collective-permute-done((f32[64,128]{1,0:T(8,128)S(1)}, f32[64,128]{1,0:T(8,128)S(1)}, u32[]{:S(2)}, u32[]{:S(2)}) %collective-permute-start.12) | collective-permute-done | bytes 32800 | tf_op jit(solution)/shard_map/ppermute | solution.py:37
  48.1 2.0 %collective-permute-done.11 = f32[64,128]{1,0:T(8,128)S(1)} collective-permute-done((f32[64,128]{1,0:T(8,128)S(1)}, f32[64,128]{1,0:T(8,128)S(1)}, u32[]{:S(2)}, u32[]{:S(2)}) %collective-permute-start.11) | collective-permute-done | bytes 32800 | tf_op jit(solution)/shard_map/ppermute | solution.py:37
  50.1 0.0 collective-permute-done.10
  50.1 3.5 %collective-permute-start.13 = (f32[64,128]{1,0:T(8,128)S(1)}, f32[64,128]{1,0:T(8,128)S(1)}, u32[]{:S(2)}, u32[]{:S(2)}) collective-permute-start(f32[64,128]{1,0:T(8,128)S(1)} %add_add_fusion), channel_id=1, source_target_pairs={{0,16},{4,20},{8,24},{12,28},{16,0},{20,4},{24,8},{28,12},{1,17},{... | collective-permute-start | bytes 98312 | tf_op jit(solution)/shard_map/ppermute | solution.py:37
  53.6 1.9 %collective-permute-done.13 = f32[64,128]{1,0:T(8,128)S(1)} collective-permute-done((f32[64,128]{1,0:T(8,128)S(1)}, f32[64,128]{1,0:T(8,128)S(1)}, u32[]{:S(2)}, u32[]{:S(2)}) %collective-permute-start.13) | collective-permute-done | bytes 32800 | tf_op jit(solution)/shard_map/ppermute | solution.py:37
  55.5 0.0 collective-permute-start.14
  55.5 0.0 collective-permute-done.15.theirs
  55.5 0.1 shard_map.46.parts
  55.7 1.0 %collective-permute-done.14.theirs = f32[64,128]{1,0:T(8,128)S(1)} collective-permute-done((f32[64,128]{1,0:T(8,128)S(1)}, f32[64,128]{1,0:T(8,128)S(1)}, u32[]{:S(2)}, u32[]{:S(2)}) %collective-permute-start.14) | collective-permute-done | bytes 32800 | tf_op jit(solution)/shard_map/ppermute | solution.py:37
  56.7 5.2 %shard_map.47 = f32[1536,128]{1,0:T(8,128)} custom-call(f32[64,128]{1,0:T(8,128)S(1)} %add.19.own, f32[64,128]{1,0:T(8,128)S(1)} %collective-permute-done.14.theirs, bf16[1536,384]{1,0:T(8,128)(2,1)S(1)} %shard_map.46.parts), custom_call_target="tpu_custom_call" | custom-call | bytes 1048576 | tf_op jit(solution)/shard_map/pallas_call | solution.py:47
  (4 shorter events, 0.1 us)
Async XLA Ops:
  1.7 14.9 %collective-permute-start.2 = (bf16[128,896]{1,0:T(8,128)(2,1)}, bf16[128,896]{1,0:T(8,128)(2,1)S(1)}, u32[]{:S(2)}, u32[]{:S(2)}) collective-permute-start(bf16[128,896]{1,0:T(8,128)(2,1)} %shard_map.37.block), channel_id=1, source_target_pairs={{0,16},{4,20},{8,24},{12,28},{16,0},{20,4},{24,8},{28,12},{1,17},{... | collective-permute-start | bytes 688136 | tf_op jit(solution)/shard_map/ppermute | solution.py:37
  5.8 11.0 %collective-permute-start.1 = (bf16[128,896]{1,0:T(8,128)(2,1)}, bf16[128,896]{1,0:T(8,128)(2,1)S(1)}, u32[]{:S(2)}, u32[]{:S(2)}) collective-permute-start(bf16[128,896]{1,0:T(8,128)(2,1)} %shard_map.37.block), channel_id=1, source_target_pairs={{0,8},{4,12},{8,0},{12,4},{16,24},{20,28},{24,16},{28,20},{1,9},{5... | collective-permute-start | bytes 688136 | tf_op jit(solution)/shard_map/ppermute | solution.py:37
  7.3 9.5 %collective-permute-start = (bf16[128,896]{1,0:T(8,128)(2,1)}, bf16[128,896]{1,0:T(8,128)(2,1)S(1)}, u32[]{:S(2)}, u32[]{:S(2)}) collective-permute-start(bf16[128,896]{1,0:T(8,128)(2,1)} %shard_map.37.block), channel_id=1, source_target_pairs={{0,4},{4,0},{8,12},{12,8},{16,20},{20,16},{24,28},{28,24},{1,5},{5... | collective-permute-start | bytes 688136 | tf_op jit(solution)/shard_map/ppermute | solution.py:37
  8.8 1.0 %copy-start = (bf16[128,896]{1,0:T(8,128)(2,1)S(1)}, bf16[128,896]{1,0:T(8,128)(2,1)}, u32[]{:S(2)}) copy-start(bf16[128,896]{1,0:T(8,128)(2,1)} %shard_map.37.block) | copy-start | bytes 688132
  16.8 6.8 %collective-permute-start.4 = (bf16[128,896]{1,0:T(8,128)(2,1)S(1)}, bf16[128,896]{1,0:T(8,128)(2,1)S(1)}, u32[]{:S(2)}, u32[]{:S(2)}) collective-permute-start(bf16[128,896]{1,0:T(8,128)(2,1)S(1)} %collective-permute-done.2.refs_0_), channel_id=1, source_target_pairs={{0,8},{4,12},{8,0},{12,4},{16,24},{20,28},{24,16},{28,20},{1,9},{5... | collective-permute-start | bytes 688136 | tf_op jit(solution)/shard_map/ppermute | solution.py:37
  18.3 6.3 %collective-permute-start.3 = (bf16[128,896]{1,0:T(8,128)(2,1)S(1)}, bf16[128,896]{1,0:T(8,128)(2,1)S(1)}, u32[]{:S(2)}, u32[]{:S(2)}) collective-permute-start(bf16[128,896]{1,0:T(8,128)(2,1)S(1)} %collective-permute-done.2.refs_0_), channel_id=1, source_target_pairs={{0,4},{4,0},{8,12},{12,8},{16,20},{20,16},{24,28},{28,24},{1,5},{5... | collective-permute-start | bytes 688136 | tf_op jit(solution)/shard_map/ppermute | solution.py:37
  22.1 6.2 %collective-permute-start.6 = (bf16[128,896]{1,0:T(8,128)(2,1)S(1)}, bf16[128,896]{1,0:T(8,128)(2,1)S(1)}, u32[]{:S(2)}, u32[]{:S(2)}) collective-permute-start(bf16[128,896]{1,0:T(8,128)(2,1)S(1)} %collective-permute-done.refs_2_), channel_id=1, source_target_pairs={{0,8},{4,12},{8,0},{12,4},{16,24},{20,28},{24,16},{28,20},{1,9},{5... | collective-permute-start | bytes 688136 | tf_op jit(solution)/shard_map/ppermute | solution.py:37
  24.6 6.0 %collective-permute-start.5 = (bf16[128,896]{1,0:T(8,128)(2,1)S(1)}, bf16[128,896]{1,0:T(8,128)(2,1)S(1)}, u32[]{:S(2)}, u32[]{:S(2)}) collective-permute-start(bf16[128,896]{1,0:T(8,128)(2,1)S(1)} %collective-permute-done.4.refs_0_), channel_id=1, source_target_pairs={{0,4},{4,0},{8,12},{12,8},{16,20},{20,16},{24,28},{28,24},{1,5},{5... | collective-permute-start | bytes 688136 | tf_op jit(solution)/shard_map/ppermute | solution.py:37
  31.5 1.8 %collective-permute-start.7 = (f32[776,128]{1,0:T(8,128)S(1)}, f32[776,128]{1,0:T(8,128)S(1)}, u32[]{:S(2)}, u32[]{:S(2)}) collective-permute-start(f32[776,128]{1,0:T(8,128)S(1)} %shard_map.43), channel_id=1, source_target_pairs={{0,1},{1,0},{2,3},{3,2},{4,5},{5,4},{6,7},{7,6},{8,9},{9,8},{10,11... | collective-permute-start | bytes 1191944 | tf_op jit(solution)/shard_map/ppermute | solution.py:37
  33.3 7.2 %collective-permute-start.8 = (bf16[800,128]{1,0:T(8,128)(2,1)S(1)}, bf16[800,128]{1,0:T(8,128)(2,1)S(1)}, u32[]{:S(2)}, u32[]{:S(2)}) collective-permute-start(bf16[800,128]{1,0:T(8,128)(2,1)S(1)} %shard_map.44.mine), channel_id=1, source_target_pairs={{0,2},{1,3},{2,0},{3,1},{4,6},{5,7},{6,4},{7,5},{8,10},{9,11},{10,... | collective-permute-start | bytes 614408 | tf_op jit(solution)/shard_map/ppermute | solution.py:37
  41.2 14.3 %collective-permute-start.15 = (f32[768,128]{1,0:T(8,128)S(1)}, f32[768,128]{1,0:T(8,128)S(1)}, u32[]{:S(2)}, u32[]{:S(2)}) collective-permute-start(f32[768,128]{1,0:T(8,128)S(1)} %get-tuple-element.32.own), channel_id=1, source_target_pairs={{0,1},{1,0},{2,3},{3,2},{4,5},{5,4},{6,7},{7,6},{8,9},{9,8},{10,11... | collective-permute-start | bytes 1179656 | tf_op jit(solution)/shard_map/ppermute | solution.py:37
  41.3 1.8 %collective-permute-start.9 = (f32[64,128]{1,0:T(8,128)S(1)}, f32[64,128]{1,0:T(8,128)S(1)}, u32[]{:S(2)}, u32[]{:S(2)}) collective-permute-start(f32[64,128]{1,0:T(8,128)S(1)} %get-tuple-element.31), channel_id=1, source_target_pairs={{0,1},{1,0},{2,3},{3,2},{4,5},{5,4},{6,7},{7,6},{8,9},{9,8},{10,11... | collective-permute-start | bytes 98312 | tf_op jit(solution)/shard_map/ppermute | solution.py:37
  43.0 5.1 %collective-permute-start.12 = (f32[64,128]{1,0:T(8,128)S(1)}, f32[64,128]{1,0:T(8,128)S(1)}, u32[]{:S(2)}, u32[]{:S(2)}) collective-permute-start(f32[64,128]{1,0:T(8,128)S(1)} %add.15), channel_id=1, source_target_pairs={{0,12},{4,8},{8,4},{12,0},{16,28},{20,24},{24,20},{28,16},{1,13},{... | collective-permute-start | bytes 98312 | tf_op jit(solution)/shard_map/ppermute | solution.py:37
  46.2 3.9 %collective-permute-start.11 = (f32[64,128]{1,0:T(8,128)S(1)}, f32[64,128]{1,0:T(8,128)S(1)}, u32[]{:S(2)}, u32[]{:S(2)}) collective-permute-start(f32[64,128]{1,0:T(8,128)S(1)} %add.15), channel_id=1, source_target_pairs={{0,8},{4,12},{8,0},{12,4},{16,24},{20,28},{24,16},{28,20},{1,9},{5... | collective-permute-start | bytes 98312 | tf_op jit(solution)/shard_map/ppermute | solution.py:37
  46.2 3.9 %collective-permute-start.10 = (f32[64,128]{1,0:T(8,128)S(1)}, f32[64,128]{1,0:T(8,128)S(1)}, u32[]{:S(2)}, u32[]{:S(2)}) collective-permute-start(f32[64,128]{1,0:T(8,128)S(1)} %add.15), channel_id=1, source_target_pairs={{0,4},{4,0},{8,12},{12,8},{16,20},{20,16},{24,28},{28,24},{1,5},{5... | collective-permute-start | bytes 98312 | tf_op jit(solution)/shard_map/ppermute | solution.py:37
  50.1 5.3 %collective-permute-start.13 = (f32[64,128]{1,0:T(8,128)S(1)}, f32[64,128]{1,0:T(8,128)S(1)}, u32[]{:S(2)}, u32[]{:S(2)}) collective-permute-start(f32[64,128]{1,0:T(8,128)S(1)} %add_add_fusion), channel_id=1, source_target_pairs={{0,16},{4,20},{8,24},{12,28},{16,0},{20,4},{24,8},{28,12},{1,17},{... | collective-permute-start | bytes 98312 | tf_op jit(solution)/shard_map/ppermute | solution.py:37
  55.5 1.2 %collective-permute-start.14 = (f32[64,128]{1,0:T(8,128)S(1)}, f32[64,128]{1,0:T(8,128)S(1)}, u32[]{:S(2)}, u32[]{:S(2)}) collective-permute-start(f32[64,128]{1,0:T(8,128)S(1)} %add.19.own), channel_id=1, source_target_pairs={{0,1},{1,0},{2,3},{3,2},{4,5},{5,4},{6,7},{7,6},{8,9},{9,8},{10,11... | collective-permute-start | bytes 98312 | tf_op jit(solution)/shard_map/ppermute | solution.py:37

commit v8 on v7

--- a/solution.py
+++ b/solution.py
@@ -11,7 +11,7 @@
 kernel_gain = 16.0
 LANES = 128
 TILE = 512
-PANEL = 8
+PANEL = 16
 VMEM = pl.BlockSpec(memory_space=pltpu.VMEM)
 BF16 = jnp.bfloat16
 F32 = jnp.float32
@@ -56,6 +56,11 @@
         ),
         compiler_params=pltpu.CompilerParams(vmem_limit_bytes=48 << 20),
     )(*operands)
+
+
+def join_kernel(left, right, out):
+    out[:, : left.shape[1]] = left[...]
+    out[:, left.shape[1] :] = right[...]
 
 
 def beside_kernel(left, right, out, sems):
@@ -260,15 +265,18 @@
     lmk_bits = [1 << b for b in range(1, num_lmk.bit_length() - 1)]
     shape = jax.ShapeDtypeStruct
 
-    held = {
-        0: pl.pallas_call(
-            beside_kernel,
-            out_shape=shape((landmarks.shape[0], features + size), BF16),
-            in_specs=[pl.BlockSpec(memory_space=pltpu.HBM)] * 2,
-            out_specs=VMEM,
-            scratch_shapes=[pltpu.SemaphoreType.DMA((1 + landmarks.shape[0] // 16,))],
-        )(landmarks, eigvecs)
-    }
+    own = (landmarks, eigvecs)
+    joined = shape((landmarks.shape[0], features + size), BF16)
+    held = {}
+    if num_pts == 8:
+        held[4] = [swap(value, "pts", num_pts, 4) for value in own]
+    held[0] = pl.pallas_call(
+        beside_kernel,
+        out_shape=joined,
+        in_specs=[pl.BlockSpec(memory_space=pltpu.HBM)] * 2,
+        out_specs=VMEM,
+        scratch_shapes=[pltpu.SemaphoreType.DMA((1 + landmarks.shape[0] // 16,))],
+    )(*own)
     if num_pts == 8:
         rounds = [[(0, 4), (0, 2), (0, 1)], [(4, 2), (4, 1)], [(6, 1)]]
         late = (1, 2)
@@ -292,13 +300,15 @@
     ready, unit, total = [0], None, None
     for turn, hops in enumerate(rounds):
         for mask, bit in hops:
+            if mask ^ bit in held:
+                continue
             held[mask ^ bit] = swap(held[mask], "pts", num_pts, bit)
         if unit is None:
             unit, total = call_on(
                 first_kernel,
                 (shape((num_rows, features), BF16), shape((num_rows, 2 * size), F32)),
                 (points, held[0]),
-                flops=flops,
+                flops=flops * 4,
             )
         else:
             total = more(total, ready)
@@ -312,6 +322,8 @@
             tied = list(dict.fromkeys(ready + sources))[::-1]
             *fresh, total = lax.optimization_barrier((*[held[mask] for mask in tied], total))
             held.update(zip(tied, fresh))
+            if turn == 0 and late:
+                held[4] = call_on(join_kernel, joined, held[4])
     if late:
         total = more(total, [late[0] ^ late[1]])
     group = ready

time: 62.1 us -> 67.7 us (1.090)
  Pallas kernels: 17.7 us -> 22.7 us
  starting transfers between devices: 21.8 us -> 23.3 us
  waiting for transfers between devices: 21.2 us -> 20.2 us
    pallas_call x10 -> x11, Pallas kernels: 16.1 us -> 21.1 us  [call_on(): pl.pallas_call(kernel, out_shape=out, in_specs=[rest.get('in_specs', VMEM...]
    ppermute x16 -> x17, starting transfers between devices: 21.8 us -> 23.3 us  [swap(): return lax.ppermute(value, axis, [(i, i ^ bit) for i in range(size)])]
    ppermute x16 -> x17, waiting for transfers between devices: 21.2 us -> 20.2 us  [swap(): return lax.ppermute(value, axis, [(i, i ^ bit) for i in range(size)])]
  transfers between devices with their start and end apart: 16 -> 17, of which waited for: 13 -> 12; matrix products, arithmetic and copies ran while one was open for 0% -> 0% of each run, Pallas kernels for 15% -> 16%
where the time goes in v8:
time: 67.7 us; the launch traced here: 67.5 us
  starting transfers between devices  23.3 us (34%)
  Pallas kernels  22.7 us (34%)
  waiting for transfers between devices  20.2 us (30%)
  local copies, waits for them, and re-layouts  0.97 us (1%)
    ppermute x17, starting transfers between devices, swap(): return lax.ppermute(value, axis, [(i, i ^ bit) for i in range(size)])  23.3 us
    pallas_call x11, Pallas kernels, call_on(): pl.pallas_call(kernel, out_shape=out, in_specs=[rest.get('in_specs', VMEM...  21.1 us
    ppermute x17, waiting for transfers between devices, swap(): return lax.ppermute(value, axis, [(i, i ^ bit) for i in range(size)])  20.2 us
    pallas_call x1, Pallas kernels, per_device(): pl.pallas_call(beside_kernel, out_shape=joined, in_specs=[pl.BlockSpec(me...  1.64 us
  transfers between devices with their start and end apart: 17, of which 12 were waited for; matrix products, arithmetic and copies ran while one was open for 0% of the time, Pallas kernels for 16%

profile of v8, /device:TPU:0, one launch (start us, length us, event | category | flops | bytes accessed | tf_op | source)
XLA Modules:
  0.0 67.5 jit_solution(9277760780044846618)
XLA Ops:
  0.0 4.0 %collective-permute-start.3 = (bf16[128,128]{1,0:T(8,128)(2,1)}, bf16[128,128]{1,0:T(8,128)(2,1)S(1)}, u32[]{:S(2)}, u32[]{:S(2)}) collective-permute-start(bf16[128,128]{1,0:T(8,128)(2,1)} %right.1), channel_id=1, source_target_pairs={{0,16},{4,20},{8,24},{12,28},{16,0},{20,4},{24,8},{28,12},{1,17},{... | collective-permute-start | bytes 98312 | tf_op jit(solution)/shard_map/ppermute | solution.py:37
  4.0 0.0 collective-permute-start.2
  4.1 1.6 %shard_map.37.block = bf16[128,896]{1,0:T(8,128)(2,1)} custom-call(bf16[128,768]{1,0:T(8,128)(2,1)} %left.1, bf16[128,128]{1,0:T(8,128)(2,1)} %right.1), custom_call_target="tpu_custom_call" | custom-call | tf_op jit(solution)/shard_map/pallas_call | solution.py:273
  5.7 1.9 %collective-permute-start.1 = (bf16[128,896]{1,0:T(8,128)(2,1)}, bf16[128,896]{1,0:T(8,128)(2,1)S(1)}, u32[]{:S(2)}, u32[]{:S(2)}) collective-permute-start(bf16[128,896]{1,0:T(8,128)(2,1)} %shard_map.37.block), channel_id=1, source_target_pairs={{0,8},{4,12},{8,0},{12,4},{16,24},{20,28},{24,16},{28,20},{1,9},{5... | collective-permute-start | bytes 688136 | tf_op jit(solution)/shard_map/ppermute | solution.py:37
  7.7 1.5 %collective-permute-start = (bf16[128,896]{1,0:T(8,128)(2,1)}, bf16[128,896]{1,0:T(8,128)(2,1)S(1)}, u32[]{:S(2)}, u32[]{:S(2)}) collective-permute-start(bf16[128,896]{1,0:T(8,128)(2,1)} %shard_map.37.block), channel_id=1, source_target_pairs={{0,4},{4,0},{8,12},{12,8},{16,20},{20,16},{24,28},{28,24},{1,5},{5... | collective-permute-start | bytes 688136 | tf_op jit(solution)/shard_map/ppermute | solution.py:37
  9.2 0.0 copy-start
  9.2 1.0 %copy-done = bf16[128,896]{1,0:T(8,128)(2,1)S(1)} copy-done((bf16[128,896]{1,0:T(8,128)(2,1)S(1)}, bf16[128,896]{1,0:T(8,128)(2,1)}, u32[]{:S(2)}) %copy-start) | copy-done | bytes 229400
  10.1 3.1 %shard_map.38 = (bf16[1536,768]{1,0:T(8,128)(2,1)S(1)}, f32[1536,256]{1,0:T(8,128)S(1)}) custom-call(bf16[1536,768]{1,0:T(8,128)(2,1)} %points.1, bf16[128,896]{1,0:T(8,128)(2,1)S(1)} %copy-done), custom_call_target="tpu_custom_call" | custom-call | flops 6442450944 | bytes 1048576 | tf_op jit(solution)/shard_map/pallas_call | solution.py:47
  13.2 0.0 collective-permute-done.3.right
  13.2 2.8 %collective-permute-done.2.left = bf16[128,768]{1,0:T(8,128)(2,1)S(1)} collective-permute-done((bf16[128,768]{1,0:T(8,128)(2,1)}, bf16[128,768]{1,0:T(8,128)(2,1)S(1)}, u32[]{:S(2)}, u32[]{:S(2)}) %collective-permute-start.2) | collective-permute-done | bytes 196640 | tf_op jit(solution)/shard_map/ppermute | solution.py:37
  16.0 0.6 collective-permute-done.1.refs_1_
  16.6 0.0 collective-permute-done.refs_2_
  16.6 0.1 collective-permute-start.5
  16.7 1.6 %collective-permute-start.4 = (bf16[128,896]{1,0:T(8,128)(2,1)S(1)}, bf16[128,896]{1,0:T(8,128)(2,1)S(1)}, u32[]{:S(2)}, u32[]{:S(2)}) collective-permute-start(bf16[128,896]{1,0:T(8,128)(2,1)S(1)} %shard_map.39.refs_0_), channel_id=1, source_target_pairs={{0,4},{4,0},{8,12},{12,8},{16,20},{20,16},{24,28},{28,24},{1,5},{5... | collective-permute-start | bytes 688136 | tf_op jit(solution)/shard_map/ppermute | solution.py:37
  18.3 2.3 %shard_map.40.refs_2_ = f32[1536,256]{1,0:T(8,128)S(1)} custom-call(bf16[1536,768]{1,0:T(8,128)(2,1)S(1)} %get-tuple-element.20.unit, bf16[128,896]{1,0:T(8,128)(2,1)S(1)} %shard_map.39.refs_0_, bf16[128,896]{1,0:T(8,128)(2,1)S(1)} %collective-permute-done.1.refs_1_, ...), custom_call_target="tpu_custom_call", output_to_operand_aliasing={{}: (4, {})} | custom-call | flops 4831838208 | bytes 1048576 | tf_op jit(solution)/shard_map/pallas_call | solution.py:47
  20.6 2.0 %collective-permute-start.7 = (bf16[128,896]{1,0:T(8,128)(2,1)S(1)}, bf16[128,896]{1,0:T(8,128)(2,1)S(1)}, u32[]{:S(2)}, u32[]{:S(2)}) collective-permute-start(bf16[128,896]{1,0:T(8,128)(2,1)S(1)} %collective-permute-done.refs_2_), channel_id=1, source_target_pairs={{0,8},{4,12},{8,0},{12,4},{16,24},{20,28},{24,16},{28,20},{1,9},{5... | collective-permute-start | bytes 688136 | tf_op jit(solution)/shard_map/ppermute | solution.py:37
  22.6 1.2 %collective-permute-done.5.refs_0_ = bf16[128,896]{1,0:T(8,128)(2,1)S(1)} collective-permute-done((bf16[128,896]{1,0:T(8,128)(2,1)S(1)}, bf16[128,896]{1,0:T(8,128)(2,1)S(1)}, u32[]{:S(2)}, u32[]{:S(2)}) %collective-permute-start.5) | collective-permute-done | bytes 229408 | tf_op jit(solution)/shard_map/ppermute | solution.py:37
  23.8 0.0 collective-permute-done.4.refs_1_
  23.8 2.6 %collective-permute-start.6 = (bf16[128,896]{1,0:T(8,128)(2,1)S(1)}, bf16[128,896]{1,0:T(8,128)(2,1)S(1)}, u32[]{:S(2)}, u32[]{:S(2)}) collective-permute-start(bf16[128,896]{1,0:T(8,128)(2,1)S(1)} %collective-permute-done.5.refs_0_), channel_id=1, source_target_pairs={{0,4},{4,0},{8,12},{12,8},{16,20},{20,16},{24,28},{28,24},{1,5},{5... | collective-permute-start | bytes 688136 | tf_op jit(solution)/shard_map/ppermute | solution.py:37
  26.3 1.7 %shard_map.41.refs_1_ = f32[1536,256]{1,0:T(8,128)S(1)} custom-call(bf16[1536,768]{1,0:T(8,128)(2,1)S(1)} %get-tuple-element.20.unit, bf16[128,896]{1,0:T(8,128)(2,1)S(1)} %collective-permute-done.5.refs_0_, bf16[128,896]{1,0:T(8,128)(2,1)S(1)} %collective-permute-done.4.refs_1_, f32[1536,256]{1,0:T(8,128)S(1)} %shard_map.40.refs_2_), custom_call_target="tpu_custom_call", output_to_operand_aliasing={{}: (3, {})} | custom-call | flops 3221225472 | bytes 1048576 | tf_op jit(solution)/shard_map/pallas_call | solution.py:47
  28.0 0.0 collective-permute-done.7.refs_0_
  28.1 1.3 %shard_map.42.refs_1_ = f32[1536,256]{1,0:T(8,128)S(1)} custom-call(bf16[1536,768]{1,0:T(8,128)(2,1)S(1)} %get-tuple-element.20.unit, bf16[128,896]{1,0:T(8,128)(2,1)S(1)} %collective-permute-done.7.refs_0_, f32[1536,256]{1,0:T(8,128)S(1)} %shard_map.41.refs_1_), custom_call_target="tpu_custom_call", output_to_operand_aliasing={{}: (2, {})} | custom-call | flops 1610612736 | bytes 1048576 | tf_op jit(solution)/shard_map/pallas_call | solution.py:47
  29.3 1.0 %collective-permute-done.6.refs_0_ = bf16[128,896]{1,0:T(8,128)(2,1)S(1)} collective-permute-done((bf16[128,896]{1,0:T(8,128)(2,1)S(1)}, bf16[128,896]{1,0:T(8,128)(2,1)S(1)}, u32[]{:S(2)}, u32[]{:S(2)}) %collective-permute-start.6) | collective-permute-done | bytes 229408 | tf_op jit(solution)/shard_map/ppermute | solution.py:37
  30.3 0.9 %shard_map.44 = f32[776,128]{1,0:T(8,128)S(1)} custom-call(bf16[1536,768]{1,0:T(8,128)(2,1)S(1)} %get-tuple-element.20.unit, bf16[128,896]{1,0:T(8,128)(2,1)S(1)} %collective-permute-done.6.refs_0_, f32[1536,256]{1,0:T(8,128)S(1)} %shard_map.42.refs_1_), custom_call_target="tpu_custom_call" | custom-call | flops 805306368 | bytes 1048576 | tf_op jit(solution)/shard_map/pallas_call | solution.py:47
  31.2 0.1 collective-permute-start.8
  31.3 0.9 %shard_map.43.mine = f32[776,128]{1,0:T(8,128)S(1)} custom-call(bf16[1536,768]{1,0:T(8,128)(2,1)S(1)} %get-tuple-element.20.unit, bf16[128,896]{1,0:T(8,128)(2,1)S(1)} %collective-permute-done.6.refs_0_, f32[1536,256]{1,0:T(8,128)S(1)} %shard_map.42.refs_1_), custom_call_target="tpu_custom_call" | custom-call | flops 805306368 | bytes 1048576 | tf_op jit(solution)/shard_map/pallas_call | solution.py:47
  32.2 0.8 %collective-permute-done.8.other = f32[776,128]{1,0:T(8,128)S(1)} collective-permute-done((f32[776,128]{1,0:T(8,128)S(1)}, f32[776,128]{1,0:T(8,128)S(1)}, u32[]{:S(2)}, u32[]{:S(2)}) %collective-permute-start.8) | collective-permute-done | bytes 397344 | tf_op jit(solution)/shard_map/ppermute | solution.py:37
  33.1 1.6 %collective-permute-start.9 = (bf16[800,128]{1,0:T(8,128)(2,1)S(1)}, bf16[800,128]{1,0:T(8,128)(2,1)S(1)}, u32[]{:S(2)}, u32[]{:S(2)}) collective-permute-start(bf16[800,128]{1,0:T(8,128)(2,1)S(1)} %shard_map.45.mine), channel_id=1, source_target_pairs={{0,2},{1,3},{2,0},{3,1},{4,6},{5,7},{6,4},{7,5},{8,10},{9,11},{10,... | collective-permute-start | bytes 614408 | tf_op jit(solution)/shard_map/ppermute | solution.py:37
  34.6 5.6 %collective-permute-done.9.other = bf16[800,128]{1,0:T(8,128)(2,1)S(1)} collective-permute-done((bf16[800,128]{1,0:T(8,128)(2,1)S(1)}, bf16[800,128]{1,0:T(8,128)(2,1)S(1)}, u32[]{:S(2)}, u32[]{:S(2)}) %collective-permute-start.9) | collective-permute-done | bytes 204832 | tf_op jit(solution)/shard_map/ppermute | solution.py:37
  40.2 0.7 %shard_map.46 = (f32[768,128]{1,0:T(8,128)S(1)}, f32[64,128]{1,0:T(8,128)S(1)}, f32[64,128]{1,0:T(8,128)S(1)}) custom-call(bf16[800,128]{1,0:T(8,128)(2,1)S(1)} %shard_map.45.mine, bf16[800,128]{1,0:T(8,128)(2,1)S(1)} %collective-permute-done.9.other), custom_call_target="tpu_custom_call" | custom-call | bytes 1048576 | tf_op jit(solution)/shard_map/pallas_call | solution.py:47
  40.9 0.1 collective-permute-start.16
  41.0 0.5 collective-permute-start.10
  41.5 1.3 %collective-permute-done.10 = f32[64,128]{1,0:T(8,128)S(1)} collective-permute-done((f32[64,128]{1,0:T(8,128)S(1)}, f32[64,128]{1,0:T(8,128)S(1)}, u32[]{:S(2)}, u32[]{:S(2)}) %collective-permute-start.10) | collective-permute-done | bytes 32800 | tf_op jit(solution)/shard_map/ppermute | solution.py:37
  42.8 1.4 %collective-permute-start.13 = (f32[64,128]{1,0:T(8,128)S(1)}, f32[64,128]{1,0:T(8,128)S(1)}, u32[]{:S(2)}, u32[]{:S(2)}) collective-permute-start(f32[64,128]{1,0:T(8,128)S(1)} %add.15), channel_id=1, source_target_pairs={{0,12},{4,8},{8,4},{12,0},{16,28},{20,24},{24,20},{28,16},{1,13},{... | collective-permute-start | bytes 98312 | tf_op jit(solution)/shard_map/ppermute | solution.py:37
  44.2 2.1 %collective-permute-start.12 = (f32[64,128]{1,0:T(8,128)S(1)}, f32[64,128]{1,0:T(8,128)S(1)}, u32[]{:S(2)}, u32[]{:S(2)}) collective-permute-start(f32[64,128]{1,0:T(8,128)S(1)} %add.15), channel_id=1, source_target_pairs={{0,8},{4,12},{8,0},{12,4},{16,24},{20,28},{24,16},{28,20},{1,9},{5... | collective-permute-start | bytes 98312 | tf_op jit(solution)/shard_map/ppermute | solution.py:37
  46.3 0.0 collective-permute-start.11
  46.3 1.5 %collective-permute-done.13 = f32[64,128]{1,0:T(8,128)S(1)} collective-permute-done((f32[64,128]{1,0:T(8,128)S(1)}, f32[64,128]{1,0:T(8,128)S(1)}, u32[]{:S(2)}, u32[]{:S(2)}) %collective-permute-start.13) | collective-permute-done | bytes 32800 | tf_op jit(solution)/shard_map/ppermute | solution.py:37
  47.8 0.8 %collective-permute-done.12 = f32[64,128]{1,0:T(8,128)S(1)} collective-permute-done((f32[64,128]{1,0:T(8,128)S(1)}, f32[64,128]{1,0:T(8,128)S(1)}, u32[]{:S(2)}, u32[]{:S(2)}) %collective-permute-start.12) | collective-permute-done | bytes 32800 | tf_op jit(solution)/shard_map/ppermute | solution.py:37
  48.5 1.7 %collective-permute-done.11 = f32[64,128]{1,0:T(8,128)S(1)} collective-permute-done((f32[64,128]{1,0:T(8,128)S(1)}, f32[64,128]{1,0:T(8,128)S(1)}, u32[]{:S(2)}, u32[]{:S(2)}) %collective-permute-start.11) | collective-permute-done | bytes 32800 | tf_op jit(solution)/shard_map/ppermute | solution.py:37
  50.2 3.9 %collective-permute-start.14 = (f32[64,128]{1,0:T(8,128)S(1)}, f32[64,128]{1,0:T(8,128)S(1)}, u32[]{:S(2)}, u32[]{:S(2)}) collective-permute-start(f32[64,128]{1,0:T(8,128)S(1)} %add_add_fusion), channel_id=1, source_target_pairs={{0,16},{4,20},{8,24},{12,28},{16,0},{20,4},{24,8},{28,12},{1,17},{... | collective-permute-start | bytes 98312 | tf_op jit(solution)/shard_map/ppermute | solution.py:37
  54.1 1.9 %collective-permute-done.14 = f32[64,128]{1,0:T(8,128)S(1)} collective-permute-done((f32[64,128]{1,0:T(8,128)S(1)}, f32[64,128]{1,0:T(8,128)S(1)}, u32[]{:S(2)}, u32[]{:S(2)}) %collective-permute-start.14) | collective-permute-done | bytes 32800 | tf_op jit(solution)/shard_map/ppermute | solution.py:37
  56.0 0.0 collective-permute-start.15
  56.0 0.0 collective-permute-done.16.theirs
  56.0 0.1 shard_map.47.parts
  56.2 1.0 %collective-permute-done.15.theirs = f32[64,128]{1,0:T(8,128)S(1)} collective-permute-done((f32[64,128]{1,0:T(8,128)S(1)}, f32[64,128]{1,0:T(8,128)S(1)}, u32[]{:S(2)}, u32[]{:S(2)}) %collective-permute-start.15) | collective-permute-done | bytes 32800 | tf_op jit(solution)/shard_map/ppermute | solution.py:37
  57.2 10.1 %shard_map.48 = f32[1536,128]{1,0:T(8,128)} custom-call(f32[64,128]{1,0:T(8,128)S(1)} %add.19.own, f32[64,128]{1,0:T(8,128)S(1)} %collective-permute-done.15.theirs, bf16[1536,384]{1,0:T(8,128)(2,1)S(1)} %shard_map.47.parts), custom_call_target="tpu_custom_call" | custom-call | bytes 1048576 | tf_op jit(solution)/shard_map/pallas_call | solution.py:47
  (5 shorter events, 0.1 us)
Async XLA Ops:
  0.0 13.2 %collective-permute-start.3 = (bf16[128,128]{1,0:T(8,128)(2,1)}, bf16[128,128]{1,0:T(8,128)(2,1)S(1)}, u32[]{:S(2)}, u32[]{:S(2)}) collective-permute-start(bf16[128,128]{1,0:T(8,128)(2,1)} %right.1), channel_id=1, source_target_pairs={{0,16},{4,20},{8,24},{12,28},{16,0},{20,4},{24,8},{28,12},{1,17},{... | collective-permute-start | bytes 98312 | tf_op jit(solution)/shard_map/ppermute | solution.py:37
  4.0 12.0 %collective-permute-start.2 = (bf16[128,768]{1,0:T(8,128)(2,1)}, bf16[128,768]{1,0:T(8,128)(2,1)S(1)}, u32[]{:S(2)}, u32[]{:S(2)}) collective-permute-start(bf16[128,768]{1,0:T(8,128)(2,1)} %left.1), channel_id=1, source_target_pairs={{0,16},{4,20},{8,24},{12,28},{16,0},{20,4},{24,8},{28,12},{1,17},{... | collective-permute-start | bytes 589832 | tf_op jit(solution)/shard_map/ppermute | solution.py:37
  5.7 10.9 %collective-permute-start.1 = (bf16[128,896]{1,0:T(8,128)(2,1)}, bf16[128,896]{1,0:T(8,128)(2,1)S(1)}, u32[]{:S(2)}, u32[]{:S(2)}) collective-permute-start(bf16[128,896]{1,0:T(8,128)(2,1)} %shard_map.37.block), channel_id=1, source_target_pairs={{0,8},{4,12},{8,0},{12,4},{16,24},{20,28},{24,16},{28,20},{1,9},{5... | collective-permute-start | bytes 688136 | tf_op jit(solution)/shard_map/ppermute | solution.py:37
  7.7 9.0 %collective-permute-start = (bf16[128,896]{1,0:T(8,128)(2,1)}, bf16[128,896]{1,0:T(8,128)(2,1)S(1)}, u32[]{:S(2)}, u32[]{:S(2)}) collective-permute-start(bf16[128,896]{1,0:T(8,128)(2,1)} %shard_map.37.block), channel_id=1, source_target_pairs={{0,4},{4,0},{8,12},{12,8},{16,20},{20,16},{24,28},{28,24},{1,5},{5... | collective-permute-start | bytes 688136 | tf_op jit(solution)/shard_map/ppermute | solution.py:37
  9.2 1.0 %copy-start = (bf16[128,896]{1,0:T(8,128)(2,1)S(1)}, bf16[128,896]{1,0:T(8,128)(2,1)}, u32[]{:S(2)}) copy-start(bf16[128,896]{1,0:T(8,128)(2,1)} %shard_map.37.block) | copy-start | bytes 688132
  16.6 7.1 %collective-permute-start.5 = (bf16[128,896]{1,0:T(8,128)(2,1)S(1)}, bf16[128,896]{1,0:T(8,128)(2,1)S(1)}, u32[]{:S(2)}, u32[]{:S(2)}) collective-permute-start(bf16[128,896]{1,0:T(8,128)(2,1)S(1)} %shard_map.39.refs_0_), channel_id=1, source_target_pairs={{0,8},{4,12},{8,0},{12,4},{16,24},{20,28},{24,16},{28,20},{1,9},{5... | collective-permute-start | bytes 688136 | tf_op jit(solution)/shard_map/ppermute | solution.py:37
  16.7 7.0 %collective-permute-start.4 = (bf16[128,896]{1,0:T(8,128)(2,1)S(1)}, bf16[128,896]{1,0:T(8,128)(2,1)S(1)}, u32[]{:S(2)}, u32[]{:S(2)}) collective-permute-start(bf16[128,896]{1,0:T(8,128)(2,1)S(1)} %shard_map.39.refs_0_), channel_id=1, source_target_pairs={{0,4},{4,0},{8,12},{12,8},{16,20},{20,16},{24,28},{28,24},{1,5},{5... | collective-permute-start | bytes 688136 | tf_op jit(solution)/shard_map/ppermute | solution.py:37
  20.6 7.5 %collective-permute-start.7 = (bf16[128,896]{1,0:T(8,128)(2,1)S(1)}, bf16[128,896]{1,0:T(8,128)(2,1)S(1)}, u32[]{:S(2)}, u32[]{:S(2)}) collective-permute-start(bf16[128,896]{1,0:T(8,128)(2,1)S(1)} %collective-permute-done.refs_2_), channel_id=1, source_target_pairs={{0,8},{4,12},{8,0},{12,4},{16,24},{20,28},{24,16},{28,20},{1,9},{5... | collective-permute-start | bytes 688136 | tf_op jit(solution)/shard_map/ppermute | solution.py:37
  23.8 6.6 %collective-permute-start.6 = (bf16[128,896]{1,0:T(8,128)(2,1)S(1)}, bf16[128,896]{1,0:T(8,128)(2,1)S(1)}, u32[]{:S(2)}, u32[]{:S(2)}) collective-permute-start(bf16[128,896]{1,0:T(8,128)(2,1)S(1)} %collective-permute-done.5.refs_0_), channel_id=1, source_target_pairs={{0,4},{4,0},{8,12},{12,8},{16,20},{20,16},{24,28},{28,24},{1,5},{5... | collective-permute-start | bytes 688136 | tf_op jit(solution)/shard_map/ppermute | solution.py:37
  31.2 1.8 %collective-permute-start.8 = (f32[776,128]{1,0:T(8,128)S(1)}, f32[776,128]{1,0:T(8,128)S(1)}, u32[]{:S(2)}, u32[]{:S(2)}) collective-permute-start(f32[776,128]{1,0:T(8,128)S(1)} %shard_map.44), channel_id=1, source_target_pairs={{0,1},{1,0},{2,3},{3,2},{4,5},{5,4},{6,7},{7,6},{8,9},{9,8},{10,11... | collective-permute-start | bytes 1191944 | tf_op jit(solution)/shard_map/ppermute | solution.py:37
  33.1 7.2 %collective-permute-start.9 = (bf16[800,128]{1,0:T(8,128)(2,1)S(1)}, bf16[800,128]{1,0:T(8,128)(2,1)S(1)}, u32[]{:S(2)}, u32[]{:S(2)}) collective-permute-start(bf16[800,128]{1,0:T(8,128)(2,1)S(1)} %shard_map.45.mine), channel_id=1, source_target_pairs={{0,2},{1,3},{2,0},{3,1},{4,6},{5,7},{6,4},{7,5},{8,10},{9,11},{10,... | collective-permute-start | bytes 614408 | tf_op jit(solution)/shard_map/ppermute | solution.py:37
  40.9 15.1 %collective-permute-start.16 = (f32[768,128]{1,0:T(8,128)S(1)}, f32[768,128]{1,0:T(8,128)S(1)}, u32[]{:S(2)}, u32[]{:S(2)}) collective-permute-start(f32[768,128]{1,0:T(8,128)S(1)} %get-tuple-element.34.own), channel_id=1, source_target_pairs={{0,1},{1,0},{2,3},{3,2},{4,5},{5,4},{6,7},{7,6},{8,9},{9,8},{10,11... | collective-permute-start | bytes 1179656 | tf_op jit(solution)/shard_map/ppermute | solution.py:37
  41.0 1.8 %collective-permute-start.10 = (f32[64,128]{1,0:T(8,128)S(1)}, f32[64,128]{1,0:T(8,128)S(1)}, u32[]{:S(2)}, u32[]{:S(2)}) collective-permute-start(f32[64,128]{1,0:T(8,128)S(1)} %get-tuple-element.33), channel_id=1, source_target_pairs={{0,1},{1,0},{2,3},{3,2},{4,5},{5,4},{6,7},{7,6},{8,9},{9,8},{10,11... | collective-permute-start | bytes 98312 | tf_op jit(solution)/shard_map/ppermute | solution.py:37
  42.8 5.0 %collective-permute-start.13 = (f32[64,128]{1,0:T(8,128)S(1)}, f32[64,128]{1,0:T(8,128)S(1)}, u32[]{:S(2)}, u32[]{:S(2)}) collective-permute-start(f32[64,128]{1,0:T(8,128)S(1)} %add.15), channel_id=1, source_target_pairs={{0,12},{4,8},{8,4},{12,0},{16,28},{20,24},{24,20},{28,16},{1,13},{... | collective-permute-start | bytes 98312 | tf_op jit(solution)/shard_map/ppermute | solution.py:37
  44.2 4.3 %collective-permute-start.12 = (f32[64,128]{1,0:T(8,128)S(1)}, f32[64,128]{1,0:T(8,128)S(1)}, u32[]{:S(2)}, u32[]{:S(2)}) collective-permute-start(f32[64,128]{1,0:T(8,128)S(1)} %add.15), channel_id=1, source_target_pairs={{0,8},{4,12},{8,0},{12,4},{16,24},{20,28},{24,16},{28,20},{1,9},{5... | collective-permute-start | bytes 98312 | tf_op jit(solution)/shard_map/ppermute | solution.py:37
  46.3 3.9 %collective-permute-start.11 = (f32[64,128]{1,0:T(8,128)S(1)}, f32[64,128]{1,0:T(8,128)S(1)}, u32[]{:S(2)}, u32[]{:S(2)}) collective-permute-start(f32[64,128]{1,0:T(8,128)S(1)} %add.15), channel_id=1, source_target_pairs={{0,4},{4,0},{8,12},{12,8},{16,20},{20,16},{24,28},{28,24},{1,5},{5... | collective-permute-start | bytes 98312 | tf_op jit(solution)/shard_map/ppermute | solution.py:37
  50.2 5.8 %collective-permute-start.14 = (f32[64,128]{1,0:T(8,128)S(1)}, f32[64,128]{1,0:T(8,128)S(1)}, u32[]{:S(2)}, u32[]{:S(2)}) collective-permute-start(f32[64,128]{1,0:T(8,128)S(1)} %add_add_fusion), channel_id=1, source_target_pairs={{0,16},{4,20},{8,24},{12,28},{16,0},{20,4},{24,8},{28,12},{1,17},{... | collective-permute-start | bytes 98312 | tf_op jit(solution)/shard_map/ppermute | solution.py:37
  56.0 1.2 %collective-permute-start.15 = (f32[64,128]{1,0:T(8,128)S(1)}, f32[64,128]{1,0:T(8,128)S(1)}, u32[]{:S(2)}, u32[]{:S(2)}) collective-permute-start(f32[64,128]{1,0:T(8,128)S(1)} %add.19.own), channel_id=1, source_target_pairs={{0,1},{1,0},{2,3},{3,2},{4,5},{5,4},{6,7},{7,6},{8,9},{9,8},{10,11... | collective-permute-start | bytes 98312 | tf_op jit(solution)/shard_map/ppermute | solution.py:37

commit v9 on v8

--- a/solution.py
+++ b/solution.py
@@ -11,7 +11,7 @@
 kernel_gain = 16.0
 LANES = 128
 TILE = 512
-PANEL = 16
+PANEL = 8
 VMEM = pl.BlockSpec(memory_space=pltpu.VMEM)
 BF16 = jnp.bfloat16
 F32 = jnp.float32
@@ -184,42 +184,53 @@
         )
 
 
-def eliminate(work, rows):
+def eliminate(work, rows, spread):
     size = work.shape[0]
 
-    def load(start):
-        return [
-            jnp.broadcast_to(work[start + i : start + i + 1, :], (8, 2 * size))
+    def wide(value):
+        return jnp.broadcast_to(value, (PANEL, size))
+
+    def twice(value):
+        return jnp.concatenate([value, value], axis=1)
+
+    here = work[:PANEL, :]
+    for start in range(0, size, PANEL):
+        after, behind = start + PANEL, start + 2 * PANEL
+        place = (start // PANEL % 2) * PANEL * PANEL
+        for k in range(PANEL):
+            lines = slice(place + k * PANEL, place + (k + 1) * PANEL)
+            spread[lines, :] = wide(here[:, start + k : start + k + 1])
+        block = {
+            (i, k): wide(spread[place + k * PANEL + i : place + k * PANEL + i + 1, :])
+            for i in range(PANEL)
+            for k in range(i, PANEL)
+        }
+        lines = [
+            jnp.broadcast_to(work[start + i : start + i + 1, :], (PANEL, 2 * size))
             for i in range(PANEL)
         ]
-
-    def twice(value):
-        return jnp.concatenate([value, value], axis=1)
-
-    lines = load(0)
-    for start in range(0, size, PANEL):
-        ahead = load(start + PANEL) if start + PANEL < size else []
-
-        def lane(i, k):
-            return jnp.broadcast_to(lines[i][:, start + k : start + k + 1], (8, size))
-
-        block = {(i, k): lane(i, k) for i in range(PANEL) for k in range(i, PANEL)}
+        below, columns = None, []
+        if after < size:
+            below = work[after:behind, :]
+            columns = [wide(below[:, start + k : start + k + 1]) for k in range(PANEL)]
         for j in range(PANEL):
             scale = lax.rsqrt(block[j, j])
-            lines[j] = lines[j] * twice(scale)
-            rows[start + j : start + j + 1, :] = lines[j][:1]
+            line = lines[j] * twice(scale)
+            rows[start + j : start + j + 1, :] = line[:1]
             times = {i: block[j, i] * scale for i in range(j + 1, PANEL)}
             for i, factor in times.items():
-                lines[i] = lines[i] - twice(factor) * lines[j]
+                lines[i] = lines[i] - twice(factor) * line
                 for k in range(i, PANEL):
                     block[i, k] = block[i, k] - factor * times[k]
-            for i in range(len(ahead)):
-                ahead[i] = ahead[i] - twice(lane(j, PANEL + i)) * lines[j]
-        behind = start + 2 * PANEL
+            if columns:
+                factor = columns[j] * scale
+                for k in range(j + 1, PANEL):
+                    columns[k] = columns[k] - factor * times[k]
+                below = below - twice(factor) * line
+        if after < size:
+            work[after:behind, :] = below
         if behind < size:
-            high, mid, low = [
-                part.astype(F32) for part in split3(rows[start : start + PANEL, :])
-            ]
+            high, mid, low = [part.astype(F32) for part in split3(rows[start:after, :])]
             left = jnp.concatenate([high, high, mid, high, low, mid], axis=0)[:, :size]
             right = jnp.concatenate([high, mid, high, low, high, mid], axis=0)
             update = lax.dot_general(
@@ -229,16 +240,16 @@
                 preferred_element_type=F32,
             )
             work[behind:, :] = work[behind:, :] - update[behind:, :]
-        lines = ahead
-
-
-def finish_kernel(points, own, theirs, parts, out, work, rows, result, sems):
+        here = below
+
+
+def finish_kernel(points, own, theirs, parts, out, work, rows, spread, result, sems):
     some, size = own.shape
     begin = lax.rem(lax.axis_index("lmk"), 2) * some
     work[pl.ds(pl.multiple_of(begin, some), some), :size] = own[...] / points
     work[pl.ds(pl.multiple_of(some - begin, some), some), :size] = theirs[...] / points
     work[:, size:] = jnp.where(eye(size), 1.0, 0.0)
-    eliminate(work, rows)
+    eliminate(work, rows, spread)
     high, low, _ = split3(rows[:, size:])
     right = jnp.concatenate([high, low, high], axis=1)
     copies = []
@@ -370,6 +381,7 @@
         (part, swap(part, "lmk", num_lmk, 1), parts),
         scratch=[
             *[pltpu.VMEM((size, 2 * size), F32)] * 2,
+            pltpu.VMEM((2 * PANEL * PANEL, size), F32),
             pltpu.VMEM((num_rows, size), F32),
             pltpu.SemaphoreType.DMA((-(-num_rows // TILE),)),
         ],

time: 67.7 us -> 62.2 us (0.919)
  Pallas kernels: 22.7 us -> 17.3 us
    pallas_call x11, Pallas kernels: 21.1 us -> 15.7 us  [call_on(): pl.pallas_call(kernel, out_shape=out, in_specs=[rest.get('in_specs', VMEM...]
  transfers between devices with their start and end apart: 17 -> 17, of which waited for: 12 -> 12; matrix products, arithmetic and copies ran while one was open for 0% -> 0% of each run, Pallas kernels for 16% -> 18%
where the time goes in v9:
time: 62.2 us; the launch traced here: 61.9 us
  starting transfers between devices  23.3 us (37%)
  waiting for transfers between devices  20.1 us (32%)
  Pallas kernels  17.3 us (28%)
  local copies, waits for them, and re-layouts  0.97 us (2%)
    ppermute x17, starting transfers between devices, swap(): return lax.ppermute(value, axis, [(i, i ^ bit) for i in range(size)])  23.3 us
    ppermute x17, waiting for transfers between devices, swap(): return lax.ppermute(value, axis, [(i, i ^ bit) for i in range(size)])  20.1 us
    pallas_call x11, Pallas kernels, call_on(): pl.pallas_call(kernel, out_shape=out, in_specs=[rest.get('in_specs', VMEM...  15.7 us
    pallas_call x1, Pallas kernels, per_device(): pl.pallas_call(beside_kernel, out_shape=joined, in_specs=[pl.BlockSpec(me...  1.64 us
  transfers between devices with their start and end apart: 17, of which 12 were waited for; matrix products, arithmetic and copies ran while one was open for 0% of the time, Pallas kernels for 18%

profile of v9, /device:TPU:0, one launch (start us, length us, event | category | flops | bytes accessed | tf_op | source)
XLA Modules:
  0.0 61.9 jit_solution(12910683773460045537)
XLA Ops:
  0.0 4.0 %collective-permute-start.3 = (bf16[128,128]{1,0:T(8,128)(2,1)}, bf16[128,128]{1,0:T(8,128)(2,1)S(1)}, u32[]{:S(2)}, u32[]{:S(2)}) collective-permute-start(bf16[128,128]{1,0:T(8,128)(2,1)} %right.1), channel_id=1, source_target_pairs={{0,16},{4,20},{8,24},{12,28},{16,0},{20,4},{24,8},{28,12},{1,17},{... | collective-permute-start | bytes 98312 | tf_op jit(solution)/shard_map/ppermute | solution.py:37
  4.0 0.0 collective-permute-start.2
  4.1 1.6 %shard_map.37.block = bf16[128,896]{1,0:T(8,128)(2,1)} custom-call(bf16[128,768]{1,0:T(8,128)(2,1)} %left.1, bf16[128,128]{1,0:T(8,128)(2,1)} %right.1), custom_call_target="tpu_custom_call" | custom-call | tf_op jit(solution)/shard_map/pallas_call | solution.py:284
  5.7 1.9 %collective-permute-start.1 = (bf16[128,896]{1,0:T(8,128)(2,1)}, bf16[128,896]{1,0:T(8,128)(2,1)S(1)}, u32[]{:S(2)}, u32[]{:S(2)}) collective-permute-start(bf16[128,896]{1,0:T(8,128)(2,1)} %shard_map.37.block), channel_id=1, source_target_pairs={{0,8},{4,12},{8,0},{12,4},{16,24},{20,28},{24,16},{28,20},{1,9},{5... | collective-permute-start | bytes 688136 | tf_op jit(solution)/shard_map/ppermute | solution.py:37
  7.7 1.5 %collective-permute-start = (bf16[128,896]{1,0:T(8,128)(2,1)}, bf16[128,896]{1,0:T(8,128)(2,1)S(1)}, u32[]{:S(2)}, u32[]{:S(2)}) collective-permute-start(bf16[128,896]{1,0:T(8,128)(2,1)} %shard_map.37.block), channel_id=1, source_target_pairs={{0,4},{4,0},{8,12},{12,8},{16,20},{20,16},{24,28},{28,24},{1,5},{5... | collective-permute-start | bytes 688136 | tf_op jit(solution)/shard_map/ppermute | solution.py:37
  9.2 0.0 copy-start
  9.2 1.0 %copy-done = bf16[128,896]{1,0:T(8,128)(2,1)S(1)} copy-done((bf16[128,896]{1,0:T(8,128)(2,1)S(1)}, bf16[128,896]{1,0:T(8,128)(2,1)}, u32[]{:S(2)}) %copy-start) | copy-done | bytes 229400
  10.1 3.1 %shard_map.38 = (bf16[1536,768]{1,0:T(8,128)(2,1)S(1)}, f32[1536,256]{1,0:T(8,128)S(1)}) custom-call(bf16[1536,768]{1,0:T(8,128)(2,1)} %points.1, bf16[128,896]{1,0:T(8,128)(2,1)S(1)} %copy-done), custom_call_target="tpu_custom_call" | custom-call | flops 6442450944 | bytes 1048576 | tf_op jit(solution)/shard_map/pallas_call | solution.py:47
  13.2 0.0 collective-permute-done.3.right
  13.2 2.8 %collective-permute-done.2.left = bf16[128,768]{1,0:T(8,128)(2,1)S(1)} collective-permute-done((bf16[128,768]{1,0:T(8,128)(2,1)}, bf16[128,768]{1,0:T(8,128)(2,1)S(1)}, u32[]{:S(2)}, u32[]{:S(2)}) %collective-permute-start.2) | collective-permute-done | bytes 196640 | tf_op jit(solution)/shard_map/ppermute | solution.py:37
  16.0 0.6 collective-permute-done.1.refs_1_
  16.6 0.0 collective-permute-done.refs_2_
  16.6 0.1 collective-permute-start.5
  16.7 1.6 %collective-permute-start.4 = (bf16[128,896]{1,0:T(8,128)(2,1)S(1)}, bf16[128,896]{1,0:T(8,128)(2,1)S(1)}, u32[]{:S(2)}, u32[]{:S(2)}) collective-permute-start(bf16[128,896]{1,0:T(8,128)(2,1)S(1)} %shard_map.39.refs_0_), channel_id=1, source_target_pairs={{0,4},{4,0},{8,12},{12,8},{16,20},{20,16},{24,28},{28,24},{1,5},{5... | collective-permute-start | bytes 688136 | tf_op jit(solution)/shard_map/ppermute | solution.py:37
  18.3 2.3 %shard_map.40.refs_2_ = f32[1536,256]{1,0:T(8,128)S(1)} custom-call(bf16[1536,768]{1,0:T(8,128)(2,1)S(1)} %get-tuple-element.20.unit, bf16[128,896]{1,0:T(8,128)(2,1)S(1)} %shard_map.39.refs_0_, bf16[128,896]{1,0:T(8,128)(2,1)S(1)} %collective-permute-done.1.refs_1_, ...), custom_call_target="tpu_custom_call", output_to_operand_aliasing={{}: (4, {})} | custom-call | flops 4831838208 | bytes 1048576 | tf_op jit(solution)/shard_map/pallas_call | solution.py:47
  20.6 2.0 %collective-permute-start.7 = (bf16[128,896]{1,0:T(8,128)(2,1)S(1)}, bf16[128,896]{1,0:T(8,128)(2,1)S(1)}, u32[]{:S(2)}, u32[]{:S(2)}) collective-permute-start(bf16[128,896]{1,0:T(8,128)(2,1)S(1)} %collective-permute-done.refs_2_), channel_id=1, source_target_pairs={{0,8},{4,12},{8,0},{12,4},{16,24},{20,28},{24,16},{28,20},{1,9},{5... | collective-permute-start | bytes 688136 | tf_op jit(solution)/shard_map/ppermute | solution.py:37
  22.6 1.2 %collective-permute-done.5.refs_0_ = bf16[128,896]{1,0:T(8,128)(2,1)S(1)} collective-permute-done((bf16[128,896]{1,0:T(8,128)(2,1)S(1)}, bf16[128,896]{1,0:T(8,128)(2,1)S(1)}, u32[]{:S(2)}, u32[]{:S(2)}) %collective-permute-start.5) | collective-permute-done | bytes 229408 | tf_op jit(solution)/shard_map/ppermute | solution.py:37
  23.8 0.0 collective-permute-done.4.refs_1_
  23.8 2.6 %collective-permute-start.6 = (bf16[128,896]{1,0:T(8,128)(2,1)S(1)}, bf16[128,896]{1,0:T(8,128)(2,1)S(1)}, u32[]{:S(2)}, u32[]{:S(2)}) collective-permute-start(bf16[128,896]{1,0:T(8,128)(2,1)S(1)} %collective-permute-done.5.refs_0_), channel_id=1, source_target_pairs={{0,4},{4,0},{8,12},{12,8},{16,20},{20,16},{24,28},{28,24},{1,5},{5... | collective-permute-start | bytes 688136 | tf_op jit(solution)/shard_map/ppermute | solution.py:37
  26.3 1.7 %shard_map.41.refs_1_ = f32[1536,256]{1,0:T(8,128)S(1)} custom-call(bf16[1536,768]{1,0:T(8,128)(2,1)S(1)} %get-tuple-element.20.unit, bf16[128,896]{1,0:T(8,128)(2,1)S(1)} %collective-permute-done.5.refs_0_, bf16[128,896]{1,0:T(8,128)(2,1)S(1)} %collective-permute-done.4.refs_1_, f32[1536,256]{1,0:T(8,128)S(1)} %shard_map.40.refs_2_), custom_call_target="tpu_custom_call", output_to_operand_aliasing={{}: (3, {})} | custom-call | flops 3221225472 | bytes 1048576 | tf_op jit(solution)/shard_map/pallas_call | solution.py:47
  28.0 0.0 collective-permute-done.7.refs_0_
  28.1 1.3 %shard_map.42.refs_1_ = f32[1536,256]{1,0:T(8,128)S(1)} custom-call(bf16[1536,768]{1,0:T(8,128)(2,1)S(1)} %get-tuple-element.20.unit, bf16[128,896]{1,0:T(8,128)(2,1)S(1)} %collective-permute-done.7.refs_0_, f32[1536,256]{1,0:T(8,128)S(1)} %shard_map.41.refs_1_), custom_call_target="tpu_custom_call", output_to_operand_aliasing={{}: (2, {})} | custom-call | flops 1610612736 | bytes 1048576 | tf_op jit(solution)/shard_map/pallas_call | solution.py:47
  29.3 1.0 %collective-permute-done.6.refs_0_ = bf16[128,896]{1,0:T(8,128)(2,1)S(1)} collective-permute-done((bf16[128,896]{1,0:T(8,128)(2,1)S(1)}, bf16[128,896]{1,0:T(8,128)(2,1)S(1)}, u32[]{:S(2)}, u32[]{:S(2)}) %collective-permute-start.6) | collective-permute-done | bytes 229408 | tf_op jit(solution)/shard_map/ppermute | solution.py:37
  30.3 0.9 %shard_map.44 = f32[776,128]{1,0:T(8,128)S(1)} custom-call(bf16[1536,768]{1,0:T(8,128)(2,1)S(1)} %get-tuple-element.20.unit, bf16[128,896]{1,0:T(8,128)(2,1)S(1)} %collective-permute-done.6.refs_0_, f32[1536,256]{1,0:T(8,128)S(1)} %shard_map.42.refs_1_), custom_call_target="tpu_custom_call" | custom-call | flops 805306368 | bytes 1048576 | tf_op jit(solution)/shard_map/pallas_call | solution.py:47
  31.2 0.1 collective-permute-start.8
  31.3 0.9 %shard_map.43.mine = f32[776,128]{1,0:T(8,128)S(1)} custom-call(bf16[1536,768]{1,0:T(8,128)(2,1)S(1)} %get-tuple-element.20.unit, bf16[128,896]{1,0:T(8,128)(2,1)S(1)} %collective-permute-done.6.refs_0_, f32[1536,256]{1,0:T(8,128)S(1)} %shard_map.42.refs_1_), custom_call_target="tpu_custom_call" | custom-call | flops 805306368 | bytes 1048576 | tf_op jit(solution)/shard_map/pallas_call | solution.py:47
  32.2 0.8 %collective-permute-done.8.other = f32[776,128]{1,0:T(8,128)S(1)} collective-permute-done((f32[776,128]{1,0:T(8,128)S(1)}, f32[776,128]{1,0:T(8,128)S(1)}, u32[]{:S(2)}, u32[]{:S(2)}) %collective-permute-start.8) | collective-permute-done | bytes 397344 | tf_op jit(solution)/shard_map/ppermute | solution.py:37
  33.1 1.6 %collective-permute-start.9 = (bf16[800,128]{1,0:T(8,128)(2,1)S(1)}, bf16[800,128]{1,0:T(8,128)(2,1)S(1)}, u32[]{:S(2)}, u32[]{:S(2)}) collective-permute-start(bf16[800,128]{1,0:T(8,128)(2,1)S(1)} %shard_map.45.mine), channel_id=1, source_target_pairs={{0,2},{1,3},{2,0},{3,1},{4,6},{5,7},{6,4},{7,5},{8,10},{9,11},{10,... | collective-permute-start | bytes 614408 | tf_op jit(solution)/shard_map/ppermute | solution.py:37
  34.6 5.6 %collective-permute-done.9.other = bf16[800,128]{1,0:T(8,128)(2,1)S(1)} collective-permute-done((bf16[800,128]{1,0:T(8,128)(2,1)S(1)}, bf16[800,128]{1,0:T(8,128)(2,1)S(1)}, u32[]{:S(2)}, u32[]{:S(2)}) %collective-permute-start.9) | collective-permute-done | bytes 204832 | tf_op jit(solution)/shard_map/ppermute | solution.py:37
  40.2 0.7 %shard_map.46 = (f32[768,128]{1,0:T(8,128)S(1)}, f32[64,128]{1,0:T(8,128)S(1)}, f32[64,128]{1,0:T(8,128)S(1)}) custom-call(bf16[800,128]{1,0:T(8,128)(2,1)S(1)} %shard_map.45.mine, bf16[800,128]{1,0:T(8,128)(2,1)S(1)} %collective-permute-done.9.other), custom_call_target="tpu_custom_call" | custom-call | bytes 1048576 | tf_op jit(solution)/shard_map/pallas_call | solution.py:47
  41.0 0.1 collective-permute-start.16
  41.0 0.5 collective-permute-start.10
  41.5 1.3 %collective-permute-done.10 = f32[64,128]{1,0:T(8,128)S(1)} collective-permute-done((f32[64,128]{1,0:T(8,128)S(1)}, f32[64,128]{1,0:T(8,128)S(1)}, u32[]{:S(2)}, u32[]{:S(2)}) %collective-permute-start.10) | collective-permute-done | bytes 32800 | tf_op jit(solution)/shard_map/ppermute | solution.py:37
  42.8 1.4 %collective-permute-start.13 = (f32[64,128]{1,0:T(8,128)S(1)}, f32[64,128]{1,0:T(8,128)S(1)}, u32[]{:S(2)}, u32[]{:S(2)}) collective-permute-start(f32[64,128]{1,0:T(8,128)S(1)} %add.15), channel_id=1, source_target_pairs={{0,12},{4,8},{8,4},{12,0},{16,28},{20,24},{24,20},{28,16},{1,13},{... | collective-permute-start | bytes 98312 | tf_op jit(solution)/shard_map/ppermute | solution.py:37
  44.2 2.1 %collective-permute-start.12 = (f32[64,128]{1,0:T(8,128)S(1)}, f32[64,128]{1,0:T(8,128)S(1)}, u32[]{:S(2)}, u32[]{:S(2)}) collective-permute-start(f32[64,128]{1,0:T(8,128)S(1)} %add.15), channel_id=1, source_target_pairs={{0,8},{4,12},{8,0},{12,4},{16,24},{20,28},{24,16},{28,20},{1,9},{5... | collective-permute-start | bytes 98312 | tf_op jit(solution)/shard_map/ppermute | solution.py:37
  46.3 0.0 collective-permute-start.11
  46.3 1.5 %collective-permute-done.13 = f32[64,128]{1,0:T(8,128)S(1)} collective-permute-done((f32[64,128]{1,0:T(8,128)S(1)}, f32[64,128]{1,0:T(8,128)S(1)}, u32[]{:S(2)}, u32[]{:S(2)}) %collective-permute-start.13) | collective-permute-done | bytes 32800 | tf_op jit(solution)/shard_map/ppermute | solution.py:37
  47.7 0.8 %collective-permute-done.12 = f32[64,128]{1,0:T(8,128)S(1)} collective-permute-done((f32[64,128]{1,0:T(8,128)S(1)}, f32[64,128]{1,0:T(8,128)S(1)}, u32[]{:S(2)}, u32[]{:S(2)}) %collective-permute-start.12) | collective-permute-done | bytes 32800 | tf_op jit(solution)/shard_map/ppermute | solution.py:37
  48.5 1.7 %collective-permute-done.11 = f32[64,128]{1,0:T(8,128)S(1)} collective-permute-done((f32[64,128]{1,0:T(8,128)S(1)}, f32[64,128]{1,0:T(8,128)S(1)}, u32[]{:S(2)}, u32[]{:S(2)}) %collective-permute-start.11) | collective-permute-done | bytes 32800 | tf_op jit(solution)/shard_map/ppermute | solution.py:37
  50.2 3.9 %collective-permute-start.14 = (f32[64,128]{1,0:T(8,128)S(1)}, f32[64,128]{1,0:T(8,128)S(1)}, u32[]{:S(2)}, u32[]{:S(2)}) collective-permute-start(f32[64,128]{1,0:T(8,128)S(1)} %add_add_fusion), channel_id=1, source_target_pairs={{0,16},{4,20},{8,24},{12,28},{16,0},{20,4},{24,8},{28,12},{1,17},{... | collective-permute-start | bytes 98312 | tf_op jit(solution)/shard_map/ppermute | solution.py:37
  54.1 1.9 %collective-permute-done.14 = f32[64,128]{1,0:T(8,128)S(1)} collective-permute-done((f32[64,128]{1,0:T(8,128)S(1)}, f32[64,128]{1,0:T(8,128)S(1)}, u32[]{:S(2)}, u32[]{:S(2)}) %collective-permute-start.14) | collective-permute-done | bytes 32800 | tf_op jit(solution)/shard_map/ppermute | solution.py:37
  56.0 0.0 collective-permute-start.15
  56.0 0.0 collective-permute-done.16.theirs
  56.0 0.1 shard_map.47.parts
  56.2 1.0 %collective-permute-done.15.theirs = f32[64,128]{1,0:T(8,128)S(1)} collective-permute-done((f32[64,128]{1,0:T(8,128)S(1)}, f32[64,128]{1,0:T(8,128)S(1)}, u32[]{:S(2)}, u32[]{:S(2)}) %collective-permute-start.15) | collective-permute-done | bytes 32800 | tf_op jit(solution)/shard_map/ppermute | solution.py:37
  57.2 4.7 %shard_map.48 = f32[1536,128]{1,0:T(8,128)} custom-call(f32[64,128]{1,0:T(8,128)S(1)} %add.19.own, f32[64,128]{1,0:T(8,128)S(1)} %collective-permute-done.15.theirs, bf16[1536,384]{1,0:T(8,128)(2,1)S(1)} %shard_map.47.parts), custom_call_target="tpu_custom_call" | custom-call | bytes 1048576 | tf_op jit(solution)/shard_map/pallas_call | solution.py:47
  (5 shorter events, 0.1 us)
Async XLA Ops:
  0.0 13.2 %collective-permute-start.3 = (bf16[128,128]{1,0:T(8,128)(2,1)}, bf16[128,128]{1,0:T(8,128)(2,1)S(1)}, u32[]{:S(2)}, u32[]{:S(2)}) collective-permute-start(bf16[128,128]{1,0:T(8,128)(2,1)} %right.1), channel_id=1, source_target_pairs={{0,16},{4,20},{8,24},{12,28},{16,0},{20,4},{24,8},{28,12},{1,17},{... | collective-permute-start | bytes 98312 | tf_op jit(solution)/shard_map/ppermute | solution.py:37
  4.0 12.0 %collective-permute-start.2 = (bf16[128,768]{1,0:T(8,128)(2,1)}, bf16[128,768]{1,0:T(8,128)(2,1)S(1)}, u32[]{:S(2)}, u32[]{:S(2)}) collective-permute-start(bf16[128,768]{1,0:T(8,128)(2,1)} %left.1), channel_id=1, source_target_pairs={{0,16},{4,20},{8,24},{12,28},{16,0},{20,4},{24,8},{28,12},{1,17},{... | collective-permute-start | bytes 589832 | tf_op jit(solution)/shard_map/ppermute | solution.py:37
  5.7 10.9 %collective-permute-start.1 = (bf16[128,896]{1,0:T(8,128)(2,1)}, bf16[128,896]{1,0:T(8,128)(2,1)S(1)}, u32[]{:S(2)}, u32[]{:S(2)}) collective-permute-start(bf16[128,896]{1,0:T(8,128)(2,1)} %shard_map.37.block), channel_id=1, source_target_pairs={{0,8},{4,12},{8,0},{12,4},{16,24},{20,28},{24,16},{28,20},{1,9},{5... | collective-permute-start | bytes 688136 | tf_op jit(solution)/shard_map/ppermute | solution.py:37
  7.7 9.0 %collective-permute-start = (bf16[128,896]{1,0:T(8,128)(2,1)}, bf16[128,896]{1,0:T(8,128)(2,1)S(1)}, u32[]{:S(2)}, u32[]{:S(2)}) collective-permute-start(bf16[128,896]{1,0:T(8,128)(2,1)} %shard_map.37.block), channel_id=1, source_target_pairs={{0,4},{4,0},{8,12},{12,8},{16,20},{20,16},{24,28},{28,24},{1,5},{5... | collective-permute-start | bytes 688136 | tf_op jit(solution)/shard_map/ppermute | solution.py:37
  9.2 1.0 %copy-start = (bf16[128,896]{1,0:T(8,128)(2,1)S(1)}, bf16[128,896]{1,0:T(8,128)(2,1)}, u32[]{:S(2)}) copy-start(bf16[128,896]{1,0:T(8,128)(2,1)} %shard_map.37.block) | copy-start | bytes 688132
  16.6 7.1 %collective-permute-start.5 = (bf16[128,896]{1,0:T(8,128)(2,1)S(1)}, bf16[128,896]{1,0:T(8,128)(2,1)S(1)}, u32[]{:S(2)}, u32[]{:S(2)}) collective-permute-start(bf16[128,896]{1,0:T(8,128)(2,1)S(1)} %shard_map.39.refs_0_), channel_id=1, source_target_pairs={{0,8},{4,12},{8,0},{12,4},{16,24},{20,28},{24,16},{28,20},{1,9},{5... | collective-permute-start | bytes 688136 | tf_op jit(solution)/shard_map/ppermute | solution.py:37
  16.7 7.0 %collective-permute-start.4 = (bf16[128,896]{1,0:T(8,128)(2,1)S(1)}, bf16[128,896]{1,0:T(8,128)(2,1)S(1)}, u32[]{:S(2)}, u32[]{:S(2)}) collective-permute-start(bf16[128,896]{1,0:T(8,128)(2,1)S(1)} %shard_map.39.refs_0_), channel_id=1, source_target_pairs={{0,4},{4,0},{8,12},{12,8},{16,20},{20,16},{24,28},{28,24},{1,5},{5... | collective-permute-start | bytes 688136 | tf_op jit(solution)/shard_map/ppermute | solution.py:37
  20.6 7.5 %collective-permute-start.7 = (bf16[128,896]{1,0:T(8,128)(2,1)S(1)}, bf16[128,896]{1,0:T(8,128)(2,1)S(1)}, u32[]{:S(2)}, u32[]{:S(2)}) collective-permute-start(bf16[128,896]{1,0:T(8,128)(2,1)S(1)} %collective-permute-done.refs_2_), channel_id=1, source_target_pairs={{0,8},{4,12},{8,0},{12,4},{16,24},{20,28},{24,16},{28,20},{1,9},{5... | collective-permute-start | bytes 688136 | tf_op jit(solution)/shard_map/ppermute | solution.py:37
  23.8 6.6 %collective-permute-start.6 = (bf16[128,896]{1,0:T(8,128)(2,1)S(1)}, bf16[128,896]{1,0:T(8,128)(2,1)S(1)}, u32[]{:S(2)}, u32[]{:S(2)}) collective-permute-start(bf16[128,896]{1,0:T(8,128)(2,1)S(1)} %collective-permute-done.5.refs_0_), channel_id=1, source_target_pairs={{0,4},{4,0},{8,12},{12,8},{16,20},{20,16},{24,28},{28,24},{1,5},{5... | collective-permute-start | bytes 688136 | tf_op jit(solution)/shard_map/ppermute | solution.py:37
  31.2 1.8 %collective-permute-start.8 = (f32[776,128]{1,0:T(8,128)S(1)}, f32[776,128]{1,0:T(8,128)S(1)}, u32[]{:S(2)}, u32[]{:S(2)}) collective-permute-start(f32[776,128]{1,0:T(8,128)S(1)} %shard_map.44), channel_id=1, source_target_pairs={{0,1},{1,0},{2,3},{3,2},{4,5},{5,4},{6,7},{7,6},{8,9},{9,8},{10,11... | collective-permute-start | bytes 1191944 | tf_op jit(solution)/shard_map/ppermute | solution.py:37
  33.1 7.2 %collective-permute-start.9 = (bf16[800,128]{1,0:T(8,128)(2,1)S(1)}, bf16[800,128]{1,0:T(8,128)(2,1)S(1)}, u32[]{:S(2)}, u32[]{:S(2)}) collective-permute-start(bf16[800,128]{1,0:T(8,128)(2,1)S(1)} %shard_map.45.mine), channel_id=1, source_target_pairs={{0,2},{1,3},{2,0},{3,1},{4,6},{5,7},{6,4},{7,5},{8,10},{9,11},{10,... | collective-permute-start | bytes 614408 | tf_op jit(solution)/shard_map/ppermute | solution.py:37
  41.0 15.1 %collective-permute-start.16 = (f32[768,128]{1,0:T(8,128)S(1)}, f32[768,128]{1,0:T(8,128)S(1)}, u32[]{:S(2)}, u32[]{:S(2)}) collective-permute-start(f32[768,128]{1,0:T(8,128)S(1)} %get-tuple-element.34.own), channel_id=1, source_target_pairs={{0,1},{1,0},{2,3},{3,2},{4,5},{5,4},{6,7},{7,6},{8,9},{9,8},{10,11... | collective-permute-start | bytes 1179656 | tf_op jit(solution)/shard_map/ppermute | solution.py:37
  41.0 1.8 %collective-permute-start.10 = (f32[64,128]{1,0:T(8,128)S(1)}, f32[64,128]{1,0:T(8,128)S(1)}, u32[]{:S(2)}, u32[]{:S(2)}) collective-permute-start(f32[64,128]{1,0:T(8,128)S(1)} %get-tuple-element.33), channel_id=1, source_target_pairs={{0,1},{1,0},{2,3},{3,2},{4,5},{5,4},{6,7},{7,6},{8,9},{9,8},{10,11... | collective-permute-start | bytes 98312 | tf_op jit(solution)/shard_map/ppermute | solution.py:37
  42.8 5.0 %collective-permute-start.13 = (f32[64,128]{1,0:T(8,128)S(1)}, f32[64,128]{1,0:T(8,128)S(1)}, u32[]{:S(2)}, u32[]{:S(2)}) collective-permute-start(f32[64,128]{1,0:T(8,128)S(1)} %add.15), channel_id=1, source_target_pairs={{0,12},{4,8},{8,4},{12,0},{16,28},{20,24},{24,20},{28,16},{1,13},{... | collective-permute-start | bytes 98312 | tf_op jit(solution)/shard_map/ppermute | solution.py:37
  44.2 4.3 %collective-permute-start.12 = (f32[64,128]{1,0:T(8,128)S(1)}, f32[64,128]{1,0:T(8,128)S(1)}, u32[]{:S(2)}, u32[]{:S(2)}) collective-permute-start(f32[64,128]{1,0:T(8,128)S(1)} %add.15), channel_id=1, source_target_pairs={{0,8},{4,12},{8,0},{12,4},{16,24},{20,28},{24,16},{28,20},{1,9},{5... | collective-permute-start | bytes 98312 | tf_op jit(solution)/shard_map/ppermute | solution.py:37
  46.3 3.9 %collective-permute-start.11 = (f32[64,128]{1,0:T(8,128)S(1)}, f32[64,128]{1,0:T(8,128)S(1)}, u32[]{:S(2)}, u32[]{:S(2)}) collective-permute-start(f32[64,128]{1,0:T(8,128)S(1)} %add.15), channel_id=1, source_target_pairs={{0,4},{4,0},{8,12},{12,8},{16,20},{20,16},{24,28},{28,24},{1,5},{5... | collective-permute-start | bytes 98312 | tf_op jit(solution)/shard_map/ppermute | solution.py:37
  50.2 5.8 %collective-permute-start.14 = (f32[64,128]{1,0:T(8,128)S(1)}, f32[64,128]{1,0:T(8,128)S(1)}, u32[]{:S(2)}, u32[]{:S(2)}) collective-permute-start(f32[64,128]{1,0:T(8,128)S(1)} %add_add_fusion), channel_id=1, source_target_pairs={{0,16},{4,20},{8,24},{12,28},{16,0},{20,4},{24,8},{28,12},{1,17},{... | collective-permute-start | bytes 98312 | tf_op jit(solution)/shard_map/ppermute | solution.py:37
  56.0 1.2 %collective-permute-start.15 = (f32[64,128]{1,0:T(8,128)S(1)}, f32[64,128]{1,0:T(8,128)S(1)}, u32[]{:S(2)}, u32[]{:S(2)}) collective-permute-start(f32[64,128]{1,0:T(8,128)S(1)} %add.19.own), channel_id=1, source_target_pairs={{0,1},{1,0},{2,3},{3,2},{4,5},{5,4},{6,7},{7,6},{8,9},{9,8},{10,11... | collective-permute-start | bytes 98312 | tf_op jit(solution)/shard_map/ppermute | solution.py:37

commit v10 on v9

--- a/solution.py
+++ b/solution.py
@@ -56,11 +56,6 @@
         ),
         compiler_params=pltpu.CompilerParams(vmem_limit_bytes=48 << 20),
     )(*operands)
-
-
-def join_kernel(left, right, out):
-    out[:, : left.shape[1]] = left[...]
-    out[:, left.shape[1] :] = right[...]
 
 
 def beside_kernel(left, right, out, sems):
@@ -276,18 +271,15 @@
     lmk_bits = [1 << b for b in range(1, num_lmk.bit_length() - 1)]
     shape = jax.ShapeDtypeStruct
 
-    own = (landmarks, eigvecs)
-    joined = shape((landmarks.shape[0], features + size), BF16)
-    held = {}
-    if num_pts == 8:
-        held[4] = [swap(value, "pts", num_pts, 4) for value in own]
-    held[0] = pl.pallas_call(
-        beside_kernel,
-        out_shape=joined,
-        in_specs=[pl.BlockSpec(memory_space=pltpu.HBM)] * 2,
-        out_specs=VMEM,
-        scratch_shapes=[pltpu.SemaphoreType.DMA((1 + landmarks.shape[0] // 16,))],
-    )(*own)
+    held = {
+        0: pl.pallas_call(
+            beside_kernel,
+            out_shape=shape((landmarks.shape[0], features + size), BF16),
+            in_specs=[pl.BlockSpec(memory_space=pltpu.HBM)] * 2,
+            out_specs=VMEM,
+            scratch_shapes=[pltpu.SemaphoreType.DMA((1 + landmarks.shape[0] // 16,))],
+        )(landmarks, eigvecs)
+    }
     if num_pts == 8:
         rounds = [[(0, 4), (0, 2), (0, 1)], [(4, 2), (4, 1)], [(6, 1)]]
         late = (1, 2)
@@ -311,15 +303,13 @@
     ready, unit, total = [0], None, None
     for turn, hops in enumerate(rounds):
         for mask, bit in hops:
-            if mask ^ bit in held:
-                continue
             held[mask ^ bit] = swap(held[mask], "pts", num_pts, bit)
         if unit is None:
             unit, total = call_on(
                 first_kernel,
                 (shape((num_rows, features), BF16), shape((num_rows, 2 * size), F32)),
                 (points, held[0]),
-                flops=flops * 4,
+                flops=flops,
             )
         else:
             total = more(total, ready)
@@ -333,8 +323,6 @@
             tied = list(dict.fromkeys(ready + sources))[::-1]
             *fresh, total = lax.optimization_barrier((*[held[mask] for mask in tied], total))
             held.update(zip(tied, fresh))
-            if turn == 0 and late:
-                held[4] = call_on(join_kernel, joined, held[4])
     if late:
         total = more(total, [late[0] ^ late[1]])
     group = ready

time: 62.2 us -> 61.7 us (level)
  starting transfers between devices: 23.3 us -> 21.8 us
  waiting for transfers between devices: 20.1 us -> 21.2 us
    ppermute x17 -> x16, starting transfers between devices: 23.3 us -> 21.8 us  [swap(): return lax.ppermute(value, axis, [(i, i ^ bit) for i in range(size)])]
    ppermute x17 -> x16, waiting for transfers between devices: 20.1 us -> 21.2 us  [swap(): return lax.ppermute(value, axis, [(i, i ^ bit) for i in range(size)])]
    pallas_call x11 -> x10, Pallas kernels: 15.7 us -> 15.6 us  [call_on(): pl.pallas_call(kernel, out_shape=out, in_specs=[rest.get('in_specs', VMEM...]
  transfers between devices with their start and end apart: 17 -> 16, of which waited for: 12 -> 13; matrix products, arithmetic and copies ran while one was open for 0% -> 0% of each run, Pallas kernels for 18% -> 15%
where the time goes in v10:
time: 61.7 us; the launch traced here: 61.4 us
  starting transfers between devices  21.8 us (35%)
  waiting for transfers between devices  21.2 us (34%)
  Pallas kernels  17.3 us (28%)
  local copies, waits for them, and re-layouts  0.97 us (2%)
    ppermute x16, starting transfers between devices, swap(): return lax.ppermute(value, axis, [(i, i ^ bit) for i in range(size)])  21.8 us
    ppermute x16, waiting for transfers between devices, swap(): return lax.ppermute(value, axis, [(i, i ^ bit) for i in range(size)])  21.2 us
    pallas_call x10, Pallas kernels, call_on(): pl.pallas_call(kernel, out_shape=out, in_specs=[rest.get('in_specs', VMEM...  15.6 us
    pallas_call x1, Pallas kernels, per_device(): pl.pallas_call(beside_kernel, out_shape=shape((landmarks.shape[0], featur...  1.64 us
  transfers between devices with their start and end apart: 16, of which 13 were waited for; matrix products, arithmetic and copies ran while one was open for 0% of the time, Pallas kernels for 15%

profile of v10, /device:TPU:0, one launch (start us, length us, event | category | flops | bytes accessed | tf_op | source)
XLA Modules:
  0.0 61.4 jit_solution(14824804289419273710)
XLA Ops:
  0.0 1.6 %shard_map.37.block = bf16[128,896]{1,0:T(8,128)(2,1)} custom-call(bf16[128,768]{1,0:T(8,128)(2,1)} %left.1, bf16[128,128]{1,0:T(8,128)(2,1)} %right.1), custom_call_target="tpu_custom_call" | custom-call | tf_op jit(solution)/shard_map/pallas_call | solution.py:275
  1.7 4.1 %collective-permute-start.2 = (bf16[128,896]{1,0:T(8,128)(2,1)}, bf16[128,896]{1,0:T(8,128)(2,1)S(1)}, u32[]{:S(2)}, u32[]{:S(2)}) collective-permute-start(bf16[128,896]{1,0:T(8,128)(2,1)} %shard_map.37.block), channel_id=1, source_target_pairs={{0,16},{4,20},{8,24},{12,28},{16,0},{20,4},{24,8},{28,12},{1,17},{... | collective-permute-start | bytes 688136 | tf_op jit(solution)/shard_map/ppermute | solution.py:37
  5.8 1.6 %collective-permute-start.1 = (bf16[128,896]{1,0:T(8,128)(2,1)}, bf16[128,896]{1,0:T(8,128)(2,1)S(1)}, u32[]{:S(2)}, u32[]{:S(2)}) collective-permute-start(bf16[128,896]{1,0:T(8,128)(2,1)} %shard_map.37.block), channel_id=1, source_target_pairs={{0,8},{4,12},{8,0},{12,4},{16,24},{20,28},{24,16},{28,20},{1,9},{5... | collective-permute-start | bytes 688136 | tf_op jit(solution)/shard_map/ppermute | solution.py:37
  7.3 1.5 %collective-permute-start = (bf16[128,896]{1,0:T(8,128)(2,1)}, bf16[128,896]{1,0:T(8,128)(2,1)S(1)}, u32[]{:S(2)}, u32[]{:S(2)}) collective-permute-start(bf16[128,896]{1,0:T(8,128)(2,1)} %shard_map.37.block), channel_id=1, source_target_pairs={{0,4},{4,0},{8,12},{12,8},{16,20},{20,16},{24,28},{28,24},{1,5},{5... | collective-permute-start | bytes 688136 | tf_op jit(solution)/shard_map/ppermute | solution.py:37
  8.8 0.0 copy-start
  8.8 1.0 %copy-done = bf16[128,896]{1,0:T(8,128)(2,1)S(1)} copy-done((bf16[128,896]{1,0:T(8,128)(2,1)S(1)}, bf16[128,896]{1,0:T(8,128)(2,1)}, u32[]{:S(2)}) %copy-start) | copy-done | bytes 229400
  9.8 3.1 %shard_map.38 = (bf16[1536,768]{1,0:T(8,128)(2,1)S(1)}, f32[1536,256]{1,0:T(8,128)S(1)}) custom-call(bf16[1536,768]{1,0:T(8,128)(2,1)} %points.1, bf16[128,896]{1,0:T(8,128)(2,1)S(1)} %copy-done), custom_call_target="tpu_custom_call" | custom-call | flops 1610612736 | bytes 1048576 | tf_op jit(solution)/shard_map/pallas_call | solution.py:47
  12.9 3.7 %collective-permute-done.2.refs_0_ = bf16[128,896]{1,0:T(8,128)(2,1)S(1)} collective-permute-done((bf16[128,896]{1,0:T(8,128)(2,1)}, bf16[128,896]{1,0:T(8,128)(2,1)S(1)}, u32[]{:S(2)}, u32[]{:S(2)}) %collective-permute-start.2) | collective-permute-done | bytes 229408 | tf_op jit(solution)/shard_map/ppermute | solution.py:37
  16.6 0.2 collective-permute-done.1.refs_1_
  16.8 0.0 collective-permute-done.refs_2_
  16.8 1.5 %collective-permute-start.4 = (bf16[128,896]{1,0:T(8,128)(2,1)S(1)}, bf16[128,896]{1,0:T(8,128)(2,1)S(1)}, u32[]{:S(2)}, u32[]{:S(2)}) collective-permute-start(bf16[128,896]{1,0:T(8,128)(2,1)S(1)} %collective-permute-done.2.refs_0_), channel_id=1, source_target_pairs={{0,8},{4,12},{8,0},{12,4},{16,24},{20,28},{24,16},{28,20},{1,9},{5... | collective-permute-start | bytes 688136 | tf_op jit(solution)/shard_map/ppermute | solution.py:37
  18.3 1.5 %collective-permute-start.3 = (bf16[128,896]{1,0:T(8,128)(2,1)S(1)}, bf16[128,896]{1,0:T(8,128)(2,1)S(1)}, u32[]{:S(2)}, u32[]{:S(2)}) collective-permute-start(bf16[128,896]{1,0:T(8,128)(2,1)S(1)} %collective-permute-done.2.refs_0_), channel_id=1, source_target_pairs={{0,4},{4,0},{8,12},{12,8},{16,20},{20,16},{24,28},{28,24},{1,5},{5... | collective-permute-start | bytes 688136 | tf_op jit(solution)/shard_map/ppermute | solution.py:37
  19.8 2.3 %shard_map.39.refs_2_ = f32[1536,256]{1,0:T(8,128)S(1)} custom-call(bf16[1536,768]{1,0:T(8,128)(2,1)S(1)} %get-tuple-element.19.unit, bf16[128,896]{1,0:T(8,128)(2,1)S(1)} %collective-permute-done.2.refs_0_, bf16[128,896]{1,0:T(8,128)(2,1)S(1)} %collective-permute-done.1.refs_1_, ...), custom_call_target="tpu_custom_call", output_to_operand_aliasing={{}: (4, {})} | custom-call | flops 4831838208 | bytes 1048576 | tf_op jit(solution)/shard_map/pallas_call | solution.py:47
  22.1 0.7 %collective-permute-start.6 = (bf16[128,896]{1,0:T(8,128)(2,1)S(1)}, bf16[128,896]{1,0:T(8,128)(2,1)S(1)}, u32[]{:S(2)}, u32[]{:S(2)}) collective-permute-start(bf16[128,896]{1,0:T(8,128)(2,1)S(1)} %collective-permute-done.refs_2_), channel_id=1, source_target_pairs={{0,8},{4,12},{8,0},{12,4},{16,24},{20,28},{24,16},{28,20},{1,9},{5... | collective-permute-start | bytes 688136 | tf_op jit(solution)/shard_map/ppermute | solution.py:37
  22.7 0.9 %collective-permute-done.4.refs_0_ = bf16[128,896]{1,0:T(8,128)(2,1)S(1)} collective-permute-done((bf16[128,896]{1,0:T(8,128)(2,1)S(1)}, bf16[128,896]{1,0:T(8,128)(2,1)S(1)}, u32[]{:S(2)}, u32[]{:S(2)}) %collective-permute-start.4) | collective-permute-done | bytes 229408 | tf_op jit(solution)/shard_map/ppermute | solution.py:37
  23.6 1.0 %collective-permute-done.3.refs_1_ = bf16[128,896]{1,0:T(8,128)(2,1)S(1)} collective-permute-done((bf16[128,896]{1,0:T(8,128)(2,1)S(1)}, bf16[128,896]{1,0:T(8,128)(2,1)S(1)}, u32[]{:S(2)}, u32[]{:S(2)}) %collective-permute-start.3) | collective-permute-done | bytes 229408 | tf_op jit(solution)/shard_map/ppermute | solution.py:37
  24.6 1.5 %collective-permute-start.5 = (bf16[128,896]{1,0:T(8,128)(2,1)S(1)}, bf16[128,896]{1,0:T(8,128)(2,1)S(1)}, u32[]{:S(2)}, u32[]{:S(2)}) collective-permute-start(bf16[128,896]{1,0:T(8,128)(2,1)S(1)} %collective-permute-done.4.refs_0_), channel_id=1, source_target_pairs={{0,4},{4,0},{8,12},{12,8},{16,20},{20,16},{24,28},{28,24},{1,5},{5... | collective-permute-start | bytes 688136 | tf_op jit(solution)/shard_map/ppermute | solution.py:37
  26.1 1.7 %shard_map.40.refs_1_ = f32[1536,256]{1,0:T(8,128)S(1)} custom-call(bf16[1536,768]{1,0:T(8,128)(2,1)S(1)} %get-tuple-element.19.unit, bf16[128,896]{1,0:T(8,128)(2,1)S(1)} %collective-permute-done.4.refs_0_, bf16[128,896]{1,0:T(8,128)(2,1)S(1)} %collective-permute-done.3.refs_1_, f32[1536,256]{1,0:T(8,128)S(1)} %shard_map.39.refs_2_), custom_call_target="tpu_custom_call", output_to_operand_aliasing={{}: (3, {})} | custom-call | flops 3221225472 | bytes 1048576 | tf_op jit(solution)/shard_map/pallas_call | solution.py:47
  27.8 0.5 collective-permute-done.6.refs_0_
  28.2 1.3 %shard_map.41.refs_1_ = f32[1536,256]{1,0:T(8,128)S(1)} custom-call(bf16[1536,768]{1,0:T(8,128)(2,1)S(1)} %get-tuple-element.19.unit, bf16[128,896]{1,0:T(8,128)(2,1)S(1)} %collective-permute-done.6.refs_0_, f32[1536,256]{1,0:T(8,128)S(1)} %shard_map.40.refs_1_), custom_call_target="tpu_custom_call", output_to_operand_aliasing={{}: (2, {})} | custom-call | flops 1610612736 | bytes 1048576 | tf_op jit(solution)/shard_map/pallas_call | solution.py:47
  29.5 1.1 %collective-permute-done.5.refs_0_ = bf16[128,896]{1,0:T(8,128)(2,1)S(1)} collective-permute-done((bf16[128,896]{1,0:T(8,128)(2,1)S(1)}, bf16[128,896]{1,0:T(8,128)(2,1)S(1)}, u32[]{:S(2)}, u32[]{:S(2)}) %collective-permute-start.5) | collective-permute-done | bytes 229408 | tf_op jit(solution)/shard_map/ppermute | solution.py:37
  30.6 0.9 %shard_map.43 = f32[776,128]{1,0:T(8,128)S(1)} custom-call(bf16[1536,768]{1,0:T(8,128)(2,1)S(1)} %get-tuple-element.19.unit, bf16[128,896]{1,0:T(8,128)(2,1)S(1)} %collective-permute-done.5.refs_0_, f32[1536,256]{1,0:T(8,128)S(1)} %shard_map.41.refs_1_), custom_call_target="tpu_custom_call" | custom-call | flops 805306368 | bytes 1048576 | tf_op jit(solution)/shard_map/pallas_call | solution.py:47
  31.5 0.1 collective-permute-start.7
  31.5 0.9 %shard_map.42.mine = f32[776,128]{1,0:T(8,128)S(1)} custom-call(bf16[1536,768]{1,0:T(8,128)(2,1)S(1)} %get-tuple-element.19.unit, bf16[128,896]{1,0:T(8,128)(2,1)S(1)} %collective-permute-done.5.refs_0_, f32[1536,256]{1,0:T(8,128)S(1)} %shard_map.41.refs_1_), custom_call_target="tpu_custom_call" | custom-call | flops 805306368 | bytes 1048576 | tf_op jit(solution)/shard_map/pallas_call | solution.py:47
  32.4 0.8 %collective-permute-done.7.other = f32[776,128]{1,0:T(8,128)S(1)} collective-permute-done((f32[776,128]{1,0:T(8,128)S(1)}, f32[776,128]{1,0:T(8,128)S(1)}, u32[]{:S(2)}, u32[]{:S(2)}) %collective-permute-start.7) | collective-permute-done | bytes 397344 | tf_op jit(solution)/shard_map/ppermute | solution.py:37
  33.3 1.6 %collective-permute-start.8 = (bf16[800,128]{1,0:T(8,128)(2,1)S(1)}, bf16[800,128]{1,0:T(8,128)(2,1)S(1)}, u32[]{:S(2)}, u32[]{:S(2)}) collective-permute-start(bf16[800,128]{1,0:T(8,128)(2,1)S(1)} %shard_map.44.mine), channel_id=1, source_target_pairs={{0,2},{1,3},{2,0},{3,1},{4,6},{5,7},{6,4},{7,5},{8,10},{9,11},{10,... | collective-permute-start | bytes 614408 | tf_op jit(solution)/shard_map/ppermute | solution.py:37
  34.9 5.6 %collective-permute-done.8.other = bf16[800,128]{1,0:T(8,128)(2,1)S(1)} collective-permute-done((bf16[800,128]{1,0:T(8,128)(2,1)S(1)}, bf16[800,128]{1,0:T(8,128)(2,1)S(1)}, u32[]{:S(2)}, u32[]{:S(2)}) %collective-permute-start.8) | collective-permute-done | bytes 204832 | tf_op jit(solution)/shard_map/ppermute | solution.py:37
  40.5 0.7 %shard_map.45 = (f32[768,128]{1,0:T(8,128)S(1)}, f32[64,128]{1,0:T(8,128)S(1)}, f32[64,128]{1,0:T(8,128)S(1)}) custom-call(bf16[800,128]{1,0:T(8,128)(2,1)S(1)} %shard_map.44.mine, bf16[800,128]{1,0:T(8,128)(2,1)S(1)} %collective-permute-done.8.other), custom_call_target="tpu_custom_call" | custom-call | bytes 1048576 | tf_op jit(solution)/shard_map/pallas_call | solution.py:47
  41.2 0.1 collective-permute-start.15
  41.3 0.5 collective-permute-start.9
  41.8 1.3 %collective-permute-done.9 = f32[64,128]{1,0:T(8,128)S(1)} collective-permute-done((f32[64,128]{1,0:T(8,128)S(1)}, f32[64,128]{1,0:T(8,128)S(1)}, u32[]{:S(2)}, u32[]{:S(2)}) %collective-permute-start.9) | collective-permute-done | bytes 32800 | tf_op jit(solution)/shard_map/ppermute | solution.py:37
  43.0 3.2 %collective-permute-start.12 = (f32[64,128]{1,0:T(8,128)S(1)}, f32[64,128]{1,0:T(8,128)S(1)}, u32[]{:S(2)}, u32[]{:S(2)}) collective-permute-start(f32[64,128]{1,0:T(8,128)S(1)} %add.15), channel_id=1, source_target_pairs={{0,12},{4,8},{8,4},{12,0},{16,28},{20,24},{24,20},{28,16},{1,13},{... | collective-permute-start | bytes 98312 | tf_op jit(solution)/shard_map/ppermute | solution.py:37
  46.2 0.0 collective-permute-start.11
  46.2 0.6 %collective-permute-start.10 = (f32[64,128]{1,0:T(8,128)S(1)}, f32[64,128]{1,0:T(8,128)S(1)}, u32[]{:S(2)}, u32[]{:S(2)}) collective-permute-start(f32[64,128]{1,0:T(8,128)S(1)} %add.15), channel_id=1, source_target_pairs={{0,4},{4,0},{8,12},{12,8},{16,20},{20,16},{24,28},{28,24},{1,5},{5... | collective-permute-start | bytes 98312 | tf_op jit(solution)/shard_map/ppermute | solution.py:37
  46.8 1.3 %collective-permute-done.12 = f32[64,128]{1,0:T(8,128)S(1)} collective-permute-done((f32[64,128]{1,0:T(8,128)S(1)}, f32[64,128]{1,0:T(8,128)S(1)}, u32[]{:S(2)}, u32[]{:S(2)}) %collective-permute-start.12) | collective-permute-done | bytes 32800 | tf_op jit(solution)/shard_map/ppermute | solution.py:37
  48.1 2.0 %collective-permute-done.11 = f32[64,128]{1,0:T(8,128)S(1)} collective-permute-done((f32[64,128]{1,0:T(8,128)S(1)}, f32[64,128]{1,0:T(8,128)S(1)}, u32[]{:S(2)}, u32[]{:S(2)}) %collective-permute-start.11) | collective-permute-done | bytes 32800 | tf_op jit(solution)/shard_map/ppermute | solution.py:37
  50.1 0.0 collective-permute-done.10
  50.1 3.5 %collective-permute-start.13 = (f32[64,128]{1,0:T(8,128)S(1)}, f32[64,128]{1,0:T(8,128)S(1)}, u32[]{:S(2)}, u32[]{:S(2)}) collective-permute-start(f32[64,128]{1,0:T(8,128)S(1)} %add_add_fusion), channel_id=1, source_target_pairs={{0,16},{4,20},{8,24},{12,28},{16,0},{20,4},{24,8},{28,12},{1,17},{... | collective-permute-start | bytes 98312 | tf_op jit(solution)/shard_map/ppermute | solution.py:37
  53.6 1.9 %collective-permute-done.13 = f32[64,128]{1,0:T(8,128)S(1)} collective-permute-done((f32[64,128]{1,0:T(8,128)S(1)}, f32[64,128]{1,0:T(8,128)S(1)}, u32[]{:S(2)}, u32[]{:S(2)}) %collective-permute-start.13) | collective-permute-done | bytes 32800 | tf_op jit(solution)/shard_map/ppermute | solution.py:37
  55.5 0.0 collective-permute-start.14
  55.5 0.0 collective-permute-done.15.theirs
  55.5 0.1 shard_map.46.parts
  55.7 1.0 %collective-permute-done.14.theirs = f32[64,128]{1,0:T(8,128)S(1)} collective-permute-done((f32[64,128]{1,0:T(8,128)S(1)}, f32[64,128]{1,0:T(8,128)S(1)}, u32[]{:S(2)}, u32[]{:S(2)}) %collective-permute-start.14) | collective-permute-done | bytes 32800 | tf_op jit(solution)/shard_map/ppermute | solution.py:37
  56.7 4.7 %shard_map.47 = f32[1536,128]{1,0:T(8,128)} custom-call(f32[64,128]{1,0:T(8,128)S(1)} %add.19.own, f32[64,128]{1,0:T(8,128)S(1)} %collective-permute-done.14.theirs, bf16[1536,384]{1,0:T(8,128)(2,1)S(1)} %shard_map.46.parts), custom_call_target="tpu_custom_call" | custom-call | bytes 1048576 | tf_op jit(solution)/shard_map/pallas_call | solution.py:47
  (4 shorter events, 0.1 us)
Async XLA Ops:
  1.7 14.9 %collective-permute-start.2 = (bf16[128,896]{1,0:T(8,128)(2,1)}, bf16[128,896]{1,0:T(8,128)(2,1)S(1)}, u32[]{:S(2)}, u32[]{:S(2)}) collective-permute-start(bf16[128,896]{1,0:T(8,128)(2,1)} %shard_map.37.block), channel_id=1, source_target_pairs={{0,16},{4,20},{8,24},{12,28},{16,0},{20,4},{24,8},{28,12},{1,17},{... | collective-permute-start | bytes 688136 | tf_op jit(solution)/shard_map/ppermute | solution.py:37
  5.8 11.0 %collective-permute-start.1 = (bf16[128,896]{1,0:T(8,128)(2,1)}, bf16[128,896]{1,0:T(8,128)(2,1)S(1)}, u32[]{:S(2)}, u32[]{:S(2)}) collective-permute-start(bf16[128,896]{1,0:T(8,128)(2,1)} %shard_map.37.block), channel_id=1, source_target_pairs={{0,8},{4,12},{8,0},{12,4},{16,24},{20,28},{24,16},{28,20},{1,9},{5... | collective-permute-start | bytes 688136 | tf_op jit(solution)/shard_map/ppermute | solution.py:37
  7.3 9.5 %collective-permute-start = (bf16[128,896]{1,0:T(8,128)(2,1)}, bf16[128,896]{1,0:T(8,128)(2,1)S(1)}, u32[]{:S(2)}, u32[]{:S(2)}) collective-permute-start(bf16[128,896]{1,0:T(8,128)(2,1)} %shard_map.37.block), channel_id=1, source_target_pairs={{0,4},{4,0},{8,12},{12,8},{16,20},{20,16},{24,28},{28,24},{1,5},{5... | collective-permute-start | bytes 688136 | tf_op jit(solution)/shard_map/ppermute | solution.py:37
  8.8 1.0 %copy-start = (bf16[128,896]{1,0:T(8,128)(2,1)S(1)}, bf16[128,896]{1,0:T(8,128)(2,1)}, u32[]{:S(2)}) copy-start(bf16[128,896]{1,0:T(8,128)(2,1)} %shard_map.37.block) | copy-start | bytes 688132
  16.8 6.8 %collective-permute-start.4 = (bf16[128,896]{1,0:T(8,128)(2,1)S(1)}, bf16[128,896]{1,0:T(8,128)(2,1)S(1)}, u32[]{:S(2)}, u32[]{:S(2)}) collective-permute-start(bf16[128,896]{1,0:T(8,128)(2,1)S(1)} %collective-permute-done.2.refs_0_), channel_id=1, source_target_pairs={{0,8},{4,12},{8,0},{12,4},{16,24},{20,28},{24,16},{28,20},{1,9},{5... | collective-permute-start | bytes 688136 | tf_op jit(solution)/shard_map/ppermute | solution.py:37
  18.3 6.3 %collective-permute-start.3 = (bf16[128,896]{1,0:T(8,128)(2,1)S(1)}, bf16[128,896]{1,0:T(8,128)(2,1)S(1)}, u32[]{:S(2)}, u32[]{:S(2)}) collective-permute-start(bf16[128,896]{1,0:T(8,128)(2,1)S(1)} %collective-permute-done.2.refs_0_), channel_id=1, source_target_pairs={{0,4},{4,0},{8,12},{12,8},{16,20},{20,16},{24,28},{28,24},{1,5},{5... | collective-permute-start | bytes 688136 | tf_op jit(solution)/shard_map/ppermute | solution.py:37
  22.1 6.2 %collective-permute-start.6 = (bf16[128,896]{1,0:T(8,128)(2,1)S(1)}, bf16[128,896]{1,0:T(8,128)(2,1)S(1)}, u32[]{:S(2)}, u32[]{:S(2)}) collective-permute-start(bf16[128,896]{1,0:T(8,128)(2,1)S(1)} %collective-permute-done.refs_2_), channel_id=1, source_target_pairs={{0,8},{4,12},{8,0},{12,4},{16,24},{20,28},{24,16},{28,20},{1,9},{5... | collective-permute-start | bytes 688136 | tf_op jit(solution)/shard_map/ppermute | solution.py:37
  24.6 6.0 %collective-permute-start.5 = (bf16[128,896]{1,0:T(8,128)(2,1)S(1)}, bf16[128,896]{1,0:T(8,128)(2,1)S(1)}, u32[]{:S(2)}, u32[]{:S(2)}) collective-permute-start(bf16[128,896]{1,0:T(8,128)(2,1)S(1)} %collective-permute-done.4.refs_0_), channel_id=1, source_target_pairs={{0,4},{4,0},{8,12},{12,8},{16,20},{20,16},{24,28},{28,24},{1,5},{5... | collective-permute-start | bytes 688136 | tf_op jit(solution)/shard_map/ppermute | solution.py:37
  31.5 1.8 %collective-permute-start.7 = (f32[776,128]{1,0:T(8,128)S(1)}, f32[776,128]{1,0:T(8,128)S(1)}, u32[]{:S(2)}, u32[]{:S(2)}) collective-permute-start(f32[776,128]{1,0:T(8,128)S(1)} %shard_map.43), channel_id=1, source_target_pairs={{0,1},{1,0},{2,3},{3,2},{4,5},{5,4},{6,7},{7,6},{8,9},{9,8},{10,11... | collective-permute-start | bytes 1191944 | tf_op jit(solution)/shard_map/ppermute | solution.py:37
  33.3 7.2 %collective-permute-start.8 = (bf16[800,128]{1,0:T(8,128)(2,1)S(1)}, bf16[800,128]{1,0:T(8,128)(2,1)S(1)}, u32[]{:S(2)}, u32[]{:S(2)}) collective-permute-start(bf16[800,128]{1,0:T(8,128)(2,1)S(1)} %shard_map.44.mine), channel_id=1, source_target_pairs={{0,2},{1,3},{2,0},{3,1},{4,6},{5,7},{6,4},{7,5},{8,10},{9,11},{10,... | collective-permute-start | bytes 614408 | tf_op jit(solution)/shard_map/ppermute | solution.py:37
  41.2 14.3 %collective-permute-start.15 = (f32[768,128]{1,0:T(8,128)S(1)}, f32[768,128]{1,0:T(8,128)S(1)}, u32[]{:S(2)}, u32[]{:S(2)}) collective-permute-start(f32[768,128]{1,0:T(8,128)S(1)} %get-tuple-element.32.own), channel_id=1, source_target_pairs={{0,1},{1,0},{2,3},{3,2},{4,5},{5,4},{6,7},{7,6},{8,9},{9,8},{10,11... | collective-permute-start | bytes 1179656 | tf_op jit(solution)/shard_map/ppermute | solution.py:37
  41.3 1.8 %collective-permute-start.9 = (f32[64,128]{1,0:T(8,128)S(1)}, f32[64,128]{1,0:T(8,128)S(1)}, u32[]{:S(2)}, u32[]{:S(2)}) collective-permute-start(f32[64,128]{1,0:T(8,128)S(1)} %get-tuple-element.31), channel_id=1, source_target_pairs={{0,1},{1,0},{2,3},{3,2},{4,5},{5,4},{6,7},{7,6},{8,9},{9,8},{10,11... | collective-permute-start | bytes 98312 | tf_op jit(solution)/shard_map/ppermute | solution.py:37
  43.0 5.1 %collective-permute-start.12 = (f32[64,128]{1,0:T(8,128)S(1)}, f32[64,128]{1,0:T(8,128)S(1)}, u32[]{:S(2)}, u32[]{:S(2)}) collective-permute-start(f32[64,128]{1,0:T(8,128)S(1)} %add.15), channel_id=1, source_target_pairs={{0,12},{4,8},{8,4},{12,0},{16,28},{20,24},{24,20},{28,16},{1,13},{... | collective-permute-start | bytes 98312 | tf_op jit(solution)/shard_map/ppermute | solution.py:37
  46.2 3.9 %collective-permute-start.11 = (f32[64,128]{1,0:T(8,128)S(1)}, f32[64,128]{1,0:T(8,128)S(1)}, u32[]{:S(2)}, u32[]{:S(2)}) collective-permute-start(f32[64,128]{1,0:T(8,128)S(1)} %add.15), channel_id=1, source_target_pairs={{0,8},{4,12},{8,0},{12,4},{16,24},{20,28},{24,16},{28,20},{1,9},{5... | collective-permute-start | bytes 98312 | tf_op jit(solution)/shard_map/ppermute | solution.py:37
  46.2 3.9 %collective-permute-start.10 = (f32[64,128]{1,0:T(8,128)S(1)}, f32[64,128]{1,0:T(8,128)S(1)}, u32[]{:S(2)}, u32[]{:S(2)}) collective-permute-start(f32[64,128]{1,0:T(8,128)S(1)} %add.15), channel_id=1, source_target_pairs={{0,4},{4,0},{8,12},{12,8},{16,20},{20,16},{24,28},{28,24},{1,5},{5... | collective-permute-start | bytes 98312 | tf_op jit(solution)/shard_map/ppermute | solution.py:37
  50.1 5.3 %collective-permute-start.13 = (f32[64,128]{1,0:T(8,128)S(1)}, f32[64,128]{1,0:T(8,128)S(1)}, u32[]{:S(2)}, u32[]{:S(2)}) collective-permute-start(f32[64,128]{1,0:T(8,128)S(1)} %add_add_fusion), channel_id=1, source_target_pairs={{0,16},{4,20},{8,24},{12,28},{16,0},{20,4},{24,8},{28,12},{1,17},{... | collective-permute-start | bytes 98312 | tf_op jit(solution)/shard_map/ppermute | solution.py:37
  55.5 1.2 %collective-permute-start.14 = (f32[64,128]{1,0:T(8,128)S(1)}, f32[64,128]{1,0:T(8,128)S(1)}, u32[]{:S(2)}, u32[]{:S(2)}) collective-permute-start(f32[64,128]{1,0:T(8,128)S(1)} %add.19.own), channel_id=1, source_target_pairs={{0,1},{1,0},{2,3},{3,2},{4,5},{5,4},{6,7},{7,6},{8,9},{9,8},{10,11... | collective-permute-start | bytes 98312 | tf_op jit(solution)/shard_map/ppermute | solution.py:37

commit v11 on v10

--- a/solution.py
+++ b/solution.py
@@ -358,9 +358,10 @@
         (embed, swap(embed, "lmk", num_lmk, 1)),
     )
     if num_pts == 8:
+        part = part + swap(part, "pts", num_pts, 4)
         pair = part + swap(part, "pts", num_pts, 1)
         part = pair + (swap(part, "pts", num_pts, 2) + swap(part, "pts", num_pts, 3))
-        pts_bits = [4]
+        pts_bits = []
     for bit in pts_bits:
         part = part + swap(part, "pts", num_pts, bit)
     return call_on(

time: 61.7 us -> 62 us (level)
  transfers between devices with their start and end apart: 16 -> 16, of which waited for: 13 -> 14; matrix products, arithmetic and copies ran while one was open for 0% -> 0% of each run, Pallas kernels for 15% -> 15%
where the time goes in v11:
time: 62 us; the launch traced here: 61.8 us
  starting transfers between devices  21.7 us (35%)
  waiting for transfers between devices  21.7 us (35%)
  Pallas kernels  17.3 us (28%)
  local copies, waits for them, and re-layouts  0.97 us (2%)
    ppermute x16, starting transfers between devices, swap(): return lax.ppermute(value, axis, [(i, i ^ bit) for i in range(size)])  21.7 us
    ppermute x16, waiting for transfers between devices, swap(): return lax.ppermute(value, axis, [(i, i ^ bit) for i in range(size)])  21.7 us
    pallas_call x10, Pallas kernels, call_on(): pl.pallas_call(kernel, out_shape=out, in_specs=[rest.get('in_specs', VMEM...  15.6 us
    pallas_call x1, Pallas kernels, per_device(): pl.pallas_call(beside_kernel, out_shape=shape((landmarks.shape[0], featur...  1.64 us
  transfers between devices with their start and end apart: 16, of which 14 were waited for; matrix products, arithmetic and copies ran while one was open for 0% of the time, Pallas kernels for 15%

profile of v11, /device:TPU:0, one launch (start us, length us, event | category | flops | bytes accessed | tf_op | source)
XLA Modules:
  0.0 61.8 jit_solution(7780426498901556561)
XLA Ops:
  0.0 1.6 %shard_map.37.block = bf16[128,896]{1,0:T(8,128)(2,1)} custom-call(bf16[128,768]{1,0:T(8,128)(2,1)} %left.1, bf16[128,128]{1,0:T(8,128)(2,1)} %right.1), custom_call_target="tpu_custom_call" | custom-call | tf_op jit(solution)/shard_map/pallas_call | solution.py:275
  1.7 4.1 %collective-permute-start.2 = (bf16[128,896]{1,0:T(8,128)(2,1)}, bf16[128,896]{1,0:T(8,128)(2,1)S(1)}, u32[]{:S(2)}, u32[]{:S(2)}) collective-permute-start(bf16[128,896]{1,0:T(8,128)(2,1)} %shard_map.37.block), channel_id=1, source_target_pairs={{0,16},{4,20},{8,24},{12,28},{16,0},{20,4},{24,8},{28,12},{1,17},{... | collective-permute-start | bytes 688136 | tf_op jit(solution)/shard_map/ppermute | solution.py:37
  5.8 1.6 %collective-permute-start.1 = (bf16[128,896]{1,0:T(8,128)(2,1)}, bf16[128,896]{1,0:T(8,128)(2,1)S(1)}, u32[]{:S(2)}, u32[]{:S(2)}) collective-permute-start(bf16[128,896]{1,0:T(8,128)(2,1)} %shard_map.37.block), channel_id=1, source_target_pairs={{0,8},{4,12},{8,0},{12,4},{16,24},{20,28},{24,16},{28,20},{1,9},{5... | collective-permute-start | bytes 688136 | tf_op jit(solution)/shard_map/ppermute | solution.py:37
  7.3 1.5 %collective-permute-start = (bf16[128,896]{1,0:T(8,128)(2,1)}, bf16[128,896]{1,0:T(8,128)(2,1)S(1)}, u32[]{:S(2)}, u32[]{:S(2)}) collective-permute-start(bf16[128,896]{1,0:T(8,128)(2,1)} %shard_map.37.block), channel_id=1, source_target_pairs={{0,4},{4,0},{8,12},{12,8},{16,20},{20,16},{24,28},{28,24},{1,5},{5... | collective-permute-start | bytes 688136 | tf_op jit(solution)/shard_map/ppermute | solution.py:37
  8.8 0.0 copy-start
  8.8 1.0 %copy-done = bf16[128,896]{1,0:T(8,128)(2,1)S(1)} copy-done((bf16[128,896]{1,0:T(8,128)(2,1)S(1)}, bf16[128,896]{1,0:T(8,128)(2,1)}, u32[]{:S(2)}) %copy-start) | copy-done | bytes 229400
  9.8 3.1 %shard_map.38 = (bf16[1536,768]{1,0:T(8,128)(2,1)S(1)}, f32[1536,256]{1,0:T(8,128)S(1)}) custom-call(bf16[1536,768]{1,0:T(8,128)(2,1)} %points.1, bf16[128,896]{1,0:T(8,128)(2,1)S(1)} %copy-done), custom_call_target="tpu_custom_call" | custom-call | flops 1610612736 | bytes 1048576 | tf_op jit(solution)/shard_map/pallas_call | solution.py:47
  12.9 3.7 %collective-permute-done.2.refs_0_ = bf16[128,896]{1,0:T(8,128)(2,1)S(1)} collective-permute-done((bf16[128,896]{1,0:T(8,128)(2,1)}, bf16[128,896]{1,0:T(8,128)(2,1)S(1)}, u32[]{:S(2)}, u32[]{:S(2)}) %collective-permute-start.2) | collective-permute-done | bytes 229408 | tf_op jit(solution)/shard_map/ppermute | solution.py:37
  16.6 0.2 collective-permute-done.1.refs_1_
  16.8 0.0 collective-permute-done.refs_2_
  16.8 1.5 %collective-permute-start.4 = (bf16[128,896]{1,0:T(8,128)(2,1)S(1)}, bf16[128,896]{1,0:T(8,128)(2,1)S(1)}, u32[]{:S(2)}, u32[]{:S(2)}) collective-permute-start(bf16[128,896]{1,0:T(8,128)(2,1)S(1)} %collective-permute-done.2.refs_0_), channel_id=1, source_target_pairs={{0,8},{4,12},{8,0},{12,4},{16,24},{20,28},{24,16},{28,20},{1,9},{5... | collective-permute-start | bytes 688136 | tf_op jit(solution)/shard_map/ppermute | solution.py:37
  18.3 1.5 %collective-permute-start.3 = (bf16[128,896]{1,0:T(8,128)(2,1)S(1)}, bf16[128,896]{1,0:T(8,128)(2,1)S(1)}, u32[]{:S(2)}, u32[]{:S(2)}) collective-permute-start(bf16[128,896]{1,0:T(8,128)(2,1)S(1)} %collective-permute-done.2.refs_0_), channel_id=1, source_target_pairs={{0,4},{4,0},{8,12},{12,8},{16,20},{20,16},{24,28},{28,24},{1,5},{5... | collective-permute-start | bytes 688136 | tf_op jit(solution)/shard_map/ppermute | solution.py:37
  19.8 2.3 %shard_map.39.refs_2_ = f32[1536,256]{1,0:T(8,128)S(1)} custom-call(bf16[1536,768]{1,0:T(8,128)(2,1)S(1)} %get-tuple-element.19.unit, bf16[128,896]{1,0:T(8,128)(2,1)S(1)} %collective-permute-done.2.refs_0_, bf16[128,896]{1,0:T(8,128)(2,1)S(1)} %collective-permute-done.1.refs_1_, ...), custom_call_target="tpu_custom_call", output_to_operand_aliasing={{}: (4, {})} | custom-call | flops 4831838208 | bytes 1048576 | tf_op jit(solution)/shard_map/pallas_call | solution.py:47
  22.1 0.7 %collective-permute-start.6 = (bf16[128,896]{1,0:T(8,128)(2,1)S(1)}, bf16[128,896]{1,0:T(8,128)(2,1)S(1)}, u32[]{:S(2)}, u32[]{:S(2)}) collective-permute-start(bf16[128,896]{1,0:T(8,128)(2,1)S(1)} %collective-permute-done.refs_2_), channel_id=1, source_target_pairs={{0,8},{4,12},{8,0},{12,4},{16,24},{20,28},{24,16},{28,20},{1,9},{5... | collective-permute-start | bytes 688136 | tf_op jit(solution)/shard_map/ppermute | solution.py:37
  22.7 0.9 %collective-permute-done.4.refs_0_ = bf16[128,896]{1,0:T(8,128)(2,1)S(1)} collective-permute-done((bf16[128,896]{1,0:T(8,128)(2,1)S(1)}, bf16[128,896]{1,0:T(8,128)(2,1)S(1)}, u32[]{:S(2)}, u32[]{:S(2)}) %collective-permute-start.4) | collective-permute-done | bytes 229408 | tf_op jit(solution)/shard_map/ppermute | solution.py:37
  23.6 1.0 %collective-permute-done.3.refs_1_ = bf16[128,896]{1,0:T(8,128)(2,1)S(1)} collective-permute-done((bf16[128,896]{1,0:T(8,128)(2,1)S(1)}, bf16[128,896]{1,0:T(8,128)(2,1)S(1)}, u32[]{:S(2)}, u32[]{:S(2)}) %collective-permute-start.3) | collective-permute-done | bytes 229408 | tf_op jit(solution)/shard_map/ppermute | solution.py:37
  24.6 1.5 %collective-permute-start.5 = (bf16[128,896]{1,0:T(8,128)(2,1)S(1)}, bf16[128,896]{1,0:T(8,128)(2,1)S(1)}, u32[]{:S(2)}, u32[]{:S(2)}) collective-permute-start(bf16[128,896]{1,0:T(8,128)(2,1)S(1)} %collective-permute-done.4.refs_0_), channel_id=1, source_target_pairs={{0,4},{4,0},{8,12},{12,8},{16,20},{20,16},{24,28},{28,24},{1,5},{5... | collective-permute-start | bytes 688136 | tf_op jit(solution)/shard_map/ppermute | solution.py:37
  26.1 1.7 %shard_map.40.refs_1_ = f32[1536,256]{1,0:T(8,128)S(1)} custom-call(bf16[1536,768]{1,0:T(8,128)(2,1)S(1)} %get-tuple-element.19.unit, bf16[128,896]{1,0:T(8,128)(2,1)S(1)} %collective-permute-done.4.refs_0_, bf16[128,896]{1,0:T(8,128)(2,1)S(1)} %collective-permute-done.3.refs_1_, f32[1536,256]{1,0:T(8,128)S(1)} %shard_map.39.refs_2_), custom_call_target="tpu_custom_call", output_to_operand_aliasing={{}: (3, {})} | custom-call | flops 3221225472 | bytes 1048576 | tf_op jit(solution)/shard_map/pallas_call | solution.py:47
  27.8 0.5 collective-permute-done.6.refs_0_
  28.2 1.3 %shard_map.41.refs_1_ = f32[1536,256]{1,0:T(8,128)S(1)} custom-call(bf16[1536,768]{1,0:T(8,128)(2,1)S(1)} %get-tuple-element.19.unit, bf16[128,896]{1,0:T(8,128)(2,1)S(1)} %collective-permute-done.6.refs_0_, f32[1536,256]{1,0:T(8,128)S(1)} %shard_map.40.refs_1_), custom_call_target="tpu_custom_call", output_to_operand_aliasing={{}: (2, {})} | custom-call | flops 1610612736 | bytes 1048576 | tf_op jit(solution)/shard_map/pallas_call | solution.py:47
  29.5 1.1 %collective-permute-done.5.refs_0_ = bf16[128,896]{1,0:T(8,128)(2,1)S(1)} collective-permute-done((bf16[128,896]{1,0:T(8,128)(2,1)S(1)}, bf16[128,896]{1,0:T(8,128)(2,1)S(1)}, u32[]{:S(2)}, u32[]{:S(2)}) %collective-permute-start.5) | collective-permute-done | bytes 229408 | tf_op jit(solution)/shard_map/ppermute | solution.py:37
  30.6 0.9 %shard_map.43 = f32[776,128]{1,0:T(8,128)S(1)} custom-call(bf16[1536,768]{1,0:T(8,128)(2,1)S(1)} %get-tuple-element.19.unit, bf16[128,896]{1,0:T(8,128)(2,1)S(1)} %collective-permute-done.5.refs_0_, f32[1536,256]{1,0:T(8,128)S(1)} %shard_map.41.refs_1_), custom_call_target="tpu_custom_call" | custom-call | flops 805306368 | bytes 1048576 | tf_op jit(solution)/shard_map/pallas_call | solution.py:47
  31.5 0.1 collective-permute-start.7
  31.5 0.9 %shard_map.42.mine = f32[776,128]{1,0:T(8,128)S(1)} custom-call(bf16[1536,768]{1,0:T(8,128)(2,1)S(1)} %get-tuple-element.19.unit, bf16[128,896]{1,0:T(8,128)(2,1)S(1)} %collective-permute-done.5.refs_0_, f32[1536,256]{1,0:T(8,128)S(1)} %shard_map.41.refs_1_), custom_call_target="tpu_custom_call" | custom-call | flops 805306368 | bytes 1048576 | tf_op jit(solution)/shard_map/pallas_call | solution.py:47
  32.4 0.8 %collective-permute-done.7.other = f32[776,128]{1,0:T(8,128)S(1)} collective-permute-done((f32[776,128]{1,0:T(8,128)S(1)}, f32[776,128]{1,0:T(8,128)S(1)}, u32[]{:S(2)}, u32[]{:S(2)}) %collective-permute-start.7) | collective-permute-done | bytes 397344 | tf_op jit(solution)/shard_map/ppermute | solution.py:37
  33.3 1.6 %collective-permute-start.8 = (bf16[800,128]{1,0:T(8,128)(2,1)S(1)}, bf16[800,128]{1,0:T(8,128)(2,1)S(1)}, u32[]{:S(2)}, u32[]{:S(2)}) collective-permute-start(bf16[800,128]{1,0:T(8,128)(2,1)S(1)} %shard_map.44.mine), channel_id=1, source_target_pairs={{0,2},{1,3},{2,0},{3,1},{4,6},{5,7},{6,4},{7,5},{8,10},{9,11},{10,... | collective-permute-start | bytes 614408 | tf_op jit(solution)/shard_map/ppermute | solution.py:37
  34.9 5.6 %collective-permute-done.8.other = bf16[800,128]{1,0:T(8,128)(2,1)S(1)} collective-permute-done((bf16[800,128]{1,0:T(8,128)(2,1)S(1)}, bf16[800,128]{1,0:T(8,128)(2,1)S(1)}, u32[]{:S(2)}, u32[]{:S(2)}) %collective-permute-start.8) | collective-permute-done | bytes 204832 | tf_op jit(solution)/shard_map/ppermute | solution.py:37
  40.5 0.7 %shard_map.45 = (f32[768,128]{1,0:T(8,128)S(1)}, f32[64,128]{1,0:T(8,128)S(1)}, f32[64,128]{1,0:T(8,128)S(1)}) custom-call(bf16[800,128]{1,0:T(8,128)(2,1)S(1)} %shard_map.44.mine, bf16[800,128]{1,0:T(8,128)(2,1)S(1)} %collective-permute-done.8.other), custom_call_target="tpu_custom_call" | custom-call | bytes 1048576 | tf_op jit(solution)/shard_map/pallas_call | solution.py:47
  41.2 0.1 collective-permute-start.15
  41.3 0.5 collective-permute-start.9
  41.8 1.3 %collective-permute-done.9 = f32[64,128]{1,0:T(8,128)S(1)} collective-permute-done((f32[64,128]{1,0:T(8,128)S(1)}, f32[64,128]{1,0:T(8,128)S(1)}, u32[]{:S(2)}, u32[]{:S(2)}) %collective-permute-start.9) | collective-permute-done | bytes 32800 | tf_op jit(solution)/shard_map/ppermute | solution.py:37
  43.0 3.6 %collective-permute-start.10 = (f32[64,128]{1,0:T(8,128)S(1)}, f32[64,128]{1,0:T(8,128)S(1)}, u32[]{:S(2)}, u32[]{:S(2)}) collective-permute-start(f32[64,128]{1,0:T(8,128)S(1)} %add.15), channel_id=1, source_target_pairs={{0,16},{4,20},{8,24},{12,28},{16,0},{20,4},{24,8},{28,12},{1,17},{... | collective-permute-start | bytes 98312 | tf_op jit(solution)/shard_map/ppermute | solution.py:37
  46.6 2.4 %collective-permute-done.10 = f32[64,128]{1,0:T(8,128)S(1)} collective-permute-done((f32[64,128]{1,0:T(8,128)S(1)}, f32[64,128]{1,0:T(8,128)S(1)}, u32[]{:S(2)}, u32[]{:S(2)}) %collective-permute-start.10) | collective-permute-done | bytes 32800 | tf_op jit(solution)/shard_map/ppermute | solution.py:37
  49.0 2.0 %collective-permute-start.13 = (f32[64,128]{1,0:T(8,128)S(1)}, f32[64,128]{1,0:T(8,128)S(1)}, u32[]{:S(2)}, u32[]{:S(2)}) collective-permute-start(f32[64,128]{1,0:T(8,128)S(1)} %add.16), channel_id=1, source_target_pairs={{0,12},{4,8},{8,4},{12,0},{16,28},{20,24},{24,20},{28,16},{1,13},{... | collective-permute-start | bytes 98312 | tf_op jit(solution)/shard_map/ppermute | solution.py:37
  51.0 0.8 %collective-permute-start.12 = (f32[64,128]{1,0:T(8,128)S(1)}, f32[64,128]{1,0:T(8,128)S(1)}, u32[]{:S(2)}, u32[]{:S(2)}) collective-permute-start(f32[64,128]{1,0:T(8,128)S(1)} %add.16), channel_id=1, source_target_pairs={{0,8},{4,12},{8,0},{12,4},{16,24},{20,28},{24,16},{28,20},{1,9},{5... | collective-permute-start | bytes 98312 | tf_op jit(solution)/shard_map/ppermute | solution.py:37
  51.9 0.7 %collective-permute-start.11 = (f32[64,128]{1,0:T(8,128)S(1)}, f32[64,128]{1,0:T(8,128)S(1)}, u32[]{:S(2)}, u32[]{:S(2)}) collective-permute-start(f32[64,128]{1,0:T(8,128)S(1)} %add.16), channel_id=1, source_target_pairs={{0,4},{4,0},{8,12},{12,8},{16,20},{20,16},{24,28},{28,24},{1,5},{5... | collective-permute-start | bytes 98312 | tf_op jit(solution)/shard_map/ppermute | solution.py:37
  52.5 1.3 %collective-permute-done.13 = f32[64,128]{1,0:T(8,128)S(1)} collective-permute-done((f32[64,128]{1,0:T(8,128)S(1)}, f32[64,128]{1,0:T(8,128)S(1)}, u32[]{:S(2)}, u32[]{:S(2)}) %collective-permute-start.13) | collective-permute-done | bytes 32800 | tf_op jit(solution)/shard_map/ppermute | solution.py:37
  53.9 1.1 %collective-permute-done.12 = f32[64,128]{1,0:T(8,128)S(1)} collective-permute-done((f32[64,128]{1,0:T(8,128)S(1)}, f32[64,128]{1,0:T(8,128)S(1)}, u32[]{:S(2)}, u32[]{:S(2)}) %collective-permute-start.12) | collective-permute-done | bytes 32800 | tf_op jit(solution)/shard_map/ppermute | solution.py:37
  54.9 0.8 %collective-permute-done.11 = f32[64,128]{1,0:T(8,128)S(1)} collective-permute-done((f32[64,128]{1,0:T(8,128)S(1)}, f32[64,128]{1,0:T(8,128)S(1)}, u32[]{:S(2)}, u32[]{:S(2)}) %collective-permute-start.11) | collective-permute-done | bytes 32800 | tf_op jit(solution)/shard_map/ppermute | solution.py:37
  55.8 0.1 collective-permute-start.14
  55.9 0.0 collective-permute-done.15.theirs
  55.9 0.1 shard_map.46.parts
  56.0 1.0 %collective-permute-done.14.theirs = f32[64,128]{1,0:T(8,128)S(1)} collective-permute-done((f32[64,128]{1,0:T(8,128)S(1)}, f32[64,128]{1,0:T(8,128)S(1)}, u32[]{:S(2)}, u32[]{:S(2)}) %collective-permute-start.14) | collective-permute-done | bytes 32800 | tf_op jit(solution)/shard_map/ppermute | solution.py:37
  57.1 4.7 %shard_map.47 = f32[1536,128]{1,0:T(8,128)} custom-call(f32[64,128]{1,0:T(8,128)S(1)} %add_add_fusion.own, f32[64,128]{1,0:T(8,128)S(1)} %collective-permute-done.14.theirs, bf16[1536,384]{1,0:T(8,128)(2,1)S(1)} %shard_map.46.parts), custom_call_target="tpu_custom_call" | custom-call | bytes 1048576 | tf_op jit(solution)/shard_map/pallas_call | solution.py:47
  (4 shorter events, 0.1 us)
Async XLA Ops:
  1.7 14.9 %collective-permute-start.2 = (bf16[128,896]{1,0:T(8,128)(2,1)}, bf16[128,896]{1,0:T(8,128)(2,1)S(1)}, u32[]{:S(2)}, u32[]{:S(2)}) collective-permute-start(bf16[128,896]{1,0:T(8,128)(2,1)} %shard_map.37.block), channel_id=1, source_target_pairs={{0,16},{4,20},{8,24},{12,28},{16,0},{20,4},{24,8},{28,12},{1,17},{... | collective-permute-start | bytes 688136 | tf_op jit(solution)/shard_map/ppermute | solution.py:37
  5.8 11.0 %collective-permute-start.1 = (bf16[128,896]{1,0:T(8,128)(2,1)}, bf16[128,896]{1,0:T(8,128)(2,1)S(1)}, u32[]{:S(2)}, u32[]{:S(2)}) collective-permute-start(bf16[128,896]{1,0:T(8,128)(2,1)} %shard_map.37.block), channel_id=1, source_target_pairs={{0,8},{4,12},{8,0},{12,4},{16,24},{20,28},{24,16},{28,20},{1,9},{5... | collective-permute-start | bytes 688136 | tf_op jit(solution)/shard_map/ppermute | solution.py:37
  7.3 9.5 %collective-permute-start = (bf16[128,896]{1,0:T(8,128)(2,1)}, bf16[128,896]{1,0:T(8,128)(2,1)S(1)}, u32[]{:S(2)}, u32[]{:S(2)}) collective-permute-start(bf16[128,896]{1,0:T(8,128)(2,1)} %shard_map.37.block), channel_id=1, source_target_pairs={{0,4},{4,0},{8,12},{12,8},{16,20},{20,16},{24,28},{28,24},{1,5},{5... | collective-permute-start | bytes 688136 | tf_op jit(solution)/shard_map/ppermute | solution.py:37
  8.8 1.0 %copy-start = (bf16[128,896]{1,0:T(8,128)(2,1)S(1)}, bf16[128,896]{1,0:T(8,128)(2,1)}, u32[]{:S(2)}) copy-start(bf16[128,896]{1,0:T(8,128)(2,1)} %shard_map.37.block) | copy-start | bytes 688132
  16.8 6.8 %collective-permute-start.4 = (bf16[128,896]{1,0:T(8,128)(2,1)S(1)}, bf16[128,896]{1,0:T(8,128)(2,1)S(1)}, u32[]{:S(2)}, u32[]{:S(2)}) collective-permute-start(bf16[128,896]{1,0:T(8,128)(2,1)S(1)} %collective-permute-done.2.refs_0_), channel_id=1, source_target_pairs={{0,8},{4,12},{8,0},{12,4},{16,24},{20,28},{24,16},{28,20},{1,9},{5... | collective-permute-start | bytes 688136 | tf_op jit(solution)/shard_map/ppermute | solution.py:37
  18.3 6.3 %collective-permute-start.3 = (bf16[128,896]{1,0:T(8,128)(2,1)S(1)}, bf16[128,896]{1,0:T(8,128)(2,1)S(1)}, u32[]{:S(2)}, u32[]{:S(2)}) collective-permute-start(bf16[128,896]{1,0:T(8,128)(2,1)S(1)} %collective-permute-done.2.refs_0_), channel_id=1, source_target_pairs={{0,4},{4,0},{8,12},{12,8},{16,20},{20,16},{24,28},{28,24},{1,5},{5... | collective-permute-start | bytes 688136 | tf_op jit(solution)/shard_map/ppermute | solution.py:37
  22.1 6.2 %collective-permute-start.6 = (bf16[128,896]{1,0:T(8,128)(2,1)S(1)}, bf16[128,896]{1,0:T(8,128)(2,1)S(1)}, u32[]{:S(2)}, u32[]{:S(2)}) collective-permute-start(bf16[128,896]{1,0:T(8,128)(2,1)S(1)} %collective-permute-done.refs_2_), channel_id=1, source_target_pairs={{0,8},{4,12},{8,0},{12,4},{16,24},{20,28},{24,16},{28,20},{1,9},{5... | collective-permute-start | bytes 688136 | tf_op jit(solution)/shard_map/ppermute | solution.py:37
  24.6 6.0 %collective-permute-start.5 = (bf16[128,896]{1,0:T(8,128)(2,1)S(1)}, bf16[128,896]{1,0:T(8,128)(2,1)S(1)}, u32[]{:S(2)}, u32[]{:S(2)}) collective-permute-start(bf16[128,896]{1,0:T(8,128)(2,1)S(1)} %collective-permute-done.4.refs_0_), channel_id=1, source_target_pairs={{0,4},{4,0},{8,12},{12,8},{16,20},{20,16},{24,28},{28,24},{1,5},{5... | collective-permute-start | bytes 688136 | tf_op jit(solution)/shard_map/ppermute | solution.py:37
  31.5 1.8 %collective-permute-start.7 = (f32[776,128]{1,0:T(8,128)S(1)}, f32[776,128]{1,0:T(8,128)S(1)}, u32[]{:S(2)}, u32[]{:S(2)}) collective-permute-start(f32[776,128]{1,0:T(8,128)S(1)} %shard_map.43), channel_id=1, source_target_pairs={{0,1},{1,0},{2,3},{3,2},{4,5},{5,4},{6,7},{7,6},{8,9},{9,8},{10,11... | collective-permute-start | bytes 1191944 | tf_op jit(solution)/shard_map/ppermute | solution.py:37
  33.3 7.2 %collective-permute-start.8 = (bf16[800,128]{1,0:T(8,128)(2,1)S(1)}, bf16[800,128]{1,0:T(8,128)(2,1)S(1)}, u32[]{:S(2)}, u32[]{:S(2)}) collective-permute-start(bf16[800,128]{1,0:T(8,128)(2,1)S(1)} %shard_map.44.mine), channel_id=1, source_target_pairs={{0,2},{1,3},{2,0},{3,1},{4,6},{5,7},{6,4},{7,5},{8,10},{9,11},{10,... | collective-permute-start | bytes 614408 | tf_op jit(solution)/shard_map/ppermute | solution.py:37
  41.2 14.7 %collective-permute-start.15 = (f32[768,128]{1,0:T(8,128)S(1)}, f32[768,128]{1,0:T(8,128)S(1)}, u32[]{:S(2)}, u32[]{:S(2)}) collective-permute-start(f32[768,128]{1,0:T(8,128)S(1)} %get-tuple-element.32.own), channel_id=1, source_target_pairs={{0,1},{1,0},{2,3},{3,2},{4,5},{5,4},{6,7},{7,6},{8,9},{9,8},{10,11... | collective-permute-start | bytes 1179656 | tf_op jit(solution)/shard_map/ppermute | solution.py:37
  41.3 1.8 %collective-permute-start.9 = (f32[64,128]{1,0:T(8,128)S(1)}, f32[64,128]{1,0:T(8,128)S(1)}, u32[]{:S(2)}, u32[]{:S(2)}) collective-permute-start(f32[64,128]{1,0:T(8,128)S(1)} %get-tuple-element.31), channel_id=1, source_target_pairs={{0,1},{1,0},{2,3},{3,2},{4,5},{5,4},{6,7},{7,6},{8,9},{9,8},{10,11... | collective-permute-start | bytes 98312 | tf_op jit(solution)/shard_map/ppermute | solution.py:37
  43.0 6.0 %collective-permute-start.10 = (f32[64,128]{1,0:T(8,128)S(1)}, f32[64,128]{1,0:T(8,128)S(1)}, u32[]{:S(2)}, u32[]{:S(2)}) collective-permute-start(f32[64,128]{1,0:T(8,128)S(1)} %add.15), channel_id=1, source_target_pairs={{0,16},{4,20},{8,24},{12,28},{16,0},{20,4},{24,8},{28,12},{1,17},{... | collective-permute-start | bytes 98312 | tf_op jit(solution)/shard_map/ppermute | solution.py:37
  49.0 4.8 %collective-permute-start.13 = (f32[64,128]{1,0:T(8,128)S(1)}, f32[64,128]{1,0:T(8,128)S(1)}, u32[]{:S(2)}, u32[]{:S(2)}) collective-permute-start(f32[64,128]{1,0:T(8,128)S(1)} %add.16), channel_id=1, source_target_pairs={{0,12},{4,8},{8,4},{12,0},{16,28},{20,24},{24,20},{28,16},{1,13},{... | collective-permute-start | bytes 98312 | tf_op jit(solution)/shard_map/ppermute | solution.py:37
  51.0 3.9 %collective-permute-start.12 = (f32[64,128]{1,0:T(8,128)S(1)}, f32[64,128]{1,0:T(8,128)S(1)}, u32[]{:S(2)}, u32[]{:S(2)}) collective-permute-start(f32[64,128]{1,0:T(8,128)S(1)} %add.16), channel_id=1, source_target_pairs={{0,8},{4,12},{8,0},{12,4},{16,24},{20,28},{24,16},{28,20},{1,9},{5... | collective-permute-start | bytes 98312 | tf_op jit(solution)/shard_map/ppermute | solution.py:37
  51.9 3.9 %collective-permute-start.11 = (f32[64,128]{1,0:T(8,128)S(1)}, f32[64,128]{1,0:T(8,128)S(1)}, u32[]{:S(2)}, u32[]{:S(2)}) collective-permute-start(f32[64,128]{1,0:T(8,128)S(1)} %add.16), channel_id=1, source_target_pairs={{0,4},{4,0},{8,12},{12,8},{16,20},{20,16},{24,28},{28,24},{1,5},{5... | collective-permute-start | bytes 98312 | tf_op jit(solution)/shard_map/ppermute | solution.py:37
  55.8 1.3 %collective-permute-start.14 = (f32[64,128]{1,0:T(8,128)S(1)}, f32[64,128]{1,0:T(8,128)S(1)}, u32[]{:S(2)}, u32[]{:S(2)}) collective-permute-start(f32[64,128]{1,0:T(8,128)S(1)} %add_add_fusion.own), channel_id=1, source_target_pairs={{0,1},{1,0},{2,3},{3,2},{4,5},{5,4},{6,7},{7,6},{8,9},{9,8},{10,11... | collective-permute-start | bytes 98312 | tf_op jit(solution)/shard_map/ppermute | solution.py:37
